TPU v7x, 32 devices: a whole 2x2x4 slice. The times are simulated.
32 devices in a mesh: wide: 8 (over z, y), narrow: 4 (over x, core).
Axes of the slice: x: 2, y: 2, z: 4, core: 2. Of those that a mesh axis runs over, the one named last changes fastest.
Arguments:
- weights: float32 [9060864], P('narrow')
- first_moment: float32 [4, 9060864], P('narrow', 'wide'), may hold values from -9.536743e-07 to 9.536743e-07
- second_moment: float32 [4, 9060864], P('narrow', 'wide'), may hold values from 4.458736e-15 to 1.787909e-14
- outer_momentum: float32 [9060864], P('narrow'), may hold values from -0.15625 to 0.15625
- noisy_input: bfloat16 [8, 128, 128, 128], P('wide', 'narrow'), may hold values from -6 to 6
- target: bfloat16 [8, 128, 128, 128], P('wide', 'narrow'), may hold values from -6 to 6
- text_tokens: bfloat16 [8, 128, 4096], P('wide', 'narrow'), may hold values from -6 to 6
- text_mask: int32 [8, 128], P('wide', 'narrow'), may hold values 0 or 1
- noise_level: int32 [8], P('wide'), may hold values from 0 to 999
- aug_level: int32 [8], P('wide'), may hold values from 0 to 23
- crop_size: int32 [8], P('wide'), may hold values from 32 to 128
Outputs:
- new_weights: float32 [9060864], P('narrow')
- momentum_out: float32 [9060864], P('narrow')
- moment_one: float32 [4, 9060864], P('narrow', 'wide')
- moment_two: float32 [4, 9060864], P('narrow', 'wide')
- loss_terms: float32 [1], replicated
- valid_count: float32 [1], replicated
All inputs are finite; a program needn't handle non-finite values. No bound on the sum of `text_mask` on one device may be relied on, other than what follows from the above.
Results may differ from a plain program's by a relative error of at most 0.0061.
Values may be sent and summed in bfloat16 or wider, within the bound.
A program may use at most 256 MiB of HBM per device.

v0:
```python
import math

import jax
import jax.numpy as jnp
from jax import lax
from jax.sharding import PartitionSpec as P

C = 128
NORM_GROUPS = 32
HEADS = 8
HEAD = 128
TEXT_D = 4096
H = 128
W = 128
NOISE_LEVELS = 1000
AUG_LEVELS = 24
GROUPS = 4
STEP = 8


EPS_NORM = 1e-05
CLIP_NORM = 0.002
BETA_ONE = 0.9
BETA_TWO = 0.99
INNER_RATE = 0.01
DECAY_RATE = 0.01
ADAM_EPS = 1e-08
OUTER_RATE = 0.7
OUTER_MOMENTUM = 0.9
HIGH = lax.Precision.HIGHEST


def with_halo(block, sides, width):
    for axis, dim in sides:
        count = lax.axis_size(axis)
        forward = [(i, i + 1) for i in range(count - 1)]
        backward = [(target, source) for source, target in forward]
        low = lax.ppermute(
            lax.slice_in_dim(block, block.shape[dim] - width, None, axis=dim), axis, forward
        )
        high = lax.ppermute(lax.slice_in_dim(block, 0, width, axis=dim), axis, backward)
        block = jnp.concatenate([low, block, high], axis=dim)
    return block


def from_partner(value, axis, apart):
    mask = 2**apart
    pairs = [(source, source ^ mask) for source in range(lax.axis_size(axis))]
    return lax.ppermute(value, axis, pairs)


def low_value(value):
    rounded = lax.optimization_barrier(value.astype(jnp.bfloat16)).astype(jnp.float32)
    return value + lax.stop_gradient(rounded - value)


def unpack_rest(rest):
    layouts = [
        (9 * C, C),
        (NOISE_LEVELS + AUG_LEVELS, 2 * C),
        (4, C),
        (C, HEADS * HEAD),
        (HEADS * HEAD, C),
    ]
    pieces = []
    offset = 0
    for layout in layouts:
        number = layout[0] * layout[1]
        pieces.append(rest[offset : offset + number].reshape(layout))
        offset = offset + number
    return pieces


def film_norm(
    noisy_float, cond_table, norm_gains, noise_level, aug_level, group_sums, squares, element_count
):
    num_items, height, columns, channels = noisy_float.shape
    levels = jnp.arange(NOISE_LEVELS + AUG_LEVELS, dtype=jnp.int32)
    level_hot = (levels[None, :] == noise_level[:, None]).astype(jnp.float32) + (
        levels[None, :] == (aug_level + NOISE_LEVELS)[:, None]
    ).astype(jnp.float32)
    film_terms = jnp.dot(level_hot, cond_table, precision=HIGH)
    average = group_sums / element_count
    spread = lax.rsqrt(squares / element_count - average * average + EPS_NORM)
    grouped = noisy_float.reshape(num_items, height, columns, NORM_GROUPS, channels // NORM_GROUPS)
    normed = ((grouped - average[:, None, None, :, None]) * spread[:, None, None, :, None]).reshape(
        num_items, height, columns, channels
    )
    scaled = (normed * norm_gains[0] + norm_gains[1]) * (
        1.0 + film_terms[:, None, None, :channels]
    ) + film_terms[:, None, None, channels:]
    return jax.nn.silu(scaled)


def convolve(padded, conv_w, height, columns):
    channels = conv_w.shape[1]
    padded = jnp.pad(padded, ((0, 0), (0, 0), (1, 1), (0, 0)))
    running = jnp.zeros((padded.shape[0], height, columns, channels), jnp.float32)
    for offset_y in range(3):
        for offset_x in range(3):
            tap_index = offset_y * 3 + offset_x
            window = padded[:, offset_y : offset_y + height, offset_x : offset_x + columns]
            running = running + jnp.einsum(
                "ihwc,cd->ihwd",
                window,
                conv_w[tap_index * channels : (tap_index + 1) * channels],
                precision=HIGH,
            )
    return running


def attend(convolved, norm_gains, query_w, out_w, keyval, valid_keys, lowered):
    num_items, height, columns, channels = convolved.shape
    centered = convolved - jnp.mean(convolved, axis=-1, keepdims=True)
    layered = lowered(
        centered
        * lax.rsqrt(jnp.mean(centered * centered, axis=-1, keepdims=True) + EPS_NORM)
        * norm_gains[2]
        + norm_gains[3]
    )
    queries = lowered(jnp.einsum("ihwc,cd->ihwd", layered, query_w, precision=HIGH)).reshape(
        num_items, height * columns, HEADS, HEAD
    )
    key_heads = keyval[..., : HEADS * HEAD].reshape(num_items, -1, HEADS, HEAD)
    value_heads = keyval[..., HEADS * HEAD :].reshape(num_items, -1, HEADS, HEAD)
    scores = jnp.einsum("iqhd,ikhd->ihqk", queries, key_heads, precision=HIGH) * (
        1.0 / math.sqrt(HEAD)
    )
    scores = jnp.where(valid_keys[:, None, None, :], scores, -1e30)
    maximum = jnp.max(scores, axis=-1, keepdims=True)
    exponent = jnp.exp(scores - maximum)
    softmax_w = lowered(exponent / jnp.sum(exponent, axis=-1, keepdims=True))
    mixture = lowered(
        jnp.einsum("ihqk,ikhd->iqhd", softmax_w, value_heads, precision=HIGH)
    ).reshape(num_items, height, columns, HEADS * HEAD)
    return convolved + jnp.einsum("ihwd,dc->ihwc", mixture, out_w, precision=HIGH)


def per_device(
    weights,
    first_moment,
    second_moment,
    outer_momentum,
    noisy_input,
    target,
    text_tokens,
    text_mask,
    noise_level,
    aug_level,
    crop_size,
):
    piece_len = first_moment.shape[1]
    wide_count = lax.axis_size("wide")
    narrow_count = lax.axis_size("narrow")
    group_devs = wide_count // GROUPS
    group_bits = group_devs.bit_length() - 1
    wide_pos = lax.axis_index("wide")
    narrow_pos = lax.axis_index("narrow")
    my_group = wide_pos // group_devs
    inner_pos = wide_pos % group_devs
    kv_block = 2 * HEADS * HEAD // narrow_count
    kv_len = TEXT_D * kv_block
    own_kv_w = weights[:kv_len].astype(jnp.bfloat16).astype(jnp.float32).reshape(TEXT_D, kv_block)
    rest_all = lax.all_gather(
        weights[kv_len:].astype(jnp.bfloat16), "narrow", axis=0, tiled=True
    ).astype(jnp.float32)
    conv_w, cond_table, norm_gains, query_w, out_w = unpack_rest(rest_all)
    num_items, band, columns, channels = noisy_input.shape
    noisy_float = noisy_input.astype(jnp.float32)
    target_float = target.astype(jnp.float32)
    row_ids = narrow_pos * band + jnp.arange(band, dtype=jnp.int32)
    col_ids = jnp.arange(columns, dtype=jnp.int32)
    pixel_mask = (
        (row_ids[None, :, None] < crop_size[:, None, None])
        & (col_ids[None, None, :] < crop_size[:, None, None])
    ).astype(jnp.float32)
    grouped = noisy_float.reshape(num_items, band * columns, NORM_GROUPS, channels // NORM_GROUPS)
    group_sums, squares = lax.psum(
        (jnp.sum(grouped, axis=(1, 3)), jnp.sum(grouped * grouped, axis=(1, 3))), "narrow"
    )
    element_count = H * W * C // NORM_GROUPS

    def film_part(table_in, gains_in):
        return low_value(
            film_norm(
                noisy_float,
                table_in,
                gains_in,
                noise_level,
                aug_level,
                group_sums,
                squares,
                element_count,
            )
        )

    active, pull_film = jax.vjp(film_part, cond_table, norm_gains)
    padded_rows = with_halo(active.astype(jnp.bfloat16), (("narrow", 1),), 1).astype(jnp.float32)
    text_all, mask_all = (
        lax.all_gather(text_tokens, "narrow", axis=1, tiled=True),
        lax.all_gather(text_mask.astype(jnp.bfloat16), "narrow", axis=1, tiled=True),
    )
    text_float = text_all.astype(jnp.float32)

    def project(kv_in):
        return low_value(jnp.einsum("itc,cd->itd", text_float, kv_in, precision=HIGH))

    own_cols, pull_kv = jax.vjp(project, own_kv_w)
    keyval = lax.all_gather(own_cols.astype(jnp.bfloat16), "narrow", axis=2, tiled=True).astype(
        jnp.float32
    )
    token_ids = jnp.arange(mask_all.shape[1], dtype=jnp.int32)
    valid_keys = (mask_all > 0) | (token_ids[None, :] == 0)

    def conv_attend(rows_in, keyval_in, conv_in, gains_in, query_in, out_in):
        convolved = noisy_float + convolve(rows_in, conv_in, band, columns)
        output = attend(convolved, gains_in, query_in, out_in, keyval_in, valid_keys, low_value)
        residual_err = output - target_float
        return jnp.sum(residual_err * residual_err * pixel_mask[..., None])

    sq_sum, pull_main = jax.vjp(
        conv_attend, padded_rows, keyval, conv_w, norm_gains, query_w, out_w
    )
    grad_rows, grad_kv, grad_conv, gains_main, grad_query, grad_out = pull_main(
        jnp.ones((), jnp.float32)
    )
    rims = jnp.concatenate([grad_rows[:, :1], grad_rows[:, -1:]], axis=1)
    arrived = with_halo(rims.astype(jnp.bfloat16), (("narrow", 1),), 1).astype(rims.dtype)
    grad_active = grad_rows[:, 1:-1]
    grad_active = grad_active.at[:, 0].add(arrived[:, 0]).at[:, -1].add(arrived[:, -1])
    grad_table, gains_film = pull_film(grad_active)
    own_grad = lax.psum_scatter(grad_kv, "narrow", scatter_dimension=2, tiled=True)
    (grad_own_kv,) = pull_kv(own_grad)
    rest_grad = jnp.concatenate(
        [
            grad_conv.reshape(-1),
            grad_table.reshape(-1),
            (gains_main + gains_film).reshape(-1),
            grad_query.reshape(-1),
            grad_out.reshape(-1),
        ]
    )
    rest_shard = lax.psum_scatter(rest_grad, "narrow", scatter_dimension=0, tiled=True)
    shard_grad = jnp.concatenate([grad_own_kv.reshape(-1), rest_shard])
    piece_grad = shard_grad
    for level in range(group_bits - 1, -1, -1):
        half_len = piece_grad.shape[0] // 2
        upper_bit = wide_pos // 2**level % 2
        kept = jnp.where(upper_bit == 1, piece_grad[half_len:], piece_grad[:half_len])
        given = jnp.where(upper_bit == 1, piece_grad[:half_len], piece_grad[half_len:])
        piece_grad = kept + from_partner(given, "wide", level)
    group_hot = (jnp.arange(GROUPS, dtype=jnp.int32) == my_group).astype(jnp.float32)
    own_count = jnp.sum(pixel_mask)
    sq_all, count_all, loss_all = lax.psum(
        (group_hot * jnp.sum(piece_grad * piece_grad), group_hot * own_count, sq_sum),
        ("wide", "narrow"),
    )
    total_count = jnp.sum(count_all)
    norm_value = jnp.sqrt(jnp.sum(group_hot * sq_all)) / total_count
    clipped = piece_grad / total_count * jnp.minimum(1.0, CLIP_NORM / norm_value)
    moment_one = BETA_ONE * first_moment[0] + (1.0 - BETA_ONE) * clipped
    moment_two = BETA_TWO * second_moment[0] + (1.0 - BETA_TWO) * clipped * clipped
    weight_piece = lax.dynamic_slice_in_dim(weights, inner_pos * piece_len, piece_len)
    corrected_one = moment_one / (1.0 - BETA_ONE**STEP)
    corrected_two = moment_two / (1.0 - BETA_TWO**STEP)
    inner = weight_piece - INNER_RATE * (
        corrected_one / (jnp.sqrt(corrected_two) + ADAM_EPS) + DECAY_RATE * weight_piece
    )
    weighted = jnp.sum(group_hot * count_all) * (weight_piece - inner)
    holder = jnp.zeros((group_devs, piece_len), jnp.float32)
    holder = lax.dynamic_update_slice(holder, weighted[None, :], (inner_pos, jnp.int32(0)))
    summed = lax.psum(holder.reshape(-1), "wide")
    averaged = summed / total_count
    momentum_out = OUTER_MOMENTUM * outer_momentum + averaged
    new_weights = weights - OUTER_RATE * (averaged + OUTER_MOMENTUM * momentum_out)
    return (
        new_weights,
        momentum_out,
        moment_one[None, :],
        moment_two[None, :],
        loss_all[None],
        total_count[None],
    )


def solution(mesh):
    placed = (
        P("narrow"),
        P("narrow", "wide"),
        P("narrow", "wide"),
        P("narrow"),
        P("wide", "narrow", None, None),
        P("wide", "narrow", None, None),
        P("wide", "narrow", None),
        P("wide", "narrow"),
        P("wide"),
        P("wide"),
        P("wide"),
    )
    return jax.shard_map(
        per_device,
        mesh=mesh,
        in_specs=placed,
        out_specs=(P("narrow"), P("narrow"), P("narrow", "wide"), P("narrow", "wide"), P(), P()),
        check_vma=False,
    )
```

profile of v0, /device:TPU:0, one launch (start us, length us, event | category | flops | bytes accessed | tf_op | source)
XLA Modules:
  0.0 1275.9 jit_solution(11938594680524346282)
XLA Ops:
  61.3 30.6 %reduce.33 = bf16[4,168064]{1,0:T(4,128)(2,1)} reduce(bf16[4,1,168064]{2,1,0:T(2,128)(2,1)} %all-gather.6.cloned.1.call-done, bf16[]{:T(256)} %constant.247), dimensions={1}, to_apply=%all-gather.reduce_sub_computation | reduce | bytes 2689026 | tf_op jit(solution)/shard_map/all_gather | solution.py:164
  141.6 14.1 %copy.136 = f32[512,8,8,128]{3,2,1,0:T(8,128)} copy(f32[512,8,8,128]{3,1,2,0:T(8,128)} %bitcast.419) | data formatting | bytes 33554432
  155.7 17.5 %copy.103 = f32[4096,8,128]{0,2,1:T(8,128)} copy(f32[4096,8,128]{2,1,0:T(8,128)} %bitcast.421) | data formatting | bytes 33554432 | tf_op jit(solution)/shard_map/reshape.157
  173.2 18.2 %fusion.9 = (f32[8,4096]{1,0:T(8,128)S(1)}, f32[8,4096,128]{1,2,0:T(8,128)}) fusion(pred[128]{0:T(512)(128)(4,1)S(1)} %fusion.201, f32[4096,8,128]{0,2,1:T(8,128)} %copy.103, bf16[128,8,128]{2,1,0:T(8,128)(2,1)S(1)} %bitcast.427), kind=kOutput, calls=%fused_computation.20 | convolution fusion | flops 6455001088 | bytes 33947776 | tf_op jit(solution)/shard_map/jvp(iqhd,ikhd->ihqk)/dot_general | solution.py:126
  211.2 24.0 %bitcast_convert_fusion = (bf16[1,4096,8,128]{1,3,2,0:T(8,128)(2,1)}, f32[8,128,4096]{2,1,0:T(8,128)}) fusion(bf16[1,8,4096,128]{2,3,1,0:T(8,128)(2,1)} %convert_bitcast_fusion, f32[8,4096]{1,0:T(8,128)S(1)} %fusion.226, f32[8,4096]{1,0:T(8,128)S(1)} %get-tuple-element.79, f32[8,4096,128]{1,2,0:T(8,128)} %get-tuple-element.80, ...), kind=kOutput, calls=%fused_computation.9 | convolution fusion | flops 6476005376 | bytes 50856064 | tf_op jit(solution)/shard_map/jvp(ihqk,ikhd->iqhd)/dot_general | solution.py:134
  235.3 13.8 %subtract_add_fusion = f32[1,4096,8,128]{1,3,2,0:T(8,128)} fusion(f32[8,128,4096]{2,1,0:T(8,128)} %get-tuple-element.82, bf16[1,4096,8,128]{1,3,2,0:T(8,128)(2,1)} %get-tuple-element.81), kind=kLoop, calls=%fused_computation | loop fusion | flops 12582912 | bytes 41943040 | tf_op jit(solution)/shard_map/jvp()/add | solution.py:54
  259.0 24.5 %multiply_reduce_fusion.4 = (f32[]{:T(128)}, f32[1,32,128,128]{3,2,1,0:T(8,128)S(1)}) fusion(f32[32,128]{1,0:T(8,128)S(1)} %and_convert_fusion, bf16[1,32,128,128]{3,2,1,0:T(8,128)(2,1)S(1)} %copy-done.27, f32[1,32,128,128]{3,2,1,0:T(8,128)S(1)} %get-tuple-element.78, bf16[672256]{0:T(1024)(128)(2,1)} %copy-done.16, f32[32,128,1024]{1,0,2:T(8,128)S(1)} %bitcast.415), kind=kOutput, calls=%fused_computation.137 | convolution fusion | flops 6446645248 | bytes 22298628 | tf_op jit(solution)/shard_map/jvp(ihwd,dc->ihwc)/dot_general | solution.py:136
  283.5 20.1 %convolution_bitcast_fusion = f32[131072]{0:T(1024)} fusion(f32[32,128,1024]{1,0,2:T(8,128)S(1)} %bitcast.416, f32[1,32,128,128]{3,2,1,0:T(8,128)S(1)} %get-tuple-element.60), kind=kOutput, calls=%fused_computation.3 | convolution fusion | flops 6442450944 | bytes 19398656 | tf_op jit(solution)/shard_map/transpose(jvp(ihwd,dc->ihwc))/dot_general | solution.py:136
  313.0 39.3 %fusion.3 = f32[8,128,128]{2,1,0:T(8,128)} fusion(f32[4096,8,128]{2,0,1:T(8,128)} %fusion.237, bf16[1,8,4096,128]{2,3,1,0:T(8,128)(2,1)} %convert_bitcast_fusion, f32[8,4096]{1,0:T(8,128)S(1)} %fusion.226, f32[8,4096,128]{1,2,0:T(8,128)} %get-tuple-element.80, f32[8,4096]{1,0:T(8,128)S(1)} %get-tuple-element.79, pred[128]{0:T(512)(128)(4,1)S(1)} %fusion.201), kind=kOutput, calls=%fused_computation.7 | convolution fusion | flops 6471811072 | bytes 42729600 | tf_op jit(solution)/shard_map/transpose(jvp(ihqk,ikhd->iqhd))/dot_general | solution.py:134
  352.3 33.6 %convert_reduce_fusion = (f32[8,4096]{1,0:T(8,128)S(1)}, pred[8,4096,128]{1,2,0:T(32,128)(4,1)S(1)}, f32[8,4096]{1,0:T(8,128)S(1)}, f32[8,4096,128]{1,2,0:T(8,128)}) fusion(f32[8,4096]{1,0:T(8,128)S(1)} %get-tuple-element.79, f32[8,4096,128]{1,2,0:T(8,128)} %get-tuple-element.80, pred[128]{0:T(512)(128)(4,1)S(1)} %fusion.201, ...), kind=kOutput, calls=%fused_computation.11 | convolution fusion | flops 6480134144 | bytes 55312512 | tf_op jit(solution)/shard_map/transpose(jvp(ihqk,ikhd->iqhd))/dot_general | solution.py:134
  385.9 19.2 %fusion.228 = (f32[8,4096]{1,0:T(8,128)S(1)}, f32[8,4096,128]{1,2,0:T(8,128)}) fusion(f32[8,4096]{1,0:T(8,128)S(1)} %get-tuple-element.79, f32[8,4096,128]{1,2,0:T(8,128)} %get-tuple-element.80, pred[128]{0:T(512)(128)(4,1)S(1)} %fusion.201, f32[8,4096]{1,0:T(8,128)S(1)} %neg.23, f32[8,4096,128]{1,2,0:T(8,128)} %get-tuple-element.83, f32[8,4096]{1,0:T(8,128)S(1)} %fusion.226), kind=kLoop, calls=%fused_computation.276 | loop fusion | flops 29327360 | bytes 50856064 | tf_op jit(solution)/shard_map/transpose(jvp())/reduce_sum | solution.py:131
  405.1 20.7 %fusion.15 = f32[1,4096,8,128]{3,1,2,0:T(8,128)} fusion(f32[8,4096,128]{1,2,0:T(8,128)} %get-tuple-element.53, pred[8,4096,128]{1,2,0:T(32,128)(4,1)S(1)} %get-tuple-element.55, f32[8,4096]{1,0:T(8,128)S(1)} %negate_divide_fusion, pred[128]{0:T(512)(128)(4,1)S(1)} %fusion.201, bf16[128,8,128]{2,1,0:T(8,128)(2,1)S(1)} %bitcast.428), kind=kOutput, calls=%fused_computation.26 | convolution fusion | flops 6459228160 | bytes 38142080 | tf_op jit(solution)/shard_map/transpose(jvp(iqhd,ikhd->ihqk))/dot_general | solution.py:126
  425.9 17.7 %copy.107 = f32[1,4096,8,128]{3,2,1,0:T(8,128)} copy(f32[1,4096,8,128]{3,1,2,0:T(8,128)} %fusion.15) | data formatting | bytes 33554432 | tf_op jit(solution)/shard_map/transpose(jvp(iqhd,ikhd->ihqk))/transpose | solution.py:126
  443.6 18.2 %reshape.932 = f32[32,128,1024]{2,1,0:T(8,128)} reshape(f32[1,4096,8,128]{3,2,1,0:T(8,128)} %copy.107) | data formatting | bytes 33554432 | tf_op jit(solution)/shard_map/reshape.196
  461.9 17.2 %convolution_bitcast_fusion.2 = f32[16,8,8,128]{3,2,1,0:T(8,128)} fusion(f32[32,128,1024]{2,1,0:T(8,128)} %reshape.932, bf16[1,32,128,128]{3,2,1,0:T(8,128)(2,1)S(1)} %copy-done.13, f32[1,32,128,128]{3,2,1,0:T(8,128)S(1)} %get-tuple-element.78, f32[128]{0:T(128)S(1)} %copy-done.43, f32[128]{0:T(128)S(1)} %copy-done.40, f32[32,128]{1,0:T(8,128)S(1)} %copy-done.30, ...), kind=kOutput, calls=%fused_computation.160 | convolution fusion | flops 6446120960 | bytes 20481024 | tf_op jit(solution)/shard_map/transpose(jvp(ihwc,cd->ihwd))/dot_general | solution.py:121
  574.8 23.3 %fusion.11 = f32[8,128,128]{1,2,0:T(8,128)S(1)} fusion(f32[4096,8,128]{0,2,1:T(8,128)} %copy.103, f32[8,4096,128]{1,2,0:T(8,128)} %get-tuple-element.53, pred[8,4096,128]{1,2,0:T(32,128)(4,1)} %copy-done.11, f32[8,4096]{1,0:T(8,128)S(1)} %negate_divide_fusion, pred[128]{0:T(512)(128)(4,1)S(1)} %fusion.201), kind=kOutput, calls=%fused_computation.22 | convolution fusion | flops 6459228160 | bytes 38404224 | tf_op jit(solution)/shard_map/transpose(jvp(iqhd,ikhd->ihqk))/dot_general | solution.py:126
  599.9 40.1 %all-reduce.36.cloned.1.call-done = f32[672256]{0:T(1024)} async-done(((f32[672256]{0:T(1024)}), f32[672256]{0:T(1024)}) %all-reduce.36.cloned.1.call-update) | async-done | bytes 2689040
  641.4 26.5 %reduce-scatter.2.cloned.1.call-done = f32[1,128,512]{1,2,0:T(8,128)} async-done(((f32[1,128,2048]{1,2,0:T(8,128)}), f32[1,128,512]{1,2,0:T(8,128)}) %reduce-scatter.2.cloned.1.call-update) | async-done | bytes 262160 | tf_op jit(solution)/shard_map/reduce_scatter | solution.py:232
  701.6 52.3 %multiply_reduce_fusion.2 = (f32[1132608]{0:T(1024)}, f32[1132608]{0:T(1024)}) fusion(f32[1,1132608]{1,0:T(1,128)} %param.17, f32[1,1132608]{1,0:T(1,128)} %param.16), kind=kLoop, calls=%fused_computation.49 | loop fusion | flops 2265216 | bytes 18121728 | tf_op jit(solution)/shard_map/mul | solution.py:262
  753.9 44.8 %collective-permute-done.4 = f32[1132608]{0:T(1024)} collective-permute-done((f32[1132608]{0:T(1024)}, f32[1132608]{0:T(1024)}, u32[]{:S(2)}, u32[]{:S(2)}) %collective-permute-start.4) | collective-permute-done | bytes 4530464 | tf_op jit(solution)/shard_map/ppermute | solution.py:49
  807.6 39.8 %all-reduce.29 = (f32[4]{0:T(128)S(1)}, f32[4]{0:T(128)S(1)}, f32[1]{0:T(128)}) all-reduce(f32[4]{0:T(128)S(1)} %fusion.204, f32[4]{0:T(128)S(1)} %fusion.203, f32[1]{0:T(128)} %bitcast.124), channel_id=1, replica_groups=mesh['wide'=8,'narrow'=4] {'wide','narrow'}, use_global_device_ids=true, to_apply=%region_1.2 | all-reduce | flops 9 | bytes 72 | tf_op jit(solution)/shard_map/psum | solution.py:254
  870.2 77.4 %dynamic_update_slice.3 = f32[2,1132608]{1,0:T(2,128)} dynamic-update-slice(f32[2,1132608]{1,0:T(2,128)} %broadcast_in_dim.90, f32[1,1132608]{1,0:T(1,128)} %broadcast_in_dim.105, s32[]{:T(128)S(6)} %select_n.50, s32[]{:T(128)} %constant.146.clone.1) | dynamic-update-slice | bytes 9060868 | tf_op jit(solution)/shard_map/dynamic_update_slice | solution.py:271
  973.4 278.4 %all-reduce.34.cloned.1.call-done = f32[2265216]{0:T(1024)} async-done(((f32[2265216]{0:T(1024)}), f32[2265216]{0:T(1024)}) %all-reduce.34.cloned.1.call-update) | async-done | bytes 9060880 | tf_op jit(solution)/shard_map/psum | solution.py:272
  1251.7 17.4 %multiply_subtract_fusion = (f32[2265216]{0:T(1024)}, f32[2265216]{0:T(1024)}) fusion(f32[2265216]{0:T(1024)} %param.15, f32[2265216]{0:T(1024)} %all-reduce.34.cloned.1.call-done, f32[]{:T(128)} %get-tuple-element.39, f32[2265216]{0:T(1024)} %param.18), kind=kLoop, calls=%fused_computation.24 | loop fusion | flops 15856512 | bytes 45304324 | tf_op jit(solution)/shard_map/sub | solution.py:275
  (276 shorter events, 327.4 us)
Async XLA Ops:
  7.2 43.0 %all-gather.4.cloned.1.call-start = ((), (), s32[]{:S(2)}) async-start(), calls=%async_computation.1 | async-start | bytes 1310720 | tf_op jit(solution)/shard_map/all_gather | solution.py:200
  7.9 53.4 %all-gather.6.cloned.1.call-start = ((), (), s32[]{:S(2)}) async-start(), calls=%async_computation.4 | async-start | bytes 3361280 | tf_op jit(solution)/shard_map/all_gather | solution.py:164
  18.9 621.1 %all-reduce.36.cloned.1.call-start = ((), (), s32[]{:S(2)}) async-start(), calls=%async_computation.5 | async-start | bytes 5382144
  25.0 25.1 %copy-start.57 = (pred[128]{0:T(512)(128)(4,1)}, pred[128]{0:T(512)(128)(4,1)S(1)}, u32[]{:S(2)}) copy-start(pred[128]{0:T(512)(128)(4,1)S(1)} %iota_compare_fusion.2) | copy-start | bytes 388
  41.7 56.9 %copy-start.44 = (f32[128]{0:T(128)}, f32[128]{0:T(128)S(1)}, u32[]{:S(2)}) copy-start(f32[128]{0:T(128)S(1)} %sub.88) | copy-start | bytes 1540
  41.8 56.7 %copy-start.46 = (f32[128]{0:T(128)}, f32[128]{0:T(128)S(1)}, u32[]{:S(2)}) copy-start(f32[128]{0:T(128)S(1)} %mul.321) | copy-start | bytes 1540
  61.2 112.0 %copy-start.18 = (bf16[16,8,8,128]{3,2,1,0:T(8,128)(2,1)}, bf16[16,8,8,128]{3,2,1,0:T(8,128)(2,1)S(1)}, u32[]{:S(2)}) copy-start(bf16[16,8,8,128]{3,2,1,0:T(8,128)(2,1)S(1)} %copy.137) | copy-start | bytes 786436
  94.1 31.7 %copy-start.39 = (f32[128]{0:T(128)}, f32[128]{0:T(128)S(1)}, u32[]{:S(2)}) copy-start(f32[128]{0:T(128)S(1)} %get-tuple-element.63) | copy-start | bytes 1540
  94.1 31.7 %copy-start.42 = (f32[128]{0:T(128)}, f32[128]{0:T(128)S(1)}, u32[]{:S(2)}) copy-start(f32[128]{0:T(128)S(1)} %get-tuple-element.64) | copy-start | bytes 1540
  99.7 18.4 %copy-start.2 = (bf16[1,32,128,128]{3,2,1,0:T(8,128)(2,1)}, bf16[1,32,128,128]{3,2,1,0:T(8,128)(2,1)S(1)}, u32[]{:S(2)}) copy-start(bf16[1,32,128,128]{3,2,1,0:T(8,128)(2,1)S(1)} %fusion.26) | copy-start | bytes 3145732
  99.8 7.2 collective-permute-start
  102.1 4.8 collective-permute-start.1
  283.5 20.1 %copy-start.6 = (f32[1,32,128,128]{3,2,1,0:T(8,128)}, f32[1,32,128,128]{3,2,1,0:T(8,128)S(1)}, u32[]{:S(2)}) copy-start(f32[1,32,128,128]{3,2,1,0:T(8,128)S(1)} %get-tuple-element.60) | copy-start | bytes 6291460
  283.5 20.1 %copy-start.26 = (bf16[131072]{0:T(1024)(128)(2,1)S(1)}, bf16[131072]{0:T(1024)(128)(2,1)}, u32[]{:S(2)}) copy-start(bf16[131072]{0:T(1024)(128)(2,1)} %get-tuple-element.61) | copy-start | bytes 786436
  385.9 19.2 %copy-start.11 = (pred[8,4096,128]{1,2,0:T(32,128)(4,1)}, pred[8,4096,128]{1,2,0:T(32,128)(4,1)S(1)}, u32[]{:S(2)}) copy-start(pred[8,4096,128]{1,2,0:T(32,128)(4,1)S(1)} %get-tuple-element.55) | copy-start | bytes 12582916
  385.9 19.2 %copy-start.19 = (bf16[16,8,8,128]{3,2,1,0:T(8,128)(2,1)S(1)}, bf16[16,8,8,128]{3,2,1,0:T(8,128)(2,1)}, u32[]{:S(2)}) copy-start(bf16[16,8,8,128]{3,2,1,0:T(8,128)(2,1)} %copy-done.18) | copy-start | bytes 786436
  443.6 18.3 %copy-start.43 = (f32[128]{0:T(128)S(1)}, f32[128]{0:T(128)}, u32[]{:S(2)}) copy-start(f32[128]{0:T(128)} %copy-done.42) | copy-start | bytes 1540
  553.6 11.5 collective-permute-start.2
  556.9 8.2 collective-permute-start.3
  574.7 23.3 %copy-start.31 = (f32[8,128,128]{2,1,0:T(8,128)S(1)}, f32[8,128,128]{2,1,0:T(8,128)}, u32[]{:S(2)}) copy-start(f32[8,128,128]{2,1,0:T(8,128)} %fusion.3) | copy-start | bytes 1572868
  574.7 93.2 %reduce-scatter.2.cloned.1.call-start = ((), (), s32[]{:S(2)}) async-start(), calls=%async_computation.2 | async-start | bytes 1310720 | tf_op jit(solution)/shard_map/reduce_scatter | solution.py:232
  598.0 69.9 %copy-start.17 = (bf16[1,128,4096]{2,1,0:T(8,128)(2,1)S(1)}, bf16[1,128,4096]{2,1,0:T(8,128)(2,1)}, u32[]{:S(2)}) copy-start(bf16[1,128,4096]{2,1,0:T(8,128)(2,1)} %all-gather.4.cloned.1.call-done) | copy-start | bytes 3145732
  599.1 652.6 %all-reduce.34.cloned.1.call-start = ((), (), s32[]{:S(2)}) async-start(), calls=%async_computation.3 | async-start | bytes 18128896 | tf_op jit(solution)/shard_map/psum | solution.py:272
  698.8 99.9 %collective-permute-start.4 = (f32[1132608]{0:T(1024)}, f32[1132608]{0:T(1024)}, u32[]{:S(2)}, u32[]{:S(2)}) collective-permute-start(f32[1132608]{0:T(1024)} %slice_select_fusion), channel_id=1, source_target_pairs={{0,4},{4,0},{8,12},{12,8},{16,20},{20,16},{24,28},{28,24},{1,5},{5... | collective-permute-start | bytes 13591304 | tf_op jit(solution)/shard_map/ppermute | solution.py:49
  (50 other events, 339.1 us)
Sparse Core Ops, SparseCore 0:
  9.6 19.4 all-gather.3
  31.1 26.0 all-gather.5
  574.8 65.1 all-reduce.35
  643.0 24.8 reduce-scatter.1
  961.6 290.1 all-reduce.33
where the time goes:
time: 1290 us; the launch traced here: 1280 us
  waiting for transfers between devices  391 us (30%)
  matrix products  329 us (26%)
  local copies, waits for them, and re-layouts  244 us (19%)
  other arithmetic  221 us (17%)
  blocking collectives  60.6 us (5%)
  between operations  19.8 us (2%)
    psum x1, waiting for transfers between devices, per_device(): summed = lax.psum(holder.reshape(-1), 'wide')  278 us
    dot_general x3, matrix products, attend(): jnp.einsum('ihqk,ikhd->iqhd', softmax_w, value_heads, precision=HIGH)  96.9 us
    dynamic_update_slice x1, local copies, waits for them, and re-layouts, per_device(): lax.dynamic_update_slice(holder, weighted[None, :], (inner_pos, jnp.int32...  77.4 us
    dot_general x27, matrix products, convolve(): jnp.einsum('ihwc,cd->ihwd', window, conv_w[tap_index * channels:(tap_inde...  69.5 us
    dot_general x3, matrix products, attend(): jnp.einsum('iqhd,ikhd->ihqk', queries, key_heads, precision=HIGH)  62.2 us
    dot_general x3, matrix products, attend(): jnp.einsum('ihwd,dc->ihwc', mixture, out_w, precision=HIGH)  54 us
    mul x1, other arithmetic, per_device(): BETA_TWO * second_moment[0] + (1.0 - BETA_TWO) * clipped * clipped  52.3 us
    unnamed x144, local copies, waits for them, and re-layouts  50.2 us
  transfers between devices with their start and end apart: 10, of which 4 were waited for; matrix products, arithmetic and copies ran while one was open for 10% of the time, Pallas kernels for 0%

commit v1 on v0

v1 whole, which is shorter than its diff:
```python
import functools
import math

import jax
import jax.numpy as jnp
from jax import lax
from jax.experimental import pallas as pl
from jax.experimental.pallas import tpu as pltpu
from jax.sharding import PartitionSpec as P

MESH = pl.DeviceIdType.MESH
C = 128
NORM_GROUPS = 32
HEADS = 8
HEAD = 128
TEXT_D = 4096
H = 128
W = 128
NOISE_LEVELS = 1000
AUG_LEVELS = 24
LEVELS = NOISE_LEVELS + AUG_LEVELS
GROUPS = 4
STEP = 8


EPS_NORM = 1e-05
CLIP_NORM = 0.002
BETA_ONE = 0.9
BETA_TWO = 0.99
INNER_RATE = 0.01
DECAY_RATE = 0.01
ADAM_EPS = 1e-08
OUTER_RATE = 0.7
OUTER_MOMENTUM = 0.9
F32 = jnp.float32
BF16 = jnp.bfloat16
LOG2E = 1.4426950408889634
LN2 = 0.6931471805599453
NT = (((1,), (1,)), ((), ()))
TILE = 2


def dot(a, b, dims=(((1,), (0,)), ((), ()))):
    return lax.dot_general(a, b, dims, preferred_element_type=F32)


def two_parts(value):
    top = value.astype(BF16)
    return top, (value - top.astype(F32)).astype(BF16)


def shifted(value, by, keep):
    return jnp.where(keep, pltpu.roll(value, by, 0), 0.0)


def main_kernel(
    band, columns, height, heads,
    info, noisy, target, vecs, conv_w, query_w, out_w, keyval, key_ok,
    dconv_w, y_t, z_t, sums,
    act3, diff3, m_cat, m_cat_t, n_cat, n_cat_t, conv_t, probs, dscore, wt3,
):
    tok = keyval.shape[0]
    width = heads * HEAD
    row0 = info[0]
    crop = info[1]
    pix = TILE * columns
    factor = LOG2E / math.sqrt(HEAD)
    for head in range(heads):
        cols = slice(head * HEAD, (head + 1) * HEAD)
        tcols = slice(head * tok, (head + 1) * tok)
        m_head = dot(query_w[:, cols], keyval[:, cols], NT) * factor
        top, rest = two_parts(m_head)
        m_cat[:C, tcols] = top
        m_cat[C:, tcols] = rest
        top, rest = two_parts(m_head.T)
        m_cat_t[tcols, :C] = top
        m_cat_t[tcols, C:] = rest
        n_head = dot(keyval[:, width + head * HEAD : width + (head + 1) * HEAD], out_w[cols, :])
        top, rest = two_parts(n_head)
        n_cat[tcols, :C] = top
        n_cat[tcols, C:] = rest
        top, rest = two_parts(n_head.T)
        n_cat_t[:C, tcols] = top
        n_cat_t[C:, tcols] = rest
    for tap in range(9):
        rows = slice(tap * C, (tap + 1) * C)
        wt3[rows, :] = conv_w[rows, :].astype(F32).T.astype(BF16)
    y_t[...] = jnp.zeros_like(y_t)
    z_t[...] = jnp.zeros_like(z_t)
    conv_t[...] = jnp.zeros_like(conv_t)
    sums[...] = jnp.zeros_like(sums)
    mean, spread = vecs[0:1, :], vecs[1:2, :]
    gain, offset = vecs[2:3, :], vecs[3:4, :]
    ln_gain, ln_offset = vecs[4:5, :], vecs[5:6, :]
    place = lax.broadcasted_iota(jnp.int32, (columns, C), 0)
    not_first, not_last = place > 0, place < columns - 1
    slope = spread * gain
    base = offset - mean * slope

    @pl.loop(0, band + 4)
    def _(r):
        scaled = noisy[r].astype(F32) * slope + base
        value = scaled * jax.nn.sigmoid(scaled)
        row = row0 + r - 2
        value = jnp.where(jnp.logical_and(row >= 0, row < height), value, 0.0)
        value = value.astype(BF16).astype(F32)
        act3[r, :, 0:C] = shifted(value, 1, not_first).astype(BF16)
        act3[r, :, C : 2 * C] = value.astype(BF16)
        act3[r, :, 2 * C : 3 * C] = shifted(value, columns - 1, not_last).astype(BF16)

    pix_row = lax.broadcasted_iota(jnp.int32, (pix, C), 0) // columns
    pix_col = lax.broadcasted_iota(jnp.int32, (pix, C), 0) % columns
    ok = key_ok[...] > 0.0

    @pl.loop(0, (band + 2) // TILE)
    def _(t):
        q = t * TILE
        conv = noisy[pl.ds(q + 1, TILE)].astype(F32).reshape(pix, C)
        for dy in range(3):
            window = act3[pl.ds(q + dy, TILE)].reshape(pix, 3 * C)
            conv = conv + dot(window, conv_w[dy * 3 * C : (dy + 1) * 3 * C, :])
        centered = conv - jnp.mean(conv, axis=1, keepdims=True)
        rs = lax.rsqrt(jnp.mean(centered * centered, axis=1, keepdims=True) + EPS_NORM)
        xhat = centered * rs
        layered = xhat * ln_gain + ln_offset
        low = layered.astype(BF16)
        low2 = jnp.concatenate([low, low], axis=1)
        for head in range(heads):
            tcols = slice(head * tok, (head + 1) * tok)
            score = dot(low2, m_cat[:, tcols])
            score = jnp.where(ok, score, -1e30)
            e = jnp.exp2(score - jnp.max(score, axis=1, keepdims=True))
            p = e * (1.0 / jnp.sum(e, axis=1, keepdims=True))
            probs[:, tcols] = p.astype(BF16)
        mixed = dot(probs[...], n_cat[...])
        output = conv + mixed[:, :C] + mixed[:, C:]
        row = row0 + q - 1 + pix_row
        valid = (row >= 0) & (row < crop) & (pix_col < crop)
        err = jnp.where(valid, output - target[pl.ds(q, TILE)].astype(F32).reshape(pix, C), 0.0)
        own_row = q + pix_row
        own = (own_row >= 1) & (own_row <= band)
        err_own = jnp.where(own, err, 0.0)
        sums[4:5, :] += jnp.sum(err_own * err_own, axis=0, keepdims=True)
        dout = 2.0 * err
        dout_low = dout.astype(BF16)
        dout2 = jnp.concatenate([dout_low, dout_low], axis=1)
        for head in range(heads):
            tcols = slice(head * tok, (head + 1) * tok)
            dprob = dot(dout2, n_cat_t[:, tcols])
            p = probs[:, tcols].astype(F32)
            pd = p * dprob
            ds = pd - p * jnp.sum(pd, axis=1, keepdims=True)
            dscore[:, tcols] = ds.astype(BF16)
        dlay2 = dot(dscore[...], m_cat_t[...])
        dlay = (dlay2[:, :C] + dlay2[:, C:]) * LN2
        dlay_own = jnp.where(own, dlay, 0.0)
        sums[2:3, :] += jnp.sum(dlay_own * xhat, axis=0, keepdims=True)
        sums[3:4, :] += jnp.sum(dlay_own, axis=0, keepdims=True)
        dxh = dlay * ln_gain
        dconv = dout + rs * (
            dxh
            - jnp.mean(dxh, axis=1, keepdims=True)
            - xhat * jnp.mean(dxh * xhat, axis=1, keepdims=True)
        )
        dout_t = (2.0 * err_own).T.astype(BF16)
        lay_t = jnp.where(own, layered, 0.0).T.astype(BF16)
        y_t[...] += dot(dout_t, probs[...])
        z_t[...] += dot(lay_t, dscore[...])
        dconv_t = jnp.where(own, dconv, 0.0).T.astype(BF16)
        for dy in range(3):
            window = act3[pl.ds(q + dy, TILE)].reshape(pix, 3 * C)
            conv_t[:, dy * 3 * C : (dy + 1) * 3 * C] += dot(dconv_t, window)
        for k in range(TILE):
            one = dconv[k * columns : (k + 1) * columns]
            diff3[q + k, :, 0:C] = shifted(one, columns - 1, not_last).astype(BF16)
            diff3[q + k, :, C : 2 * C] = one.astype(BF16)
            diff3[q + k, :, 2 * C : 3 * C] = shifted(one, 1, not_first).astype(BF16)

    @pl.loop(0, band // TILE)
    def _(t):
        r = t * TILE
        grad = jnp.zeros((pix, C), F32)
        for dy in range(3):
            window = diff3[pl.ds(r + 2 - dy, TILE)].reshape(pix, 3 * C)
            grad = grad + dot(window, wt3[dy * 3 * C : (dy + 1) * 3 * C, :])
        x = noisy[pl.ds(r + 2, TILE)].astype(F32).reshape(pix, C)
        scaled = x * slope + base
        sig = jax.nn.sigmoid(scaled)
        ds = grad * (sig * (1.0 + scaled * (1.0 - sig)))
        sums[0:1, :] += jnp.sum(ds, axis=0, keepdims=True)
        sums[1:2, :] += jnp.sum(ds * ((x - mean) * spread), axis=0, keepdims=True)

    for tap in range(9):
        cols = slice(tap * C, (tap + 1) * C)
        dconv_w[cols, :] = conv_t[:, cols].T


def run_main(info, noisy_ext, target_ext, vecs, conv_w, query_w, out_w, keyval, key_ok):
    band = target_ext.shape[0] - 2
    columns = target_ext.shape[1]
    tok = keyval.shape[0]
    vmem = pl.BlockSpec(memory_space=pltpu.VMEM)
    pix = TILE * columns
    return pl.pallas_call(
        functools.partial(main_kernel, band, columns, H, HEADS),
        out_shape=(
            jax.ShapeDtypeStruct((9 * C, C), F32),
            jax.ShapeDtypeStruct((C, HEADS * tok), F32),
            jax.ShapeDtypeStruct((C, HEADS * tok), F32),
            jax.ShapeDtypeStruct((8, C), F32),
        ),
        in_specs=[pl.BlockSpec(memory_space=pltpu.SMEM)] + [vmem] * 8,
        out_specs=(vmem,) * 4,
        scratch_shapes=[
            pltpu.VMEM((band + 4, columns, 3 * C), BF16),
            pltpu.VMEM((band + 2, columns, 3 * C), BF16),
            pltpu.VMEM((2 * C, HEADS * tok), BF16),
            pltpu.VMEM((HEADS * tok, 2 * C), BF16),
            pltpu.VMEM((HEADS * tok, 2 * C), BF16),
            pltpu.VMEM((2 * C, HEADS * tok), BF16),
            pltpu.VMEM((C, 9 * C), F32),
            pltpu.VMEM((pix, HEADS * tok), BF16),
            pltpu.VMEM((pix, HEADS * tok), BF16),
            pltpu.VMEM((9 * C, C), BF16),
        ],
        compiler_params=pltpu.CompilerParams(vmem_limit_bytes=40 * 2**20),
        name="main",
    )(info, noisy_ext, target_ext, vecs, conv_w, query_w, out_w, keyval, key_ok)


TROWS = 512
TN = (((0,), (0,)), ((), ()))


def adam_kernel(
    length, ints, scal, text_a, text_b, dkv, rest, first, second,
    first_out, second_out, step_out, gs, carry,
):
    i = pl.program_id(0)
    tokens = text_a.shape[0]
    lane0 = ints[0]

    @pl.when(i == 0)
    def _():
        carry[...] = jnp.zeros_like(carry)

    grad = dot(text_a[...], dkv[:tokens, :], TN) + dot(text_b[...], dkv[tokens:, :], TN)
    parts = TROWS // C
    for j in range(parts):
        gs[pl.ds(j, C, stride=parts), :] = grad[:, j * C : (j + 1) * C]
    g = (gs[...] + rest[...]) * scal[0]
    one = BETA_ONE * first.reshape(TROWS, C)[...] + (1.0 - BETA_ONE) * g
    two = BETA_TWO * second.reshape(TROWS, C)[...] + (1.0 - BETA_TWO) * g * g
    first_out.reshape(TROWS, C)[...] = one
    second_out.reshape(TROWS, C)[...] = two
    fixed_one = one * (1.0 / (1.0 - BETA_ONE**STEP))
    fixed_two = two * (1.0 / (1.0 - BETA_TWO**STEP))
    step = fixed_one / (jnp.sqrt(fixed_two) + ADAM_EPS) * scal[1]
    row = lax.broadcasted_iota(jnp.int32, (TROWS, C), 0)
    lane = lax.broadcasted_iota(jnp.int32, (TROWS, C), 1)
    step = jnp.where((i * TROWS + row) * C + lane < length, step, 0.0)
    turned = pltpu.roll(step, lane0, 1)
    above = pltpu.roll(turned, 1, 0)
    above = jnp.where(row == 0, carry[0:1, :], above)
    carry[0:1, :] = turned[TROWS - 1 : TROWS, :]
    step_out[...] = jnp.where(lane < lane0, above, turned).astype(BF16)


def run_adam(ints, scal, text_a, text_b, dkv, rest, first, second):
    length = first.shape[1]
    tiles = pl.cdiv(length + C, TROWS * C)
    tokens = text_a.shape[0]
    smem = pl.BlockSpec(memory_space=pltpu.SMEM)
    flat = pl.BlockSpec((1, TROWS * C), lambda i: (0, i))
    text_spec = pl.BlockSpec((tokens, C), lambda i: (0, i))
    square = pl.BlockSpec((TROWS, C), lambda i: (i, 0))
    return pl.pallas_call(
        functools.partial(adam_kernel, length),
        out_shape=(
            jax.ShapeDtypeStruct(first.shape, F32),
            jax.ShapeDtypeStruct(first.shape, F32),
            jax.ShapeDtypeStruct((tiles * TROWS, C), BF16),
        ),
        grid=(tiles,),
        in_specs=[
            smem, smem, text_spec, text_spec,
            pl.BlockSpec((2 * tokens, 4 * C), lambda i: (0, 0)),
            square, flat, flat,
        ],
        out_specs=(flat, flat, square),
        scratch_shapes=[pltpu.VMEM((TROWS, C), F32), pltpu.VMEM((8, C), F32)],
        compiler_params=pltpu.CompilerParams(vmem_limit_bytes=24 * 2**20),
        name="adam",
    )(ints, scal, text_a, text_b, dkv, rest, first, second)


def share_kernel(gd, rows, chunk, l1, l2, u_ref, out_ref, recv_a, recv_b, part,
                 s_u, s_fo, s_fi, s_y, r_a, r_b, r_f, r_y):
    wide = lax.axis_index("wide")
    g = wide // gd
    spot = wide % gd
    chunks = rows // chunk
    is_outer = jnp.logical_or(g == 0, g == GROUPS - 1)
    is_inner = jnp.logical_not(is_outer)
    low = g < GROUPS // 2
    outer_id = jnp.where(low, g - 1, g + 1) * gd + spot
    mate_id = jnp.where(low, g + 1, g - 1) * gd + spot
    barrier = pltpu.get_barrier_semaphore()
    for k in range(1, gd):
        other = g * gd + lax.rem(spot + k, gd)
        pl.semaphore_signal(barrier, inc=1, device_id={"wide": other}, device_id_type=MESH)
    pl.semaphore_signal(barrier, inc=1, device_id={"wide": mate_id}, device_id_type=MESH)
    @pl.when(is_inner)
    def _():
        pl.semaphore_signal(barrier, inc=1, device_id={"wide": outer_id}, device_id_type=MESH)
        pl.semaphore_wait(barrier, gd + 1)
    @pl.when(is_outer)
    def _():
        pl.semaphore_wait(barrier, gd)

    def sl(c):
        return pl.ds(pl.multiple_of(c * chunk, chunk), chunk)
    def copy(src, dst, ss, rs, dev):
        return pltpu.make_async_remote_copy(src_ref=src, dst_ref=dst, send_sem=ss, recv_sem=rs,
                                            device_id={"wide": dev}, device_id_type=MESH)
    def send_a(c):
        return copy(u_ref.at[sl(c)], recv_a.at[sl(c)], s_u.at[c], r_a.at[c], mate_id)
    def send_b(c):
        return copy(part.at[sl(c)], recv_b.at[sl(c)], s_u.at[c], r_b.at[c], mate_id)
    def send_fo(c):
        return copy(out_ref.at[spot, sl(c)], out_ref.at[spot, sl(c)], s_fo.at[c], r_f.at[c], outer_id)
    def send_fi(c):
        return copy(out_ref.at[spot, sl(c)], out_ref.at[spot, sl(c)], s_fi.at[c], r_f.at[c], mate_id)
    def send_y(c, k):
        return copy(out_ref.at[spot, sl(c)], out_ref.at[spot, sl(c)], s_y.at[k - 1, c], r_y.at[k - 1, c],
                    g * gd + lax.rem(spot + k, gd))
    def wait_y(c, k):
        src = lax.rem(spot + gd - k, gd)
        copy(out_ref.at[src, sl(c)], out_ref.at[src, sl(c)], s_y.at[k - 1, c], r_y.at[k - 1, c], wide).wait_recv()
    def spread(c):
        for k in range(1, gd):
            send_y(c, k).start()
    def is_root(c):
        return lax.rem(c + g, 2) == 1

    @pl.when(is_outer)
    def _():
        @pl.loop(0, chunks)
        def _(c):
            send_a(c).start()
        @pl.loop(0, chunks)
        def _(c):
            send_fo(c).wait_recv()
            spread(c)
    @pl.when(is_inner)
    def _():
        @pl.loop(0, chunks + l2)
        def _(c):
            @pl.when(jnp.logical_and(c < chunks, jnp.logical_not(is_root(c))))
            def _():
                send_a(c).wait_recv()
                part[sl(c)] = (u_ref[sl(c)].astype(jnp.float32) + recv_a[sl(c)].astype(jnp.float32)).astype(jnp.bfloat16)
                send_b(c).start()
            d = c - l1
            @pl.when(jnp.logical_and(jnp.logical_and(d >= 0, d < chunks), is_root(d)))
            def _():
                send_a(d).wait_recv()
                send_b(d).wait_recv()
                out_ref[spot, sl(d)] = (u_ref[sl(d)].astype(jnp.float32) + recv_a[sl(d)].astype(jnp.float32) + recv_b[sl(d)].astype(jnp.float32)).astype(jnp.bfloat16)
                send_fo(d).start()
                send_fi(d).start()
                spread(d)
            e = c - l2
            @pl.when(jnp.logical_and(e >= 0, jnp.logical_not(is_root(e))))
            def _():
                send_fi(e).wait_recv()
                send_fo(e).start()
                spread(e)
    @pl.loop(0, chunks)
    def _(c):
        for k in range(1, gd):
            wait_y(c, k)
            send_y(c, k).wait_send()
        @pl.when(is_outer)
        def _():
            send_a(c).wait_send()
        @pl.when(is_inner)
        def _():
            send_fo(c).wait_send()
            @pl.when(is_root(c))
            def _():
                send_fi(c).wait_send()
            @pl.when(jnp.logical_not(is_root(c)))
            def _():
                send_b(c).wait_send()

def share(u, gd, rows, chunk, l1, l2):
    n = rows // chunk
    D = pltpu.SemaphoreType.DMA
    return pl.pallas_call(
        functools.partial(share_kernel, gd, rows, chunk, l1, l2),
        out_shape=jax.ShapeDtypeStruct((gd, rows, 128), jnp.bfloat16),
        in_specs=[pl.BlockSpec(memory_space=pltpu.VMEM)],
        out_specs=pl.BlockSpec(memory_space=pltpu.VMEM),
        scratch_shapes=[pltpu.VMEM((rows, 128), jnp.bfloat16)] * 3 + [
            D((n,)), D((n,)), D((n,)), D((max(gd - 1, 1), n)), D((n,)), D((n,)), D((n,)), D((max(gd - 1, 1), n))],
        compiler_params=pltpu.CompilerParams(collective_id=9, has_side_effects=True, vmem_limit_bytes=24 * 2**20),
        name="share",
    )(u)


def ring_gather(value, axis, group):
    size = lax.axis_size(axis)
    found = [value]
    for k in range(1, group):
        pairs = [(s, s // group * group + (s % group + k) % group) for s in range(size)]
        found.append(lax.ppermute(value, axis, pairs))
    return found


def neighbour_rows(block, width):
    count = lax.axis_size("narrow")
    up = [(i, i + 1) for i in range(count - 1)]
    down = [(i + 1, i) for i in range(count - 1)]
    before = lax.ppermute(block[-width:], "narrow", up)
    after = lax.ppermute(block[:width], "narrow", down)
    return jnp.concatenate([before, block, after], axis=0)


def per_device(
    weights, first_moment, second_moment, outer_momentum, noisy_input, target,
    text_tokens, text_mask, noise_level, aug_level, crop_size,
):
    length = first_moment.shape[1]
    wide_count = lax.axis_size("wide")
    narrow_count = lax.axis_size("narrow")
    gd = wide_count // GROUPS
    wide_pos = lax.axis_index("wide")
    narrow_pos = lax.axis_index("narrow")
    spot = wide_pos % gd
    width = HEADS * HEAD
    kv_block = 2 * width // narrow_count
    kv_len = TEXT_D * kv_block
    shard_len = weights.shape[0]
    rest_len = shard_len - kv_len

    own_kv_w = weights[:kv_len].astype(BF16).reshape(TEXT_D, kv_block)
    rest_all = lax.all_gather(weights[kv_len:].astype(BF16), "narrow", axis=0, tiled=True)
    rest_all = rest_all.reshape(-1, C)
    n_table = LEVELS * 2
    conv_w = rest_all[: 9 * C]
    table = rest_all[9 * C : 9 * C + n_table].reshape(LEVELS, 2 * C)
    at = 9 * C + n_table
    gains = rest_all[at : at + 4].astype(F32)
    query_w = rest_all[at + 4 : at + 4 + width].reshape(C, width)
    out_w = rest_all[at + 4 + width :]

    noisy = noisy_input[0]
    band, columns, _ = noisy.shape
    x = noisy.astype(F32).reshape(-1, C)
    group_of = jnp.arange(C, dtype=jnp.int32) // (C // NORM_GROUPS)
    same = (group_of[:, None] == group_of[None, :]).astype(F32)
    stat = lax.psum(jnp.stack([jnp.sum(x, axis=0), jnp.sum(x * x, axis=0)]), "narrow")
    stat = jnp.dot(stat, same, precision=lax.Precision.HIGHEST)
    count = H * W * C // NORM_GROUPS
    mean = stat[0] / count
    spread = lax.rsqrt(stat[1] / count - mean * mean + EPS_NORM)
    film = (table[noise_level[0]].astype(F32) + table[NOISE_LEVELS + aug_level[0]].astype(F32))
    gain = gains[0] * (1.0 + film[:C])
    offset = gains[1] * (1.0 + film[:C]) + film[C:]
    zero = jnp.zeros((C,), F32)
    vecs = jnp.stack([mean, spread, gain, offset, gains[2], gains[3], zero, zero])
    noisy_ext = neighbour_rows(noisy, 2)
    target_ext = neighbour_rows(target[0], 1)

    text_all = lax.all_gather(text_tokens[0], "narrow", axis=0, tiled=True)
    mask_all = lax.all_gather(text_mask[0], "narrow", axis=0, tiled=True)
    tok = text_all.shape[0]
    own_cols = dot(text_all, own_kv_w).astype(BF16)
    keyval = lax.all_gather(own_cols, "narrow", axis=1, tiled=True)
    key_ok = ((mask_all > 0) | (jnp.arange(tok) == 0)).astype(F32)[None, :]
    crop = crop_size[0]
    info = jnp.stack([narrow_pos * band, crop]).astype(jnp.int32)

    dconv_w, y_t, z_t, sums = run_main(
        info, noisy_ext, target_ext, vecs, conv_w, query_w, out_w, keyval, key_ok
    )

    half = width // kv_block
    both = jnp.concatenate([z_t, y_t], axis=1).reshape(C, narrow_count, -1).transpose(1, 0, 2)
    own_x = lax.psum_scatter(both, "narrow", scatter_dimension=0, tiled=False)
    is_key = narrow_pos < half
    scale = jnp.where(is_key, 1.0 / math.sqrt(HEAD), 1.0)
    own_x = own_x * scale
    head_block = kv_block // HEAD
    col0 = (narrow_pos % half) * kv_block
    right = jnp.where(
        is_key,
        lax.dynamic_slice_in_dim(query_w, col0, kv_block, axis=1),
        lax.dynamic_slice_in_dim(out_w, col0, kv_block, axis=0).T,
    )
    dkv, dproj = [], []
    for h in range(head_block):
        xs = own_x[:, h * tok : (h + 1) * tok]
        cols = slice(h * HEAD, (h + 1) * HEAD)
        dkv.append(dot(xs.astype(BF16), right[:, cols], TN))
        dproj.append(dot(xs.astype(BF16), own_cols[:, cols]))
    dkv = jnp.concatenate(dkv, axis=1)
    dproj = jnp.concatenate(dproj, axis=1)
    text_group = jnp.concatenate(ring_gather(text_all, "wide", gd), axis=0)
    dkv_group = jnp.concatenate(ring_gather(dkv, "wide", gd), axis=0)

    def group_sum(value):
        return sum(ring_gather(value, "wide", gd))

    dproj = lax.all_gather(group_sum(dproj), "narrow", axis=0, tiled=False)
    grad_query = jnp.concatenate([dproj[n] for n in range(half)], axis=1)
    grad_out = jnp.concatenate([dproj[half + n].T for n in range(half)], axis=0)
    sums = lax.psum(sums, "narrow")
    a, b = sums[0], sums[1]
    g_rows = jnp.stack([(1.0 + film[:C]) * b, (1.0 + film[:C]) * a, sums[2], sums[3]])
    dfilm = jnp.concatenate([gains[0] * b + gains[1] * a, a])
    small = jnp.concatenate([g_rows, dfilm.reshape(2, C)], axis=0)
    levels = jnp.stack([noise_level[0], NOISE_LEVELS + aug_level[0]])
    smalls = ring_gather(small, "wide", gd)
    level_list = ring_gather(levels, "wide", gd)
    grad_gains = sum(s[:4] for s in smalls)
    grad_table = jnp.zeros((LEVELS, 2 * C), F32)
    ids = jnp.arange(LEVELS, dtype=jnp.int32)[:, None]
    for s, lv in zip(smalls, level_list):
        d = s[4:].reshape(1, 2 * C)
        grad_table = grad_table + jnp.where(ids == lv[0], d, 0.0) + jnp.where(ids == lv[1], d, 0.0)
    grad_conv = group_sum(lax.psum(dconv_w, "narrow"))
    rest_grad = jnp.concatenate(
        [grad_conv.reshape(-1), grad_table.reshape(-1), grad_gains.reshape(-1),
         grad_query.reshape(-1), grad_out.reshape(-1)]
    )
    rest_sq = jnp.sum(rest_grad * rest_grad)
    rest_shard = lax.dynamic_slice_in_dim(rest_grad, narrow_pos * rest_len, rest_len)

    gram = dot(text_group, text_group, (((1,), (1,)), ((), ())))
    kv_sq = jnp.sum(dkv_group * jnp.dot(gram, dkv_group, precision=lax.Precision.HIGHEST))
    kv_sq = lax.psum(kv_sq, "narrow")
    crops = lax.all_gather(crop, "wide")
    counts = (jnp.minimum(crops, H) * jnp.minimum(crops, columns)).astype(F32)
    total = jnp.sum(counts)
    own_group = jnp.arange(wide_count) // gd == wide_pos // gd
    group_count = jnp.sum(jnp.where(own_group, counts, 0.0))
    loss = lax.psum(jnp.sum(sums[4]), "wide")
    norm = jnp.sqrt(kv_sq + rest_sq) / total
    clip = jnp.minimum(1.0, CLIP_NORM / norm) / total

    start = spot * length
    i0, j0 = start // kv_block, start % kv_block
    tiles = pl.cdiv(length + C, TROWS * C)
    text_rows = tiles * C
    padded = jnp.pad(text_group, ((0, 0), (0, text_rows + 1)))
    text_a = lax.dynamic_slice_in_dim(padded, i0, text_rows, axis=1)
    text_b = lax.dynamic_slice_in_dim(padded, i0 + 1, text_rows, axis=1)
    rolled = jnp.roll(dkv_group, -j0, axis=1)
    wrapped = jnp.arange(kv_block)[None, :] >= kv_block - j0
    dkv_ab = jnp.concatenate(
        [jnp.where(wrapped, 0.0, rolled), jnp.where(wrapped, rolled, 0.0)], axis=0
    ).astype(BF16)
    full = tiles * TROWS * C
    rest_line = jnp.concatenate([jnp.zeros((length,), F32), rest_shard, jnp.zeros((full,), F32)])
    rest_piece = lax.dynamic_slice_in_dim(
        rest_line, jnp.maximum(start - kv_len + length, 0), full
    ).reshape(-1, C)
    moment_one, moment_two, step = run_adam(
        jnp.stack([start % C]).astype(jnp.int32),
        jnp.stack([clip, INNER_RATE * group_count / total]),
        text_a, text_b, dkv_ab, rest_piece, first_moment, second_moment,
    )
    chunk = 320
    rows = pl.cdiv(length // C + 2, chunk) * chunk
    spread_steps = share(step, gd, rows, chunk, 2, 4)
    all_rows = shard_len // C
    averaged = 0.0
    for p in range(gd):
        r0 = p * length // C
        use = min(rows, all_rows - r0)
        averaged = averaged + jnp.pad(
            spread_steps[p, :use].astype(F32), ((r0, all_rows - r0 - use), (0, 0))
        )
    weights2 = weights.reshape(-1, C)
    outer2 = outer_momentum.reshape(-1, C)
    averaged = averaged + INNER_RATE * DECAY_RATE * weights2
    momentum_out = OUTER_MOMENTUM * outer2 + averaged
    new_weights = weights2 - OUTER_RATE * (averaged + OUTER_MOMENTUM * momentum_out)
    return (
        new_weights.reshape(-1), momentum_out.reshape(-1), moment_one, moment_two,
        loss[None], total[None],
    )


def solution(mesh):
    placed = (
        P("narrow"),
        P("narrow", "wide"),
        P("narrow", "wide"),
        P("narrow"),
        P("wide", "narrow", None, None),
        P("wide", "narrow", None, None),
        P("wide", "narrow", None),
        P("wide", "narrow"),
        P("wide"),
        P("wide"),
        P("wide"),
    )
    return jax.shard_map(
        per_device,
        mesh=mesh,
        in_specs=placed,
        out_specs=(P("narrow"), P("narrow"), P("narrow", "wide"), P("narrow", "wide"), P(), P()),
        check_vma=False,
    )
```

time: 1290 us -> 543 us (0.42)
  waiting for transfers between devices: 391 us -> 64.7 us
  matrix products: 329 us -> 10.3 us
  other arithmetic: 221 us -> 81.6 us
  Pallas kernels: 0 us -> 138 us
  local copies, waits for them, and re-layouts: 244 us -> 143 us
    dot_general x42 -> x12, matrix products: 329 us -> 10.3 us  [the longest x10 7.76 us: dot(): return lax.dot_general(a, b, dims, preferred_element_type=F32)]
    psum x1, waiting for transfers between devices: 278 us -> 28.4 us  [per_device(): grad_conv = group_sum(lax.psum(dconv_w, 'narrow'))]
    pallas_call x0 -> x3, Pallas kernels: none -> 138 us  [the longest x1 71.4 us: share(): pl.pallas_call(functools.partial(share_kernel, gd, rows, chunk, l1, l2),...]
    concatenate x1 -> x2, local copies, waits for them, and re-layouts: 1.9 us -> 82.8 us  [the longest x1 81.8 us: per_device(): jnp.concatenate([jnp.zeros((length,), F32), rest_shard, jnp.zeros((full,)...]
    dynamic_update_slice x1 -> x0, local copies, waits for them, and re-layouts: 77.4 us -> none  [per_device(): lax.dynamic_update_slice(holder, weighted[None, :], (inner_pos, jnp.int32...]
    mul x4 -> x0, other arithmetic: 65.5 us -> none  [the longest x1 52.3 us: per_device(): BETA_TWO * second_moment[0] + (1.0 - BETA_TWO) * clipped * clipped]
    reduce_sum x12 -> x4, other arithmetic: 45.8 us -> 4.82 us  [the longest x1 3.05 us: per_device(): rest_sq = jnp.sum(rest_grad * rest_grad)]
    unnamed x6 -> x5, waiting for transfers between devices: 40.8 us -> 0.75 us
  transfers between devices with their start and end apart: 10 -> 15, of which waited for: 4 -> 5; matrix products, arithmetic and copies ran while one was open for 10% -> 18% of each run, Pallas kernels for 0% -> 10%
where the time goes in v1:
time: 543 us; the launch traced here: 536 us
  local copies, waits for them, and re-layouts  143 us (26%)
  Pallas kernels  138 us (25%)
  other arithmetic  81.6 us (15%)
  waiting for transfers between devices  64.7 us (12%)
  blocking collectives  58.9 us (11%)
  between operations  21 us (4%)
  starting transfers between devices  17.9 us (3%)
  matrix products  10.3 us (2%)
    concatenate x1, local copies, waits for them, and re-layouts, per_device(): jnp.concatenate([jnp.zeros((length,), F32), rest_shard, jnp.zeros((full,)...  81.8 us
    pallas_call x1, Pallas kernels, share(): pl.pallas_call(functools.partial(share_kernel, gd, rows, chunk, l1, l2),...  71.4 us
    pallas_call x1, Pallas kernels, run_main(): pl.pallas_call(functools.partial(main_kernel, band, columns, H, HEADS), o...  53.7 us
    all_gather x1, other arithmetic, per_device(): lax.all_gather(weights[kv_len:].astype(BF16), 'narrow', axis=0, tiled=True)  30.6 us
    psum x1, waiting for transfers between devices, per_device(): grad_conv = group_sum(lax.psum(dconv_w, 'narrow'))  28.4 us
    unnamed x62, local copies, waits for them, and re-layouts  23.8 us
    reshape x1, other arithmetic, per_device(): momentum_out.reshape(-1)  22.3 us
    psum x1, blocking collectives, per_device(): loss = lax.psum(jnp.sum(sums[4]), 'wide')  21.1 us
  transfers between devices with their start and end apart: 15, of which 5 were waited for; matrix products, arithmetic and copies ran while one was open for 18% of the time, Pallas kernels for 10%

profile of v1, /device:TPU:0, one launch (start us, length us, event | category | flops | bytes accessed | tf_op | source)
XLA Modules:
  0.0 535.6 jit_solution(9858142895012404047)
XLA Ops:
  16.7 4.6 collective-permute-start
  22.6 4.3 convert.23
  29.1 4.6 reshape.228
  36.9 11.6 %all-reduce.3 = s32[8]{0:T(128)S(1)} all-reduce(s32[8]{0:T(128)S(1)} %dynamic-update-slice), channel_id=1, replica_groups=mesh['wide'=8,'narrow'=4] {'wide'}, use_global_device_ids=true, to_apply=%add.3 | all-reduce | flops 8 | bytes 64
  50.4 3.8 slice.277
  56.2 7.6 %convert_element_type.60 = bf16[4096,512]{1,0:T(8,128)(2,1)} reshape(bf16[2097152]{0:T(1024)(128)(2,1)} %slice.277) | data formatting | bytes 8388608 | tf_op jit(solution)/shard_map/convert_element_type | solution.py:447
  63.8 7.4 %all-reduce.4 = s32[128]{0:T(128)S(1)} all-reduce(s32[128]{0:T(128)S(1)} %bitcast_dynamic-update-slice_fusion.1), channel_id=3, replica_groups=mesh['wide'=8,'narrow'=4] {'narrow'}, use_global_device_ids=true, to_apply=%add.4 | all-reduce | flops 128 | bytes 1024
  71.2 5.6 %psum.35 = f32[2,128]{1,0:T(2,128)S(1)} all-reduce(f32[2,128]{1,0:T(2,128)S(1)} %pad_maximum_fusion.9), channel_id=1, replica_groups=mesh['wide'=8,'narrow'=4] {'narrow'}, use_global_device_ids=true, to_apply=%region_3.4 | all-reduce | flops 256 | bytes 2048 | tf_op jit(solution)/shard_map/psum | solution.py:463
  82.9 3.2 convolution_convert_fusion
  86.1 6.7 %all_gather.24.keyval = bf16[128,2048]{1,0:T(8,128)(2,1)S(1)} all-gather(bf16[128,512]{1,0:T(8,128)(2,1)S(1)} %convolution_convert_fusion), channel_id=1, replica_groups=mesh['wide'=8,'narrow'=4] {'narrow'}, dimensions={1}, use_global_device_ids=true | all-gather | bytes 655360 | tf_op jit(solution)/shard_map/all_gather | solution.py:480
  92.9 30.6 %reduce.3 = bf16[4,168064]{1,0:T(4,128)(2,1)} reduce(bf16[4,1,168064]{2,1,0:T(2,128)(2,1)} %all-gather.12.cloned.1.call-done, bf16[]{:T(256)} %constant.196), dimensions={1}, to_apply=%all-gather.3.reduce_sub_computation | reduce | bytes 2689026 | tf_op jit(solution)/shard_map/all_gather | solution.py:448
  123.4 3.3 reshape.229
  136.0 53.7 %main.1 = (f32[1152,128]{1,0:T(8,128)S(1)}, f32[128,1024]{1,0:T(8,128)S(1)}, f32[128,1024]{1,0:T(8,128)S(1)}, f32[8,128]{1,0:T(8,128)S(1)}) custom-call(s32[2]{0:T(128)S(1)} %pad_add_fusion.info, bf16[36,128,128]{2,1,0:T(8,128)(2,1)S(1)} %pad_maximum_fusion.1.noisy, bf16[34,128,128]{2,1,0:T(8,128)(2,1)S(1)} %pad_maximum_fusion.2.target, ...), custom_call_target="tpu_custom_call" | custom-call | tf_op jit(solution)/shard_map/main/pallas_call | solution.py:204
  195.2 28.4 %all-reduce.8.cloned.1.call-done = f32[1152,128]{1,0:T(8,128)} async-done(((f32[1152,128]{1,0:T(8,128)}), f32[1152,128]{1,0:T(8,128)}) %all-reduce.8.cloned.1.call-update) | async-done | bytes 589840 | tf_op jit(solution)/shard_map/psum | solution.py:533
  230.8 6.9 %collective-permute-done.6 = f32[1152,128]{1,0:T(8,128)S(1)} collective-permute-done((f32[1152,128]{1,0:T(8,128)}, f32[1152,128]{1,0:T(8,128)S(1)}, u32[]{:S(2)}, u32[]{:S(2)}) %collective-permute-start.6) | collective-permute-done | bytes 589856 | tf_op jit(solution)/shard_map/ppermute | solution.py:417
  238.5 12.9 %reduce-scatter.2.cloned.1.call-done = f32[1,128,512]{2,1,0:T(8,128)} async-done(((f32[4,128,512]{2,1,0:T(8,128)}), f32[1,128,512]{2,1,0:T(8,128)}) %reduce-scatter.2.cloned.1.call-update) | async-done | bytes 262160 | tf_op jit(solution)/shard_map/reduce_scatter | solution.py:491
  256.9 6.2 %collective-permute-done.4 = f32[128,512]{1,0:T(8,128)S(1)} collective-permute-done((f32[128,512]{1,0:T(8,128)S(1)}, f32[128,512]{1,0:T(8,128)S(1)}, u32[]{:S(2)}, u32[]{:S(2)}) %collective-permute-start.4) | collective-permute-done | bytes 262176 | tf_op jit(solution)/shard_map/ppermute | solution.py:417
  265.5 6.5 %all-reduce.5 = (f32[]{:T(128)}, f32[8,128]{1,0:T(8,128)S(1)}) all-reduce(f32[]{:T(128)} %fusion.4, f32[8,128]{1,0:T(8,128)S(1)} %get-tuple-element.16), channel_id=1, replica_groups=mesh['wide'=8,'narrow'=4] {'narrow'}, use_global_device_ids=true, to_apply=%region_6.7 | all-reduce | flops 1025 | bytes 8200 | tf_op jit(solution)/shard_map/psum | solution.py:543
  277.9 21.1 %psum.39 = f32[1]{0:T(128)} all-reduce(f32[1]{0:T(128)} %bitcast.50), channel_id=1, replica_groups=mesh['wide'=8,'narrow'=4] {'wide'}, use_global_device_ids=true, to_apply=%region_12.13 | all-reduce | flops 1 | bytes 8 | tf_op jit(solution)/shard_map/psum | solution.py:549
  302.6 9.4 %all-gather.10.cloned.1.call-done = f32[512,512]{0,1:T(8,128)} async-done(((f32[128,512]{0,1:T(8,128)}), f32[512,512]{0,1:T(8,128)}) %all-gather.10.cloned.1.call-update) | async-done | bytes 1048592 | tf_op jit(solution)/shard_map/all_gather | solution.py:516
  332.1 81.8 %concatenate.63 = f32[2480320]{0:T(1024)} concatenate(f32[1132608]{0:T(1024)} %broadcast_in_dim.109, f32[168064]{0:T(1024)} %dynamic_slice.35, f32[1179648]{0:T(1024)} %broadcast_in_dim.110), dimensions={0} | concatenate | bytes 19842560 | tf_op jit(solution)/shard_map/concatenate | solution.py:566
  421.6 13.4 %adam.1 = (f32[1,1132608]{1,0:T(1,128)}, f32[1,1132608]{1,0:T(1,128)}, bf16[9216,128]{1,0:T(8,128)(2,1)S(1)}) custom-call(s32[1]{0:T(128)} %bitcast.1.ints, f32[2]{0:T(128)S(1)} %pad_maximum_fusion.11.scal, bf16[256,2304]{1,0:T(8,128)(2,1)S(1)} %get-tuple-element.31.text_a, bf16[256,2304]{1,0:T(8,128)(2,1)S(1)} %get-tuple-element.30.text_b, ...), custom_call_target="tpu_custom_call" | custom-call | tf_op jit(solution)/shard_map/adam/pallas_call | solution.py:277
  435.0 71.4 %share.1 = bf16[2,8960,128]{2,1,0:T(8,128)(2,1)S(1)} custom-call(bf16[9216,128]{1,0:T(8,128)(2,1)S(1)} %get-tuple-element.17.u_ref), custom_call_target="tpu_custom_call" | custom-call | tf_op jit(solution)/shard_map/share/pallas_call | solution.py:400
  506.8 22.3 %fusion.2 = (f32[2265216]{0:T(1024)}, f32[2265216]{0:T(1024)}) fusion(f32[2265216]{0:T(1024)} %param.14, f32[2265216]{0:T(1024)S(1)} %bitcast.144, bf16[8849,128]{1,0:T(8,128)(2,1)S(1)} %slice_bitcast_fusion.1, bf16[8960,128]{1,0:T(8,128)(2,1)S(1)} %slice_bitcast_fusion), kind=kLoop, calls=%fused_computation.5 | loop fusion | flops 24917376 | bytes 40802560 | tf_op jit(solution)/shard_map/reshape | solution.py:592
  (164 shorter events, 87.4 us)
Async XLA Ops:
  7.2 75.1 %all-gather.8.cloned.1.call-start = ((), (), s32[]{:S(2)}) async-start(), calls=%async_computation.3 | async-start | bytes 1310720 | tf_op jit(solution)/shard_map/all_gather | solution.py:476
  7.9 85.0 %all-gather.12.cloned.1.call-start = ((), (), s32[]{:S(2)}) async-start(), calls=%async_computation.5 | async-start | bytes 3361280 | tf_op jit(solution)/shard_map/all_gather | solution.py:448
  9.3 69.0 %collective-permute-start.7 = (s32[2]{0:T(128)S(1)}, s32[2]{0:T(128)S(1)}, u32[]{:S(2)}, u32[]{:S(2)}) collective-permute-start(s32[2]{0:T(128)S(1)} %pad_add_fusion.1), channel_id=1, source_target_pairs={{0,4},{4,0},{8,12},{12,8},{16,20},{20,16},{24,28},{28,24},{1,5},{5... | collective-permute-start | bytes 32 | tf_op jit(solution)/shard_map/ppermute | solution.py:417
  13.1 67.7 %collective-permute-start.2 = (bf16[1,128,128]{2,1,0:T(8,128)(2,1)S(1)}, bf16[1,128,128]{2,1,0:T(8,128)(2,1)S(1)}, u32[]{:S(2)}, u32[]{:S(2)}) collective-permute-start(bf16[1,128,128]{2,1,0:T(8,128)(2,1)S(1)} %get-tuple-element.38), channel_id=1, source_target_pairs={{0,1},{1,2},{2,3},{4,5},{5,6},{6,7},{8,9},{9,10},{10,11},{12,13},{... | collective-permute-start | bytes 98312 | tf_op jit(solution)/shard_map/ppermute | solution.py:425
  14.5 66.2 %collective-permute-start.3 = (bf16[1,128,128]{2,1,0:T(8,128)(2,1)S(1)}, bf16[1,128,128]{2,1,0:T(8,128)(2,1)S(1)}, u32[]{:S(2)}, u32[]{:S(2)}) collective-permute-start(bf16[1,128,128]{2,1,0:T(8,128)(2,1)S(1)} %get-tuple-element.39), channel_id=1, source_target_pairs={{1,0},{2,1},{3,2},{5,4},{6,5},{7,6},{9,8},{10,9},{11,10},{13,12},{... | collective-permute-start | bytes 98312 | tf_op jit(solution)/shard_map/ppermute | solution.py:426
  16.7 64.2 %collective-permute-start = (bf16[2,128,128]{2,1,0:T(8,128)(2,1)S(1)}, bf16[2,128,128]{2,1,0:T(8,128)(2,1)S(1)}, u32[]{:S(2)}, u32[]{:S(2)}) collective-permute-start(bf16[2,128,128]{2,1,0:T(8,128)(2,1)S(1)} %get-tuple-element.40), channel_id=1, source_target_pairs={{0,1},{1,2},{2,3},{4,5},{5,6},{6,7},{8,9},{9,10},{10,11},{12,13},{... | collective-permute-start | bytes 196616 | tf_op jit(solution)/shard_map/ppermute | solution.py:425
  21.3 59.6 %collective-permute-start.1 = (bf16[2,128,128]{2,1,0:T(8,128)(2,1)S(1)}, bf16[2,128,128]{2,1,0:T(8,128)(2,1)S(1)}, u32[]{:S(2)}, u32[]{:S(2)}) collective-permute-start(bf16[2,128,128]{2,1,0:T(8,128)(2,1)S(1)} %get-tuple-element.41), channel_id=1, source_target_pairs={{1,0},{2,1},{3,2},{5,4},{6,5},{7,6},{9,8},{10,9},{11,10},{13,12},{... | collective-permute-start | bytes 196616 | tf_op jit(solution)/shard_map/ppermute | solution.py:426
  33.6 189.9 %all-reduce.8.cloned.1.call-start = ((), (), s32[]{:S(2)}) async-start(), calls=%async_computation.2 | async-start | bytes 1179648 | tf_op jit(solution)/shard_map/psum | solution.py:533
  82.3 142.7 %collective-permute-start.5 = (bf16[128,4096]{1,0:T(8,128)(2,1)}, bf16[128,4096]{1,0:T(8,128)(2,1)}, u32[]{:S(2)}, u32[]{:S(2)}) collective-permute-start(bf16[128,4096]{1,0:T(8,128)(2,1)} %bitcast.149), channel_id=1, source_target_pairs={{0,4},{4,0},{8,12},{12,8},{16,20},{20,16},{24,28},{28,24},{1,5},{5... | collective-permute-start | bytes 3145736 | tf_op jit(solution)/shard_map/ppermute | solution.py:417
  86.1 40.6 %copy-start.9 = (bf16[128,512]{1,0:T(8,128)(2,1)}, bf16[128,512]{1,0:T(8,128)(2,1)S(1)}, u32[]{:S(2)}) copy-start(bf16[128,512]{1,0:T(8,128)(2,1)S(1)} %convolution_convert_fusion) | copy-start | bytes 393220
  192.2 59.3 %reduce-scatter.2.cloned.1.call-start = ((), (), s32[]{:S(2)}) async-start(), calls=%async_computation.1 | async-start | bytes 1310720 | tf_op jit(solution)/shard_map/reduce_scatter | solution.py:491
  192.4 32.7 %copy-start.7 = (bf16[1,128,4096]{2,1,0:T(8,128)(2,1)S(1)}, bf16[1,128,4096]{2,1,0:T(8,128)(2,1)}, u32[]{:S(2)}) copy-start(bf16[1,128,4096]{2,1,0:T(8,128)(2,1)} %all-gather.8.cloned.1.call-done) | copy-start | bytes 3145732
  194.9 117.2 %all-gather.10.cloned.1.call-start = ((), (), s32[]{:S(2)}) async-start(), calls=%async_computation.4 | async-start | bytes 1310720 | tf_op jit(solution)/shard_map/all_gather | solution.py:516
  223.6 14.1 %collective-permute-start.6 = (f32[1152,128]{1,0:T(8,128)}, f32[1152,128]{1,0:T(8,128)S(1)}, u32[]{:S(2)}, u32[]{:S(2)}) collective-permute-start(f32[1152,128]{1,0:T(8,128)} %all-reduce.8.cloned.1.call-done), channel_id=1, source_target_pairs={{0,4},{4,0},{8,12},{12,8},{16,20},{20,16},{24,28},{28,24},{1,5},{5... | collective-permute-start | bytes 1769480 | tf_op jit(solution)/shard_map/ppermute | solution.py:417
  230.8 43.6 %copy-start.16 = (pred[512]{0:T(512)(128)(4,1)S(1)}, pred[512]{0:T(512)(128)(4,1)}, u32[]{:S(2)}) copy-start(pred[512]{0:T(512)(128)(4,1)} %iota_compare_fusion.4) | copy-start | bytes 1540
  253.9 9.3 %collective-permute-start.4 = (f32[128,512]{1,0:T(8,128)S(1)}, f32[128,512]{1,0:T(8,128)S(1)}, u32[]{:S(2)}, u32[]{:S(2)}) collective-permute-start(f32[128,512]{1,0:T(8,128)S(1)} %pad_maximum_fusion.6), channel_id=1, source_target_pairs={{0,4},{4,0},{8,12},{12,8},{16,20},{20,16},{24,28},{28,24},{1,5},{5... | collective-permute-start | bytes 786440 | tf_op jit(solution)/shard_map/ppermute | solution.py:417
  256.3 42.7 %copy-start.13 = (pred[1024]{0:T(1024)(128)(4,1)S(1)}, pred[1024]{0:T(1024)(128)(4,1)}, u32[]{:S(2)}) copy-start(pred[1024]{0:T(1024)(128)(4,1)} %get-tuple-element.58) | copy-start | bytes 3076
  256.3 42.7 %copy-start.14 = (pred[1024]{0:T(1024)(128)(4,1)S(1)}, pred[1024]{0:T(1024)(128)(4,1)}, u32[]{:S(2)}) copy-start(pred[1024]{0:T(1024)(128)(4,1)} %get-tuple-element.55) | copy-start | bytes 3076
  256.3 42.7 %copy-start.15 = (pred[1024]{0:T(1024)(128)(4,1)S(1)}, pred[1024]{0:T(1024)(128)(4,1)}, u32[]{:S(2)}) copy-start(pred[1024]{0:T(1024)(128)(4,1)} %get-tuple-element.56) | copy-start | bytes 3076
  256.3 19.9 %collective-permute-start.9 = (f32[128,512]{0,1:T(8,128)}, f32[128,512]{0,1:T(8,128)}, u32[]{:S(2)}, u32[]{:S(2)}) collective-permute-start(f32[128,512]{0,1:T(8,128)} %pad_maximum_fusion.7), channel_id=1, source_target_pairs={{0,4},{4,0},{8,12},{12,8},{16,20},{20,16},{24,28},{28,24},{1,5},{5... | collective-permute-start | bytes 786440 | tf_op jit(solution)/shard_map/ppermute | solution.py:417
  272.6 26.4 %collective-permute-start.8 = (f32[6,128]{1,0:T(8,128)S(1)}, f32[6,128]{1,0:T(8,128)S(1)}, u32[]{:S(2)}, u32[]{:S(2)}) collective-permute-start(f32[6,128]{1,0:T(8,128)S(1)} %pad_maximum_fusion.8), channel_id=1, source_target_pairs={{0,4},{4,0},{8,12},{12,8},{16,20},{20,16},{24,28},{28,24},{1,5},{5... | collective-permute-start | bytes 9224 | tf_op jit(solution)/shard_map/ppermute | solution.py:417
  421.6 85.2 %slice-start = ((s8[9064448]{0:T(1024)(128)(4,1)}), s8[4194304]{0:T(1024)(128)(4,1)S(1)}, s32[]{:S(2)}) async-start(s8[9064448]{0:T(1024)(128)(4,1)} %bitcast.143), calls=%async_computation.6 | async-start | bytes 8388608
  421.6 85.2 %slice-start.1 = ((s8[9064448]{0:T(1024)(128)(4,1)}), s8[4194304]{0:T(1024)(128)(4,1)S(1)}, s32[]{:S(2)}) async-start(s8[9064448]{0:T(1024)(128)(4,1)} %bitcast.143), calls=%async_computation.7 | async-start | bytes 8388608
  435.0 71.8 %slice-start.2 = ((s8[9064448]{0:T(1024)(128)(4,1)}), s8[675840]{0:T(1024)(128)(4,1)S(1)}, s32[]{:S(2)}) async-start(s8[9064448]{0:T(1024)(128)(4,1)} %bitcast.143), calls=%async_computation.8 | async-start | bytes 1351680
  (16 other events, 137.0 us)
Sparse Core Ops, SparseCore 0:
  9.6 19.4 all-gather.7
  33.8 28.7 all-gather.11
  192.3 31.2 all-reduce.7
  226.5 24.8 reduce-scatter.1
  299.1 12.8 all-gather.9

commit v2 on v1

v2 whole, which is shorter than its diff:
```python
import functools
import math

import jax
import jax.numpy as jnp
from jax import lax
from jax.experimental import pallas as pl
from jax.experimental.pallas import tpu as pltpu
from jax.sharding import PartitionSpec as P

MESH = pl.DeviceIdType.MESH
C = 128
NORM_GROUPS = 32
HEADS = 8
HEAD = 128
TEXT_D = 4096
H = 128
W = 128
NOISE_LEVELS = 1000
AUG_LEVELS = 24
LEVELS = NOISE_LEVELS + AUG_LEVELS
GROUPS = 4
STEP = 8


EPS_NORM = 1e-05
CLIP_NORM = 0.002
BETA_ONE = 0.9
BETA_TWO = 0.99
INNER_RATE = 0.01
DECAY_RATE = 0.01
ADAM_EPS = 1e-08
OUTER_RATE = 0.7
OUTER_MOMENTUM = 0.9

TN = (((0,), (0,)), ((), ()))
F32 = jnp.float32
BF16 = jnp.bfloat16
LOG2E = 1.4426950408889634
LN2 = 0.6931471805599453
NT = (((1,), (1,)), ((), ()))
TILE = 2


def dot(a, b, dims=(((1,), (0,)), ((), ()))):
    return lax.dot_general(a, b, dims, preferred_element_type=F32)


def two_parts(value):
    top = value.astype(BF16)
    return top, (value - top.astype(F32)).astype(BF16)


def shifted(value, by, keep):
    return jnp.where(keep, pltpu.roll(value, by, 0), 0.0)


def main_kernel(
    band, columns, height, heads,
    rest_rows, info, noisy, target, small, rest, keyval,
    blocks, dconv_w, packet, right,
    act3, diff3, m_cat, m_cat_t, n_cat, n_cat_t, conv_t, probs, dscore, wt3, y_t, z_t, sums,
    stage, query, out_w,
):
    tok, kv_block = keyval.shape[1:]
    width = heads * HEAD
    per_block = kv_block // HEAD
    row0 = info[0]
    crop = info[1]
    pix = TILE * columns
    first_gain, first_query = 9 * C + 2 * LEVELS, 9 * C + 2 * LEVELS + 4
    first_out = first_query + C * heads

    def take(first, count, place):
        while count:
            owner, local = divmod(first, rest_rows)
            use = min(count, rest_rows - local)
            a = local // 16 * 16
            b = (local + use + 15) // 16 * 16
            stage[0 : b - a, :] = rest[owner, a:b, :].astype(F32)
            place(stage[local - a : local - a + use, :], use)
            first, count = first + use, count - use

    def filler(ref):
        at = [0]

        def place(value, use):
            ref[at[0] : at[0] + use, :] = value
            at[0] += use

        return place

    gains = []
    take(first_gain, 4, lambda value, use: gains.append(value))
    gains = gains[0] if len(gains) == 1 else jnp.concatenate(gains, axis=0)
    take(first_query, C * heads, filler(query))
    take(first_out, width, filler(out_w))
    conv_w = rest.at[0]
    total = small[0] + small[1] + small[2] + small[3]
    lane_group = lax.broadcasted_iota(jnp.int32, (C, C), 0) // (C // NORM_GROUPS)
    same = (lane_group == lax.broadcasted_iota(jnp.int32, (C, C), 1) // (C // NORM_GROUPS)).astype(F32)
    stats = jnp.dot(total, same, precision=lax.Precision.HIGHEST, preferred_element_type=F32)
    count = height * columns * C // NORM_GROUPS
    mean = stats[0:1] * (1.0 / count)
    spread = lax.rsqrt(stats[1:2] * (1.0 / count) - mean * mean + EPS_NORM)
    film_scale, film_shift = 1.0 + total[2:3], total[3:4]
    gain = gains[0:1] * film_scale
    offset = gains[1:2] * film_scale + film_shift
    ln_gain, ln_offset = gains[2:3], gains[3:4]
    quarter = tok // 4
    masks = [small[owner, 4:5, 0:quarter] for owner in range(4)]
    ok = (jnp.concatenate(masks, axis=1) > 0.0) | (lax.broadcasted_iota(jnp.int32, (1, tok), 1) == 0)
    factor = LOG2E / math.sqrt(HEAD)
    for head in range(heads):
        cols = slice(head * HEAD, (head + 1) * HEAD)
        tcols = slice(head * tok, (head + 1) * tok)
        block, at = head // per_block, head % per_block * HEAD
        query_head = query[pl.ds(head, C, stride=heads), :].astype(BF16)
        out_head = out_w[cols, :].astype(BF16)
        m_head = dot(query_head, keyval[block, :, at : at + HEAD], NT) * factor

        @pl.when(info[2] == block)
        def _():
            right[:, at : at + HEAD] = query_head

        @pl.when(info[2] == block + heads // per_block)
        def _():
            right[:, at : at + HEAD] = out_w[cols, :].T.astype(BF16)

        top, rest = two_parts(m_head)
        m_cat[:C, tcols] = top
        m_cat[C:, tcols] = rest
        top, rest = two_parts(m_head.T)
        m_cat_t[tcols, :C] = top
        m_cat_t[tcols, C:] = rest
        n_head = dot(keyval[block + heads // per_block, :, at : at + HEAD], out_head)
        top, rest = two_parts(n_head)
        n_cat[tcols, :C] = top
        n_cat[tcols, C:] = rest
        top, rest = two_parts(n_head.T)
        n_cat_t[:C, tcols] = top
        n_cat_t[C:, tcols] = rest
    for tap in range(9):
        rows = slice(tap * C, (tap + 1) * C)
        wt3[rows, :] = conv_w[rows, :].astype(F32).T.astype(BF16)
    y_t[...] = jnp.zeros_like(y_t)
    z_t[...] = jnp.zeros_like(z_t)
    conv_t[...] = jnp.zeros_like(conv_t)
    sums[...] = jnp.zeros_like(sums)
    place = lax.broadcasted_iota(jnp.int32, (columns, C), 0)
    not_first, not_last = place > 0, place < columns - 1
    slope = spread * gain
    base = offset - mean * slope

    @pl.loop(0, band + 4)
    def _(r):
        scaled = noisy[r].astype(F32) * slope + base
        value = scaled * jax.nn.sigmoid(scaled)
        row = row0 + r - 2
        value = jnp.where(jnp.logical_and(row >= 0, row < height), value, 0.0)
        value = value.astype(BF16).astype(F32)
        act3[r, :, 0:C] = shifted(value, 1, not_first).astype(BF16)
        act3[r, :, C : 2 * C] = value.astype(BF16)
        act3[r, :, 2 * C : 3 * C] = shifted(value, columns - 1, not_last).astype(BF16)

    pix_row = lax.broadcasted_iota(jnp.int32, (pix, C), 0) // columns
    pix_col = lax.broadcasted_iota(jnp.int32, (pix, C), 0) % columns
    @pl.loop(0, (band + 2) // TILE)
    def _(t):
        q = t * TILE
        conv = noisy[pl.ds(q + 1, TILE)].astype(F32).reshape(pix, C)
        for dy in range(3):
            window = act3[pl.ds(q + dy, TILE)].reshape(pix, 3 * C)
            conv = conv + dot(window, conv_w[dy * 3 * C : (dy + 1) * 3 * C, :])
        centered = conv - jnp.mean(conv, axis=1, keepdims=True)
        rs = lax.rsqrt(jnp.mean(centered * centered, axis=1, keepdims=True) + EPS_NORM)
        xhat = centered * rs
        layered = xhat * ln_gain + ln_offset
        low = layered.astype(BF16)
        low2 = jnp.concatenate([low, low], axis=1)
        for head in range(heads):
            tcols = slice(head * tok, (head + 1) * tok)
            score = dot(low2, m_cat[:, tcols])
            score = jnp.where(ok, score, -1e30)
            e = jnp.exp2(score - jnp.max(score, axis=1, keepdims=True))
            p = e * (1.0 / jnp.sum(e, axis=1, keepdims=True))
            probs[:, tcols] = p.astype(BF16)
        mixed = dot(probs[...], n_cat[...])
        output = conv + mixed[:, :C] + mixed[:, C:]
        row = row0 + q - 1 + pix_row
        valid = (row >= 0) & (row < crop) & (pix_col < crop)
        err = jnp.where(valid, output - target[pl.ds(q, TILE)].astype(F32).reshape(pix, C), 0.0)
        own_row = q + pix_row
        own = (own_row >= 1) & (own_row <= band)
        err_own = jnp.where(own, err, 0.0)
        sums[4:5, :] += jnp.sum(err_own * err_own, axis=0, keepdims=True)
        dout = 2.0 * err
        dout_low = dout.astype(BF16)
        dout2 = jnp.concatenate([dout_low, dout_low], axis=1)
        for head in range(heads):
            tcols = slice(head * tok, (head + 1) * tok)
            dprob = dot(dout2, n_cat_t[:, tcols])
            p = probs[:, tcols].astype(F32)
            pd = p * dprob
            ds = pd - p * jnp.sum(pd, axis=1, keepdims=True)
            dscore[:, tcols] = ds.astype(BF16)
        dlay2 = dot(dscore[...], m_cat_t[...])
        dlay = (dlay2[:, :C] + dlay2[:, C:]) * LN2
        dlay_own = jnp.where(own, dlay, 0.0)
        sums[2:3, :] += jnp.sum(dlay_own * xhat, axis=0, keepdims=True)
        sums[3:4, :] += jnp.sum(dlay_own, axis=0, keepdims=True)
        dxh = dlay * ln_gain
        dconv = dout + rs * (
            dxh
            - jnp.mean(dxh, axis=1, keepdims=True)
            - xhat * jnp.mean(dxh * xhat, axis=1, keepdims=True)
        )
        dout_t = (2.0 * err_own).T.astype(BF16)
        lay_t = jnp.where(own, layered, 0.0).T.astype(BF16)
        y_t[...] += dot(dout_t, probs[...])
        z_t[...] += dot(lay_t, dscore[...])
        dconv_t = jnp.where(own, dconv, 0.0).T.astype(BF16)
        for dy in range(3):
            window = act3[pl.ds(q + dy, TILE)].reshape(pix, 3 * C)
            conv_t[:, dy * 3 * C : (dy + 1) * 3 * C] += dot(dconv_t, window)
        for k in range(TILE):
            one = dconv[k * columns : (k + 1) * columns]
            diff3[q + k, :, 0:C] = shifted(one, columns - 1, not_last).astype(BF16)
            diff3[q + k, :, C : 2 * C] = one.astype(BF16)
            diff3[q + k, :, 2 * C : 3 * C] = shifted(one, 1, not_first).astype(BF16)

    @pl.loop(0, band // TILE)
    def _(t):
        r = t * TILE
        grad = jnp.zeros((pix, C), F32)
        for dy in range(3):
            window = diff3[pl.ds(r + 2 - dy, TILE)].reshape(pix, 3 * C)
            grad = grad + dot(window, wt3[dy * 3 * C : (dy + 1) * 3 * C, :])
        x = noisy[pl.ds(r + 2, TILE)].astype(F32).reshape(pix, C)
        scaled = x * slope + base
        sig = jax.nn.sigmoid(scaled)
        ds = grad * (sig * (1.0 + scaled * (1.0 - sig)))
        sums[0:1, :] += jnp.sum(ds, axis=0, keepdims=True)
        sums[1:2, :] += jnp.sum(ds * ((x - mean) * spread), axis=0, keepdims=True)

    share_rows = dconv_w.shape[1]
    full = conv_t[...].T
    for owner in range(4):
        dconv_w[owner] = full[owner * share_rows : (owner + 1) * share_rows].astype(BF16)
        part = z_t if owner < 2 else y_t
        at = owner % 2 * per_block * tok
        blocks[owner] = part[:, at : at + per_block * tok].astype(BF16)
    a, b = sums[0:1], sums[1:2]
    packet[0:1] = film_scale * b
    packet[1:2] = film_scale * a
    packet[2:4] = sums[2:4]
    packet[4:5] = gains[0:1] * b + gains[1:2] * a
    packet[5:6] = a
    packet[6:7] = sums[4:5]
    lane = lax.broadcasted_iota(jnp.int32, (1, C), 1)
    facts = jnp.zeros((1, C), F32)
    for k, fact in enumerate((info[3], info[4], crop)):
        facts = jnp.where(lane == k, fact.astype(F32), facts)
    packet[7:8] = jnp.where(row0 == 0, facts, 0.0)


def run_main(info, noisy_ext, target_ext, small, rest, keyval, rest_rows):
    band = target_ext.shape[0] - 2
    columns = target_ext.shape[1]
    tok, kv_block = keyval.shape[1:]
    vmem = pl.BlockSpec(memory_space=pltpu.VMEM)
    pix = TILE * columns
    assert 9 * C <= rest_rows and kv_block % HEAD == 0 and HEAD == C
    return pl.pallas_call(
        functools.partial(main_kernel, band, columns, H, HEADS, rest_rows),
        out_shape=(
            jax.ShapeDtypeStruct((4, C, kv_block // HEAD * tok), BF16),
            jax.ShapeDtypeStruct((4, 9 * C // 4, C), BF16),
            jax.ShapeDtypeStruct((8, C), F32),
            jax.ShapeDtypeStruct((C, kv_block), BF16),
        ),
        in_specs=[pl.BlockSpec(memory_space=pltpu.SMEM)] + [vmem] * 5,
        out_specs=(vmem,) * 4,
        scratch_shapes=[
            pltpu.VMEM((band + 4, columns, 3 * C), BF16),
            pltpu.VMEM((band + 2, columns, 3 * C), BF16),
            pltpu.VMEM((2 * C, HEADS * tok), BF16),
            pltpu.VMEM((HEADS * tok, 2 * C), BF16),
            pltpu.VMEM((HEADS * tok, 2 * C), BF16),
            pltpu.VMEM((2 * C, HEADS * tok), BF16),
            pltpu.VMEM((C, 9 * C), F32),
            pltpu.VMEM((pix, HEADS * tok), BF16),
            pltpu.VMEM((pix, HEADS * tok), BF16),
            pltpu.VMEM((9 * C, C), BF16),
            pltpu.VMEM((C, HEADS * tok), F32),
            pltpu.VMEM((C, HEADS * tok), F32),
            pltpu.VMEM((8, C), F32),
            pltpu.VMEM((rest.shape[1], C), F32),
            pltpu.VMEM((C * HEADS, C), F32),
            pltpu.VMEM((HEADS * HEAD, C), F32),
        ],
        compiler_params=pltpu.CompilerParams(vmem_limit_bytes=40 * 2**20),
        name="main",
    )(info, noisy_ext, target_ext, small, rest, keyval)


def cross_ids():
    n = lax.axis_index("narrow")
    mate = n + 1 - 2 * lax.rem(n, 2)
    across = lax.rem(n + 2, 4)
    corner = lax.rem(mate + 2, 4)
    return n, mate, across, corner


def to_narrow(src, dst, send_sem, recv_sem, device):
    return pltpu.make_async_remote_copy(
        src_ref=src, dst_ref=dst, send_sem=send_sem, recv_sem=recv_sem,
        device_id={"narrow": device}, device_id_type=MESH,
    )


class Gather:
    def __init__(self, view, sems, ids):
        self.view, self.sems = view, sems
        self.n, self.mate, self.across, self.corner = ids

    def _copy(self, block, slot, device):
        ref = self.view(block)
        return to_narrow(ref, ref, self.sems.at[0, slot], self.sems.at[1, slot], device)

    def start(self):
        self._copy(self.n, 1, self.across).start()
        self._copy(self.n, 0, self.mate).start()

    def relay(self):
        self._copy(self.across, 1, self.across).wait_recv()
        self._copy(self.across, 2, self.mate).start()

    def wait(self):
        self._copy(self.mate, 0, self.mate).wait_recv()
        self._copy(self.corner, 2, self.mate).wait_recv()

    def drain(self):
        self._copy(self.n, 1, self.across).wait_send()
        self._copy(self.n, 0, self.mate).wait_send()
        self._copy(self.across, 2, self.mate).wait_send()


def rest_needs(rest_rows):
    first, last = 9 * C, 9 * C + 2 * LEVELS
    needs = []
    for owner in range(4):
        lo, hi = owner * rest_rows, (owner + 1) * rest_rows
        keep = [r for r in ((lo, min(hi, first)), (max(lo, last), hi)) if r[0] < r[1]]
        assert len(keep) <= 1
        if keep:
            a, b = keep[0][0] - lo, keep[0][1] - lo
            needs.append((a // 16 * 16, (b + 15) // 16 * 16))
        else:
            needs.append(None)
    return needs


KPARTS = 4
WPARTS = 8


def front_kernel(
    kv_rows, rest_rows, noise_level, aug_level, weights, noisy, target, text, mask,
    noisy_ext, target_ext, text_all, rest_all, keyval, own_kv, small,
    wide_f32, wide_bf, rest_f32, acc,
    w_sem, in_sem, text_sem, rest_sem, kv_sem, small_sem, halo_sem,
):
    ids = cross_ids()
    n, mate, across, corner = ids
    barrier = pltpu.get_barrier_semaphore()
    for other in (mate, across, corner):
        pl.semaphore_signal(barrier, inc=1, device_id={"narrow": other}, device_id_type=MESH)
    band = noisy.shape[1]
    tokens, depth = text.shape[1:]
    in_text = pltpu.make_async_copy(text.at[0], text_all.at[n], in_sem.at[0])
    in_text.start()
    in_rest = pltpu.make_async_copy(
        weights.at[pl.ds(kv_rows, rest_rows)], rest_f32.at[pl.ds(0, rest_rows)], in_sem.at[1]
    )
    in_rest.start()
    in_noisy = pltpu.make_async_copy(noisy.at[0], noisy_ext.at[pl.ds(2, band)], in_sem.at[2])
    in_noisy.start()
    w_step = kv_rows // WPARTS
    in_w = [
        pltpu.make_async_copy(
            weights.at[pl.ds(k * w_step, w_step)], wide_f32.at[pl.ds(k * w_step, w_step)], w_sem.at[k]
        )
        for k in range(WPARTS)
    ]
    for copy in in_w:
        copy.start()
    in_target = pltpu.make_async_copy(target.at[0], target_ext.at[pl.ds(1, band)], in_sem.at[3])
    in_target.start()
    pl.semaphore_wait(barrier, 3)

    k_step = depth // KPARTS
    texts = [
        Gather(
            lambda b, k=k: text_all.at[b, :, pl.ds(k * k_step, k_step)], text_sem.at[k], ids
        )
        for k in range(KPARTS)
    ]
    in_text.wait()
    for part in texts:
        part.start()

    in_rest.wait()
    for k in range(2):
        row_sum = jnp.zeros((1, C), F32)
        for level in (noise_level[0], NOISE_LEVELS + aug_level[0]):
            row = 9 * C + 2 * level + k - n * rest_rows
            found = rest_f32[pl.ds(jnp.clip(row, 0, rest_rows - 1), 1), :]
            found = found.astype(BF16).astype(F32)
            row_sum = row_sum + jnp.where((row >= 0) & (row < rest_rows), found, 0.0)
        small[n, 2 + k : 3 + k, :] = row_sum
    small[n, 4:8, :] = jnp.zeros((4, C), F32)
    small[n, 4:5, 0:tokens] = mask[...].astype(F32)
    in_noisy.wait()

    def add_row(r, sums):
        x = noisy_ext[r + 2].astype(F32)
        return (
            sums[0] + jnp.sum(x.reshape(-1, 8, C), axis=0),
            sums[1] + jnp.sum((x * x).reshape(-1, 8, C), axis=0),
        )

    zero = jnp.zeros((8, C), F32)
    one, two = lax.fori_loop(0, band, add_row, (zero, zero))
    small[n, 0:1, :] = jnp.sum(one, axis=0, keepdims=True)
    small[n, 1:2, :] = jnp.sum(two, axis=0, keepdims=True)
    others = (mate, across, corner)

    def small_copy(slot, block):
        return to_narrow(
            small.at[block], small.at[block], small_sem.at[0, slot], small_sem.at[1, slot], others[slot]
        )

    for slot in range(3):
        small_copy(slot, n).start()

    in_target.wait()
    up = jnp.maximum(n - 1, 0)
    down = jnp.minimum(n + 1, 3)
    noisy_up = to_narrow(
        noisy_ext.at[pl.ds(2, 2)], noisy_ext.at[pl.ds(band + 2, 2)], halo_sem.at[0, 0], halo_sem.at[1, 0], up
    )
    noisy_down = to_narrow(
        noisy_ext.at[pl.ds(band, 2)], noisy_ext.at[pl.ds(0, 2)], halo_sem.at[0, 1], halo_sem.at[1, 1], down
    )
    target_up = to_narrow(
        target_ext.at[pl.ds(1, 1)], target_ext.at[pl.ds(band + 1, 1)], halo_sem.at[0, 2], halo_sem.at[1, 2], up
    )
    target_down = to_narrow(
        target_ext.at[pl.ds(band, 1)], target_ext.at[pl.ds(0, 1)], halo_sem.at[0, 3], halo_sem.at[1, 3], down
    )

    @pl.when(n > 0)
    def _():
        noisy_up.start()
        target_up.start()

    @pl.when(n < 3)
    def _():
        noisy_down.start()
        target_down.start()

    @pl.when(n == 0)
    def _():
        noisy_ext[0:2] = jnp.zeros((2,) + noisy_ext.shape[1:], BF16)
        target_ext[0:1] = jnp.zeros((1,) + target_ext.shape[1:], BF16)

    @pl.when(n == 3)
    def _():
        noisy_ext[band + 2 : band + 4] = jnp.zeros((2,) + noisy_ext.shape[1:], BF16)
        target_ext[band + 1 : band + 2] = jnp.zeros((1,) + target_ext.shape[1:], BF16)

    needs = rest_needs(rest_rows)
    rest_all[n] = rest_f32[...].astype(BF16)

    def rest_copy(owner, slot, device):
        a, b = needs[owner]
        ref = rest_all.at[owner, pl.ds(a, b - a)]
        return to_narrow(ref, ref, rest_sem.at[0, slot, owner], rest_sem.at[1, slot, owner], device)

    for owner in range(4):
        if needs[owner] is not None:
            @pl.when(n == owner)
            def _():
                rest_copy(owner, 1, across).start()
                rest_copy(owner, 0, mate).start()

    parts = wide_bf.shape[1] // C
    rows = 256
    for k in range(WPARTS):
        in_w[k].wait()

        @pl.loop(k * w_step // parts // rows, (k + 1) * w_step // parts // rows)
        def _(i):
            for j in range(parts):
                wide_bf[pl.ds(pl.multiple_of(i * rows, rows), rows), j * C : (j + 1) * C] = wide_f32[
                    pl.ds(i * rows * parts + j, rows, stride=parts), :
                ].astype(BF16)

    acc[...] = jnp.zeros_like(acc)
    for k in range(KPARTS):
        texts[k].relay()
    for k in range(KPARTS):
        texts[k].wait()

        @pl.loop(0, k_step // 512)
        def _(i):
            at = pl.ds(pl.multiple_of(k * k_step + i * 512, 512), 512)
            acc[...] += dot(text_all[:, :, at].reshape(4 * tokens, 512), wide_bf[at, :])

    keyval[n] = acc[...].astype(BF16)
    own_kv[...] = acc[...].astype(BF16)
    keys = Gather(lambda b: keyval.at[b], kv_sem, ids)
    keys.start()

    for owner in range(4):
        if needs[owner] is not None:
            @pl.when(across == owner)
            def _():
                rest_copy(owner, 1, across).wait_recv()
                rest_copy(owner, 2, mate).start()

    keys.relay()
    for slot, block in ((0, mate), (1, across), (2, corner)):
        small_copy(slot, block).wait_recv()
        small_copy(slot, n).wait_send()

    @pl.when(n > 0)
    def _():
        noisy_down.wait_recv()
        target_down.wait_recv()
        noisy_up.wait_send()
        target_up.wait_send()

    @pl.when(n < 3)
    def _():
        noisy_up.wait_recv()
        target_up.wait_recv()
        noisy_down.wait_send()
        target_down.wait_send()

    for owner in range(4):
        if needs[owner] is not None:
            @pl.when(mate == owner)
            def _():
                rest_copy(owner, 0, mate).wait_recv()

            @pl.when(corner == owner)
            def _():
                rest_copy(owner, 2, mate).wait_recv()

            @pl.when(n == owner)
            def _():
                rest_copy(owner, 1, across).wait_send()
                rest_copy(owner, 0, mate).wait_send()

            @pl.when(across == owner)
            def _():
                rest_copy(owner, 2, mate).wait_send()

    keys.wait()
    keys.drain()
    for part in texts:
        part.drain()


def run_front(noise_level, aug_level, weights2, noisy, target, text, mask):
    _, band, columns, _ = noisy.shape
    _, tokens, depth = text.shape
    kv_block = 2 * HEADS * HEAD // 4
    kv_rows = depth * kv_block // C
    rest_rows = weights2.shape[0] - kv_rows
    rest_pad = (rest_rows + 15) // 16 * 16
    vmem = pl.BlockSpec(memory_space=pltpu.VMEM)
    smem = pl.BlockSpec(memory_space=pltpu.SMEM)
    hbm = pl.BlockSpec(memory_space=pl.ANY)
    D = pltpu.SemaphoreType.DMA
    return pl.pallas_call(
        functools.partial(front_kernel, kv_rows, rest_rows),
        out_shape=(
            jax.ShapeDtypeStruct((band + 4, columns, C), BF16),
            jax.ShapeDtypeStruct((band + 2, columns, C), BF16),
            jax.ShapeDtypeStruct((4, tokens, depth), BF16),
            jax.ShapeDtypeStruct((4, rest_pad, C), BF16),
            jax.ShapeDtypeStruct((4, 4 * tokens, kv_block), BF16),
            jax.ShapeDtypeStruct((4 * tokens, kv_block), BF16),
            jax.ShapeDtypeStruct((4, 8, C), F32),
        ),
        in_specs=[smem, smem, hbm, hbm, hbm, hbm, vmem],
        out_specs=(vmem,) * 7,
        scratch_shapes=[
            pltpu.VMEM((kv_rows, C), F32),
            pltpu.VMEM((depth, kv_block), BF16),
            pltpu.VMEM((rest_pad, C), F32),
            pltpu.VMEM((4 * tokens, kv_block), F32),
            D((WPARTS,)), D((4,)), D((KPARTS, 2, 3)), D((2, 3, 4)), D((2, 3)), D((2, 3)), D((2, 4)),
        ],
        compiler_params=pltpu.CompilerParams(
            collective_id=1, has_side_effects=True, vmem_limit_bytes=36 * 2**20
        ),
        name="front",
    )(noise_level, aug_level, weights2, noisy, target, text, mask)


def mid_kernel(
    gd, height, columns, blocks, conv, packet, right, *refs,
):
    kvs, texts, refs = refs[:gd], refs[gd : 2 * gd], refs[2 * gd :]
    (
        dkv_all, conv_all, t_all, small_all, scal,
        near_b, near_c, sum_b, sum_c, far_b, far_c, own_b, own_c, group_b, group_c,
        packets, wides, t_own, t_send, c_send, gram, norms, conv_sum,
        near_sem, far_sem, group_sem, packet_sem, wide_sem, norm_sem, give_sem,
    ) = refs
    ids = cross_ids()
    n, mate, across, corner = ids
    others = (mate, across, corner)
    wide_count = wides.shape[0]
    wide = lax.axis_index("wide")
    group = wide // gd
    spot = lax.rem(wide, gd)
    tok, kv_block = kvs[0].shape
    heads = kv_block // HEAD
    barrier = pltpu.get_barrier_semaphore()
    for other in others:
        pl.semaphore_signal(barrier, inc=1, device_id={"narrow": other}, device_id_type=MESH)

    @pl.loop(1, wide_count)
    def _(k):
        pl.semaphore_signal(
            barrier, inc=1, device_id={"wide": lax.rem(wide + k, wide_count)}, device_id_type=MESH
        )

    packets[n] = packet[...]
    pl.semaphore_wait(barrier, 3 + wide_count - 1)

    def near(slot, which):
        owner = corner if slot == 0 else mate
        src, dst = ((blocks, near_b), (conv, near_c))[which]
        return to_narrow(
            src.at[owner], dst.at[slot], near_sem.at[0, slot, which], near_sem.at[1, slot, which], mate
        )

    for slot in range(2):
        for which in range(2):
            near(slot, which).start()

    def packet_copy(slot, block):
        return to_narrow(
            packets.at[block], packets.at[block],
            packet_sem.at[0, slot], packet_sem.at[1, slot], others[slot],
        )

    for slot in range(3):
        packet_copy(slot, n).start()

    def far(which):
        src, dst = ((sum_b, far_b), (sum_c, far_c))[which]
        return to_narrow(src, dst, far_sem.at[0, which], far_sem.at[1, which], across)

    near(0, 0).wait_recv()
    sum_b[...] = (blocks[across].astype(F32) + near_b[0].astype(F32)).astype(BF16)
    far(0).start()
    near(0, 1).wait_recv()
    sum_c[...] = (conv[across].astype(F32) + near_c[0].astype(F32)).astype(BF16)
    far(1).start()

    for slot, block in enumerate(others):
        packet_copy(slot, block).wait_recv()
    item = packets[0] + packets[1] + packets[2] + packets[3]
    wides[wide] = item

    def wide_copy(k, block):
        return pltpu.make_async_remote_copy(
            src_ref=wides.at[block], dst_ref=wides.at[block],
            send_sem=wide_sem.at[0, k - 1], recv_sem=wide_sem.at[1, k - 1],
            device_id={"wide": lax.rem(wide + k, wide_count)}, device_id_type=MESH,
        )

    @pl.loop(1, wide_count)
    def _(k):
        wide_copy(k, wide).start()

    depth = texts[0].shape[-1]
    gram[...] = jnp.zeros_like(gram)

    @pl.loop(0, depth // 1024)
    def _(i):
        at = pl.ds(pl.multiple_of(i * 1024, 1024), 1024)
        for a in range(gd):
            left = texts[a][:, :, at].reshape(tok, 1024)
            for b in range(a, gd):
                part = dot(left, texts[b][:, :, at].reshape(tok, 1024), NT)
                gram[a * tok : (a + 1) * tok, b * tok : (b + 1) * tok] += part

    near(1, 0).wait_recv()
    near(1, 1).wait_recv()
    far(0).wait_recv()
    own_b[...] = (
        blocks[n].astype(F32) + near_b[1].astype(F32) + far_b[...].astype(F32)
    ).astype(BF16)

    def group_copy(k, which):
        src, dst = ((own_b, group_b), (own_c, group_c))[which]
        return pltpu.make_async_remote_copy(
            src_ref=src, dst_ref=dst.at[k - 1],
            send_sem=group_sem.at[0, which, k - 1], recv_sem=group_sem.at[1, which, k - 1],
            device_id={"wide": group * gd + lax.rem(spot + k, gd)}, device_id_type=MESH,
        )

    for k in range(1, gd):
        group_copy(k, 0).start()
    far(1).wait_recv()
    conv_sum[...] = conv[n].astype(F32) + near_c[1].astype(F32) + far_c[...].astype(F32)
    own_c[...] = conv_sum[...].astype(BF16)
    for k in range(1, gd):
        group_copy(k, 1).start()

    scale = jnp.where(n < 2, 1.0 / math.sqrt(HEAD), 1.0)

    def project(k, value):
        for h in range(heads):
            cols = slice(h * HEAD, (h + 1) * HEAD)
            part = value[:, h * tok : (h + 1) * tok]
            dkv_all[k * tok : (k + 1) * tok, cols] = (dot(part, right[:, cols], TN) * scale).astype(BF16)
            term = dot(part, kvs[k][:, cols]) * scale
            t_own[:, cols] = term if k == 0 else t_own[:, cols] + term

    project(0, own_b[...])
    for k in range(1, gd):
        group_copy(k, 0).wait_recv()
        project(k, group_b[k - 1])
        group_copy(k, 1).wait_recv()
        conv_sum[...] += group_c[k - 1].astype(F32)
    t_send[...] = t_own[...].astype(BF16)
    c_send[...] = conv_sum[...].astype(BF16)

    q_rows = 96
    q_from = 80

    def give_conv(src_n):
        return to_narrow(c_send, conv_all.at[src_n], give_sem.at[0, 0], give_sem.at[1, src_n], 0)

    def give_head(src_n):
        at = pl.ds(0, q_rows)
        return to_narrow(t_send.at[at], t_all.at[src_n, at], give_sem.at[0, 1], give_sem.at[1, src_n], 2)

    def give_tail(src_n):
        at = pl.ds(q_from, C - q_from)
        return to_narrow(t_send.at[at], t_all.at[src_n, at], give_sem.at[0, 2], give_sem.at[1, src_n], 3)

    def give_values():
        return to_narrow(t_send, t_all.at[2], give_sem.at[0, 1], give_sem.at[1, 2], 3)

    for k in range(4):
        @pl.when(n == k)
        def _():
            if k < 2:
                give_head(k).start()
                give_tail(k).start()
            if k == 2:
                give_values().start()
            if k > 0:
                give_conv(k).start()
            else:
                conv_all[0] = c_send[...]
            if k == 3:
                t_all[3] = t_send[...]

    @pl.loop(1, wide_count)
    def _(k):
        wide_copy(k, lax.rem(wide + wide_count - k, wide_count)).wait_recv()

    sq = jnp.sum(t_own[...] * t_own[...]) + jnp.sum(conv_sum[...] * conv_sum[...])
    for a in range(gd):
        da = dkv_all[a * tok : (a + 1) * tok, :]
        for b in range(a, gd):
            db = dkv_all[b * tok : (b + 1) * tok, :]
            top, low = two_parts(gram[a * tok : (a + 1) * tok, b * tok : (b + 1) * tok])
            part = jnp.sum(da.astype(F32) * (dot(top, db) + dot(low, db)))
            sq = sq + (part if a == b else 2.0 * part)
    gains = jnp.zeros((4, C), F32)
    shared = jnp.zeros((1, C), F32)
    for a in range(gd):
        mine = wides[group * gd + a]
        small_all[a] = mine
        gains = gains + mine[0:4]
        for b in range(gd):
            his = wides[group * gd + b]
            same = (mine[7:8, 0:1] == his[7:8, 0:1]).astype(F32) + (mine[7:8, 1:2] == his[7:8, 1:2]).astype(F32)
            shared = shared + same * (mine[4:5] * his[4:5] + mine[5:6] * his[5:6])
    shared_sq = jnp.sum(gains * gains) + jnp.sum(shared)
    norms[n] = jnp.full((8, C), sq + jnp.where(n == 0, shared_sq, 0.0), F32)

    def norm_copy(slot, block):
        return to_narrow(
            norms.at[block], norms.at[block], norm_sem.at[0, slot], norm_sem.at[1, slot], others[slot]
        )

    for slot in range(3):
        norm_copy(slot, n).start()

    def tally(k, found):
        there = wides[k]
        crop = there[7:8, 2:3]
        pixels = jnp.minimum(crop, float(height)) * jnp.minimum(crop, float(columns))
        mine = jnp.where(k // gd == group, pixels, 0.0)
        return found[0] + pixels, found[1] + mine, found[2] + jnp.sum(there[6:7], axis=1, keepdims=True)

    none = jnp.zeros((1, 1), F32)
    total, own_count, loss = lax.fori_loop(0, wide_count, tally, (none, none, none))
    for slot, block in enumerate(others):
        norm_copy(slot, block).wait_recv()
    squares = norms[0, 0:1] + norms[1, 0:1] + norms[2, 0:1] + norms[3, 0:1]
    norm = jnp.sqrt(squares) / total
    scal[0:1] = jnp.minimum(1.0, CLIP_NORM / norm) / total
    scal[1:2] = jnp.broadcast_to(INNER_RATE * own_count / total, (1, C))
    scal[2:3] = jnp.broadcast_to(loss, (1, C))
    scal[3:4] = jnp.broadcast_to(total, (1, C))
    scal[4:8] = jnp.zeros((4, C), F32)

    for k in range(4):
        @pl.when(n == k)
        def _():
            if k < 2:
                give_head(k).wait_send()
                give_tail(k).wait_send()
            if k == 2:
                give_values().wait_send()
                give_head(0).wait_recv()
                give_head(1).wait_recv()
            if k == 3:
                give_tail(0).wait_recv()
                give_tail(1).wait_recv()
                give_values().wait_recv()
            if k > 0:
                give_conv(k).wait_send()
            else:
                for j in range(1, 4):
                    give_conv(j).wait_recv()
    for slot in range(2):
        for which in range(2):
            near(slot, which).wait_send()
    for which in range(2):
        far(which).wait_send()
        for k in range(1, gd):
            group_copy(k, which).wait_send()
    for slot in range(3):
        packet_copy(slot, n).wait_send()
        norm_copy(slot, n).wait_send()

    @pl.loop(1, wide_count)
    def _(k):
        wide_copy(k, wide).wait_send()


def run_mid(gd, wide_count, blocks, conv, packet, right, kvs, texts):
    tok, kv_block = kvs[0].shape
    vmem = pl.BlockSpec(memory_space=pltpu.VMEM)
    D = pltpu.SemaphoreType.DMA
    bshape, cshape = blocks.shape[1:], conv.shape[1:]
    V = pltpu.VMEM
    few = max(gd - 1, 1)
    return pl.pallas_call(
        functools.partial(mid_kernel, gd, H, W),
        out_shape=(
            jax.ShapeDtypeStruct((gd * tok, kv_block), BF16),
            jax.ShapeDtypeStruct((4,) + cshape, BF16),
            jax.ShapeDtypeStruct((4, C, kv_block), BF16),
            jax.ShapeDtypeStruct((gd, 8, C), F32),
            jax.ShapeDtypeStruct((8, C), F32),
        ),
        in_specs=[vmem] * (4 + 2 * gd),
        out_specs=(vmem,) * 5,
        scratch_shapes=[
            V((2,) + bshape, BF16), V((2,) + cshape, BF16), V(bshape, BF16), V(cshape, BF16),
            V(bshape, BF16), V(cshape, BF16), V(bshape, BF16), V(cshape, BF16),
            V((few,) + bshape, BF16), V((few,) + cshape, BF16),
            V((4, 8, C), F32), V((wide_count, 8, C), F32),
            V((C, kv_block), F32), V((C, kv_block), BF16), V(cshape, BF16),
            V((gd * tok, gd * tok), F32), V((4, 8, C), F32), V(cshape, F32),
            D((2, 2, 2)), D((2, 2)), D((2, 2, few)), D((2, 3)), D((2, wide_count)), D((2, 3)), D((2, 4)),
        ],
        compiler_params=pltpu.CompilerParams(
            collective_id=2, has_side_effects=True, vmem_limit_bytes=48 * 2**20
        ),
        name="mid",
    )(blocks, conv, packet, right, *kvs, *texts)


TROWS = 512


def adam_kernel(
    gd, length, kv_rows, rest_rows, where, *refs,
):
    firsts, texts, refs = refs[:gd], refs[gd : 2 * gd], refs[2 * gd :]
    (
        dkv, conv, t_all, small, scal, first, second, first_out, second_out, step_out,
        nat, rest, shift, carry,
    ) = refs
    s = pl.program_id(0)
    tiles = pl.num_programs(0) - 1
    tok = dkv.shape[0] // gd
    n, lane0, row_off, row_shift, block0 = (where[k] for k in range(5))
    kv_blocks = kv_rows // TROWS
    parts = TROWS // C

    def natural(text_refs, block):
        @pl.when(block < kv_blocks)
        def _():
            text = jnp.concatenate([ref[...].reshape(tok, C) for ref in text_refs], axis=0)
            grad = dot(text, dkv[...], TN)
            for j in range(parts):
                nat[pl.ds(TROWS + j, C, stride=parts), :] = grad[:, j * C : (j + 1) * C]

        @pl.when(block >= kv_blocks)
        def _():
            at = jnp.minimum(block - kv_blocks, rest.shape[0] // TROWS - 1) * TROWS
            nat[TROWS : 2 * TROWS, :] = rest[pl.ds(pl.multiple_of(at, TROWS), TROWS), :]

    @pl.when(s == 0)
    def _():
        rest[...] = jnp.zeros_like(rest)
        carry[...] = jnp.zeros_like(carry)
        shift[...] = jnp.zeros_like(shift)
        first_table, first_gain = 9 * C, 9 * C + 2 * LEVELS
        first_query = first_gain + 4
        first_out = first_query + C * HEADS
        quarter = conv.shape[1]
        width = dkv.shape[1]
        heads = width // HEAD
        for owner in range(4):
            lo, hi = owner * rest_rows, (owner + 1) * rest_rows

            @pl.when(n == owner)
            def _():
                for k in range(4):
                    a, b = max(lo, k * quarter), min(hi, (k + 1) * quarter)
                    if a < b:
                        assert (a, b) == (k * quarter, (k + 1) * quarter)
                        rest[a - lo : b - lo, :] = conv[k].astype(F32)
                a, b = max(lo, first_query), min(hi, first_out)
                if a < b:
                    for h in range(HEADS):
                        c0 = max(0, -(-(a - first_query - h) // HEADS))
                        c1 = min(C, -(-(b - first_query - h) // HEADS))
                        cols = slice(h % heads * HEAD, h % heads * HEAD + HEAD)
                        c_lo, c_hi = c0 // 16 * 16, (c1 + 15) // 16 * 16
                        value = t_all[h // heads, c_lo:c_hi, cols].astype(F32)
                        start = first_query + c0 * HEADS + h - lo
                        rest[pl.ds(start, c1 - c0, stride=HEADS), :] = value[c0 - c_lo : c1 - c_lo]
                for h in range(HEADS):
                    a, b = first_out + h * HEAD, first_out + (h + 1) * HEAD
                    if lo <= a and b <= hi:
                        cols = slice(h % heads * HEAD, h % heads * HEAD + HEAD)
                        rest[a - lo : b - lo, :] = t_all[2 + h // heads, :, cols].astype(F32).T
                    else:
                        assert b <= lo or hi <= a
                if lo <= first_gain and first_gain + 4 <= hi:
                    total = small[0, 0:4]
                    for k in range(1, gd):
                        total = total + small[k, 0:4]
                    rest[first_gain - lo : first_gain + 4 - lo, :] = total

        for k in range(2 * gd):
            for half in range(2):
                row = first_table + 2 * where[5 + k] + half - n * rest_rows

                @pl.when((row >= 0) & (row < rest_rows))
                def _():
                    rest[pl.ds(row, 1), :] += small[k // 2, 4 + half : 5 + half]

        natural(firsts, block0)

    nat[0:TROWS, :] = nat[TROWS : 2 * TROWS, :]
    natural(texts, block0 + s + 1)

    lane = lax.broadcasted_iota(jnp.int32, (TROWS, C), 1)
    row = lax.broadcasted_iota(jnp.int32, (TROWS, C), 0)
    same_row = nat[pl.ds(row_off, TROWS), :]
    next_row = nat[pl.ds(row_off + 1, TROWS), :]
    g = pltpu.roll(jnp.where(lane >= lane0, same_row, next_row), C - lane0, 1) * scal[0:1]
    one = BETA_ONE * first.reshape(TROWS, C)[...] + (1.0 - BETA_ONE) * g
    two = BETA_TWO * second.reshape(TROWS, C)[...] + (1.0 - BETA_TWO) * g * g
    first_out.reshape(TROWS, C)[...] = one
    second_out.reshape(TROWS, C)[...] = two
    fixed_one = one * (scal[1:2] * (1.0 / (1.0 - BETA_ONE**STEP)))
    fixed_two = two * (1.0 / (1.0 - BETA_TWO**STEP))
    step = fixed_one / (jnp.sqrt(fixed_two) + ADAM_EPS)
    step = jnp.where((s * TROWS + row) * C + lane < length, step, 0.0)
    turned = pltpu.roll(step, lane0, 1)
    above = pltpu.roll(turned, 1, 0)
    above = jnp.where(row == 0, carry[0:1, :], above)
    carry[0:1, :] = turned[TROWS - 1 : TROWS, :]
    shift[pl.ds(row_shift, TROWS), :] = jnp.where(lane < lane0, above, turned)
    step_out[...] = shift[0:TROWS, :].astype(BF16)
    shift[0:16, :] = shift[TROWS : TROWS + 16, :]


def run_adam(where, texts, dkv, conv, t_all, small, scal, first, second, kv_rows, rest_rows):
    gd = len(texts)
    length = first.shape[1]
    tiles = pl.cdiv(length + 17 * C, TROWS * C)
    last = kv_rows // TROWS - 1
    fixed = lambda shape: pl.BlockSpec(shape, lambda s, w: (0,) * len(shape))
    flat = pl.BlockSpec((1, TROWS * C), lambda s, w: (0, s))
    block = texts[0].shape[:2] + (C,)
    rest_pad = pl.cdiv(rest_rows, TROWS) * TROWS + TROWS
    return pl.pallas_call(
        functools.partial(adam_kernel, gd, length, kv_rows, rest_rows),
        out_shape=(
            jax.ShapeDtypeStruct(first.shape, F32),
            jax.ShapeDtypeStruct(first.shape, F32),
            jax.ShapeDtypeStruct((tiles * TROWS, C), BF16),
        ),
        grid_spec=pltpu.PrefetchScalarGridSpec(
            num_scalar_prefetch=1,
            grid=(tiles,),
            in_specs=[pl.BlockSpec(block, lambda s, w: (0, 0, jnp.minimum(w[4], last)))] * gd
            + [pl.BlockSpec(block, lambda s, w: (0, 0, jnp.minimum(w[4] + s + 1, last)))] * gd
            + [fixed(v.shape) for v in (dkv, conv, t_all, small, scal)]
            + [flat, flat],
            out_specs=[flat, flat, pl.BlockSpec((TROWS, C), lambda s, w: (s, 0))],
            scratch_shapes=[
                pltpu.VMEM((2 * TROWS + 8, C), F32),
                pltpu.VMEM((rest_pad, C), F32),
                pltpu.VMEM((TROWS + 16, C), F32),
                pltpu.VMEM((8, C), F32),
            ],
        ),
        compiler_params=pltpu.CompilerParams(vmem_limit_bytes=32 * 2**20),
        name="adam",
    )(where, *texts, *texts, dkv, conv, t_all, small, scal, first, second)


def final_kernel(bases, pad, weights, outer, pieces, new_weights, momentum):
    b = pl.program_id(0)
    total = pieces.shape[1]
    averaged = jnp.zeros((TROWS, C), F32)
    for p, base in enumerate(bases):
        at = jnp.clip(b * TROWS - base + pad, 0, total - TROWS)
        averaged = averaged + pieces[p, pl.ds(pl.multiple_of(at, 16), TROWS), :].astype(F32)
    w = weights[...]
    averaged = averaged + (INNER_RATE * DECAY_RATE) * w
    moved = OUTER_MOMENTUM * outer[...] + averaged
    momentum[...] = moved
    new_weights[...] = w - OUTER_RATE * (averaged + OUTER_MOMENTUM * moved)


def run_final(weights2, outer2, pieces, bases, pad):
    rows = weights2.shape[0]
    block = pl.BlockSpec((TROWS, C), lambda b: (b, 0))
    return pl.pallas_call(
        functools.partial(final_kernel, bases, pad),
        out_shape=(jax.ShapeDtypeStruct(weights2.shape, F32),) * 2,
        grid=(pl.cdiv(rows, TROWS),),
        in_specs=[block, block, pl.BlockSpec(pieces.shape, lambda b: (0, 0, 0))],
        out_specs=(block, block),
        compiler_params=pltpu.CompilerParams(vmem_limit_bytes=24 * 2**20),
        name="final",
    )(weights2, outer2, pieces)


def share_kernel(gd, rows, chunk, pad, l1, l2, u_ref, out_ref, recv_a, recv_b, part,
                 s_u, s_fo, s_fi, s_y, r_a, r_b, r_f, r_y):
    wide = lax.axis_index("wide")
    g = wide // gd
    spot = wide % gd
    chunks = rows // chunk
    is_outer = jnp.logical_or(g == 0, g == GROUPS - 1)
    is_inner = jnp.logical_not(is_outer)
    low = g < GROUPS // 2
    outer_id = jnp.where(low, g - 1, g + 1) * gd + spot
    mate_id = jnp.where(low, g + 1, g - 1) * gd + spot
    barrier = pltpu.get_barrier_semaphore()
    for k in range(1, gd):
        other = g * gd + lax.rem(spot + k, gd)
        pl.semaphore_signal(barrier, inc=1, device_id={"wide": other}, device_id_type=MESH)
    pl.semaphore_signal(barrier, inc=1, device_id={"wide": mate_id}, device_id_type=MESH)
    @pl.when(is_inner)
    def _():
        pl.semaphore_signal(barrier, inc=1, device_id={"wide": outer_id}, device_id_type=MESH)
        pl.semaphore_wait(barrier, gd + 1)
    @pl.when(is_outer)
    def _():
        pl.semaphore_wait(barrier, gd)

    def sl(c):
        return pl.ds(pl.multiple_of(c * chunk, chunk), chunk)
    def ol(c):
        return pl.ds(pl.multiple_of(pad + c * chunk, 16), chunk)
    def copy(src, dst, ss, rs, dev):
        return pltpu.make_async_remote_copy(src_ref=src, dst_ref=dst, send_sem=ss, recv_sem=rs,
                                            device_id={"wide": dev}, device_id_type=MESH)
    def send_a(c):
        return copy(u_ref.at[sl(c)], recv_a.at[sl(c)], s_u.at[c], r_a.at[c], mate_id)
    def send_b(c):
        return copy(part.at[sl(c)], recv_b.at[sl(c)], s_u.at[c], r_b.at[c], mate_id)
    def send_fo(c):
        return copy(out_ref.at[spot, ol(c)], out_ref.at[spot, ol(c)], s_fo.at[c], r_f.at[c], outer_id)
    def send_fi(c):
        return copy(out_ref.at[spot, ol(c)], out_ref.at[spot, ol(c)], s_fi.at[c], r_f.at[c], mate_id)
    def send_y(c, k):
        return copy(out_ref.at[spot, ol(c)], out_ref.at[spot, ol(c)], s_y.at[k - 1, c], r_y.at[k - 1, c],
                    g * gd + lax.rem(spot + k, gd))
    def wait_y(c, k):
        src = lax.rem(spot + gd - k, gd)
        copy(out_ref.at[src, ol(c)], out_ref.at[src, ol(c)], s_y.at[k - 1, c], r_y.at[k - 1, c], wide).wait_recv()
    def spread(c):
        for k in range(1, gd):
            send_y(c, k).start()
    def is_root(c):
        return lax.rem(c + g, 2) == 1

    @pl.when(is_outer)
    def _():
        @pl.loop(0, chunks)
        def _(c):
            send_a(c).start()
    for p in range(gd):
        out_ref[p, 0:pad] = jnp.zeros((pad, 128), jnp.bfloat16)
        out_ref[p, pad + rows : rows + 2 * pad] = jnp.zeros((pad, 128), jnp.bfloat16)

    @pl.when(is_outer)
    def _():
        @pl.loop(0, chunks)
        def _(c):
            send_fo(c).wait_recv()
            spread(c)
    @pl.when(is_inner)
    def _():
        @pl.loop(0, chunks + l2)
        def _(c):
            @pl.when(jnp.logical_and(c < chunks, jnp.logical_not(is_root(c))))
            def _():
                send_a(c).wait_recv()
                part[sl(c)] = (u_ref[sl(c)].astype(jnp.float32) + recv_a[sl(c)].astype(jnp.float32)).astype(jnp.bfloat16)
                send_b(c).start()
            d = c - l1
            @pl.when(jnp.logical_and(jnp.logical_and(d >= 0, d < chunks), is_root(d)))
            def _():
                send_a(d).wait_recv()
                send_b(d).wait_recv()
                out_ref[spot, ol(d)] = (u_ref[sl(d)].astype(jnp.float32) + recv_a[sl(d)].astype(jnp.float32) + recv_b[sl(d)].astype(jnp.float32)).astype(jnp.bfloat16)
                send_fo(d).start()
                send_fi(d).start()
                spread(d)
            e = c - l2
            @pl.when(jnp.logical_and(e >= 0, jnp.logical_not(is_root(e))))
            def _():
                send_fi(e).wait_recv()
                send_fo(e).start()
                spread(e)
    @pl.loop(0, chunks)
    def _(c):
        for k in range(1, gd):
            wait_y(c, k)
            send_y(c, k).wait_send()
        @pl.when(is_outer)
        def _():
            send_a(c).wait_send()
        @pl.when(is_inner)
        def _():
            send_fo(c).wait_send()
            @pl.when(is_root(c))
            def _():
                send_fi(c).wait_send()
            @pl.when(jnp.logical_not(is_root(c)))
            def _():
                send_b(c).wait_send()

def share(u, gd, rows, chunk, pad, l1, l2):
    n = rows // chunk
    D = pltpu.SemaphoreType.DMA
    return pl.pallas_call(
        functools.partial(share_kernel, gd, rows, chunk, pad, l1, l2),
        out_shape=jax.ShapeDtypeStruct((gd, rows + 2 * pad, 128), jnp.bfloat16),
        in_specs=[pl.BlockSpec(memory_space=pltpu.VMEM)],
        out_specs=pl.BlockSpec(memory_space=pltpu.VMEM),
        scratch_shapes=[pltpu.VMEM((rows, 128), jnp.bfloat16)] * 3 + [
            D((n,)), D((n,)), D((n,)), D((max(gd - 1, 1), n)), D((n,)), D((n,)), D((n,)), D((max(gd - 1, 1), n))],
        compiler_params=pltpu.CompilerParams(collective_id=9, has_side_effects=True, vmem_limit_bytes=24 * 2**20),
        name="share",
    )(u)


def ring_gather(value, axis, group):
    size = lax.axis_size(axis)
    found = [value]
    for k in range(1, group):
        pairs = [(s, s // group * group + (s % group + k) % group) for s in range(size)]
        found.append(lax.ppermute(value, axis, pairs))
    return found


def per_device(
    weights, first_moment, second_moment, outer_momentum, noisy_input, target,
    text_tokens, text_mask, noise_level, aug_level, crop_size,
):
    length = first_moment.shape[1]
    wide_count = lax.axis_size("wide")
    gd = wide_count // GROUPS
    wide_pos = lax.axis_index("wide")
    narrow_pos = lax.axis_index("narrow")
    spot = wide_pos % gd
    weights2 = weights.reshape(-1, C)
    outer2 = outer_momentum.reshape(-1, C)
    band = noisy_input.shape[1]

    noisy_ext, target_ext, text_all, rest_all, keyval, own_kv, small = run_front(
        noise_level, aug_level, weights2, noisy_input, target, text_tokens, text_mask
    )
    kv_rows = TEXT_D * keyval.shape[2] // C
    rest_rows = weights2.shape[0] - kv_rows
    texts = ring_gather(text_all, "wide", gd)
    kvs = ring_gather(own_kv, "wide", gd)
    info = jnp.stack(
        [narrow_pos * band, crop_size[0], narrow_pos, noise_level[0], aug_level[0]]
    ).astype(jnp.int32)
    blocks, conv, packet, right = run_main(
        info, noisy_ext, target_ext, small, rest_all, keyval, rest_rows
    )
    dkv, conv_all, t_all, small_all, scal = run_mid(
        gd, wide_count, blocks, conv, packet, right, kvs, texts
    )
    start = spot * length
    levels = small_all[:, 7, :2].astype(jnp.int32) + jnp.array([[0, NOISE_LEVELS]], jnp.int32)
    row0 = start // C
    where = jnp.concatenate(
        [
            jnp.stack([narrow_pos, start % C, row0 % TROWS, row0 % 16, row0 // TROWS]).astype(jnp.int32),
            levels.reshape(-1),
        ]
    )
    moment_one, moment_two, step = run_adam(
        where, texts, dkv, conv_all, t_all, small_all, scal, first_moment, second_moment, kv_rows, rest_rows
    )
    chunk = 320
    rows = pl.cdiv(length // C + 18, chunk) * chunk
    pieces = share(step, gd, rows, chunk, TROWS, 2, 4)
    bases = [p * length // C // 16 * 16 for p in range(gd)]
    new_weights, momentum_out = run_final(weights2, outer2, pieces, bases, TROWS)
    return (
        new_weights.reshape(-1), momentum_out.reshape(-1), moment_one, moment_two,
        scal[2, :1], scal[3, :1],
    )


def solution(mesh):
    placed = (
        P("narrow"),
        P("narrow", "wide"),
        P("narrow", "wide"),
        P("narrow"),
        P("wide", "narrow", None, None),
        P("wide", "narrow", None, None),
        P("wide", "narrow", None),
        P("wide", "narrow"),
        P("wide"),
        P("wide"),
        P("wide"),
    )
    return jax.shard_map(
        per_device,
        mesh=mesh,
        in_specs=placed,
        out_specs=(P("narrow"), P("narrow"), P("narrow", "wide"), P("narrow", "wide"), P(), P()),
        check_vma=False,
    )
```

time: 543 us -> 233 us (0.43); the launches traced: 536 us -> 232 us
  local copies, waits for them, and re-layouts: 143 us -> 28.4 us
  other arithmetic: 81.6 us -> 0.03 us
  waiting for transfers between devices: 64.7 us -> 0.01 us
  Pallas kernels: 138 us -> 199 us
  blocking collectives: 58.9 us -> 0 us
  between operations: 21 us -> 2.71 us
  starting transfers between devices: 17.9 us -> 2.04 us
  matrix products: 10.3 us -> 0 us
    concatenate x2 -> x1, local copies, waits for them, and re-layouts: 82.8 us -> 0.09 us  [per_device(): jnp.concatenate([jnp.stack([narrow_pos, start % C, row0 % TROWS, row0 % 1...]
    pallas_call x3 -> x6, Pallas kernels: 138 us -> 199 us  [the longest x1 69.7 us: share(): pl.pallas_call(functools.partial(share_kernel, gd, rows, chunk, pad, l1,...]
    psum x3 -> x0, blocking collectives: 33.2 us -> none  [the longest x1 21.1 us: per_device(): loss = lax.psum(jnp.sum(sums[4]), 'wide')]
    all_gather x1 -> x0, other arithmetic: 30.6 us -> none  [per_device(): lax.all_gather(weights[kv_len:].astype(BF16), 'narrow', axis=0, tiled=True)]
    psum x1 -> x0, waiting for transfers between devices: 28.4 us -> none  [per_device(): grad_conv = group_sum(lax.psum(dconv_w, 'narrow'))]
    reshape x1 -> x0, other arithmetic: 22.3 us -> none  [per_device(): momentum_out.reshape(-1)]
    unnamed x2 -> x0, blocking collectives: 19 us -> none
    ppermute x6 -> x2, waiting for transfers between devices: 13.1 us -> 0.01 us  [ring_gather(): found.append(lax.ppermute(value, axis, pairs))]
  transfers between devices with their start and end apart: 15 -> 2, of which waited for: 5 -> 0; matrix products, arithmetic and copies ran while one was open for 18% -> 0% of each run, Pallas kernels for 10% -> 24%
where the time goes in v2:
time: 233 us; the launch traced here: 232 us
  Pallas kernels  199 us (85%)
  local copies, waits for them, and re-layouts  28.4 us (12%)
  between operations  2.71 us (1%)
    pallas_call x1, Pallas kernels, share(): pl.pallas_call(functools.partial(share_kernel, gd, rows, chunk, pad, l1,...  69.7 us
    pallas_call x1, Pallas kernels, run_main(): pl.pallas_call(functools.partial(main_kernel, band, columns, H, HEADS, re...  55.5 us
    unnamed x46, local copies, waits for them, and re-layouts  27.6 us
    pallas_call x1, Pallas kernels, run_front(): pl.pallas_call(functools.partial(front_kernel, kv_rows, rest_rows), out_s...  21.7 us
    pallas_call x1, Pallas kernels, run_mid(): pl.pallas_call(functools.partial(mid_kernel, gd, H, W), out_shape=(jax.Sh...  20.8 us
    pallas_call x1, Pallas kernels, run_final(): pl.pallas_call(functools.partial(final_kernel, bases, pad), out_shape=(ja...  16.1 us
    pallas_call x1, Pallas kernels, run_adam(): pl.pallas_call(functools.partial(adam_kernel, gd, length, kv_rows, rest_r...  15.1 us
  transfers between devices with their start and end apart: 2, of which 0 were waited for; matrix products, arithmetic and copies ran while one was open for 0% of the time, Pallas kernels for 24%

profile of v2, /device:TPU:0, one launch (start us, length us, event | category | flops | bytes accessed | tf_op | source)
XLA Modules:
  0.0 232.1 jit_solution(12151728893770791046)
XLA Ops:
  1.9 3.6 %copy-done = f32[2265216]{0:T(1024)S(1)} copy-done((f32[2265216]{0:T(1024)S(1)}, f32[2265216]{0:T(1024)}, u32[]{:S(2)}) %copy-start) | copy-done | bytes 9060888
  5.5 1.2 copy-done.10
  6.7 1.2 copy-done.11
  8.0 0.9 copy-done.16
  9.6 21.7 %front.1 = (bf16[36,128,128]{2,1,0:T(8,128)(2,1)S(1)}, bf16[34,128,128]{2,1,0:T(8,128)(2,1)S(1)}, bf16[4,32,4096]{2,1,0:T(8,128)(2,1)S(1)}, bf16[4,1328,128]{2,1...) custom-call(s32[1]{0:T(128)S(6)} %copy.18.noise_level, ...), custom_call_target="tpu_custom_call" | custom-call | tf_op jit(solution)/shard_map/front/pallas_call | solution.py:588
  31.3 1.1 copy-done.4
  32.3 1.0 copy-done.6
  33.4 1.0 copy-done.8
  34.3 1.5 collective-permute-start.1
  37.2 1.3 copy-done.5
  38.6 1.3 copy-done.7
  39.8 1.2 copy-done.9
  41.1 55.5 %main.1 = (bf16[4,128,512]{2,1,0:T(8,128)(2,1)S(1)}, bf16[4,288,128]{2,1,0:T(8,128)(2,1)S(1)}, f32[8,128]{1,0:T(8,128)S(1)}, bf16[128,512]{1,0:T(8,128)(2,1)S(1)}) custom-call(s32[5]{0:T(128)S(1)} %stack.28.info, bf16[36,128,128]{2,1,0:T(8,128)(2,1)S(1)} %copy-done.7, bf16[34,128,128]{2,1,0:T(8,128)(2,1)S(1)} %copy-done.9, ...), custom_call_target="tpu_custom_call" | custom-call | tf_op jit(solution)/shard_map/main/pallas_call | solution.py:274
  97.3 0.9 copy-done.18
  98.2 20.8 %mid.1 = (bf16[256,512]{1,0:T(8,128)(2,1)S(1)}, bf16[4,288,128]{2,1,0:T(8,128)(2,1)S(1)}, bf16[4,128,512]{2,1,0:T(8,128)(2,1)S(1)}, f32[2,8,128]{2,1,0:T(8,128)S(1)}, f32[8,128]{1,0:T(8,128)S(1)}) custom-call(bf16[4,128,512]{2,1,0:T(8,128)(2,1)S(1)} %get-tuple-element.32.blocks, bf16[4,288,128]{2,1,0:T(8,128)(2,1)S(1)} %get-tuple-element.33.conv, ...), custom_call_target="tpu_custom_call" | custom-call | tf_op jit(solution)/shard_map/mid/pallas_call | solution.py:874
  119.0 0.7 copy-done.12
  121.2 2.3 copy-done.2
  123.4 2.3 copy-done.3
  125.7 1.0 copy-done.13
  126.7 0.9 copy-done.15
  127.6 15.1 %adam.1 = (f32[1,1132608]{1,0:T(1,128)}, f32[1,1132608]{1,0:T(1,128)}, bf16[9216,128]{1,0:T(8,128)(2,1)S(1)}) custom-call(s32[9]{0:T(128)S(1)} %concatenate.3.where, bf16[4,32,4096]{2,1,0:T(8,128)(2,1)S(1)} %get-tuple-element.37.refs_2_.refs_0_, bf16[4,32,4096]{2,1,0:T(8,128)(2,1)S(1)} %collective-permute-done.1.refs_3_.refs_1_, ...), custom_call_target="tpu_custom_call" | custom-call | tf_op jit(solution)/shard_map/adam/pallas_call | solution.py:1020
  142.8 69.7 %share.1.pieces = bf16[2,9984,128]{2,1,0:T(8,128)(2,1)S(1)} custom-call(bf16[9216,128]{1,0:T(8,128)(2,1)S(1)} %get-tuple-element.43.u_ref), custom_call_target="tpu_custom_call" | custom-call | tf_op jit(solution)/shard_map/share/pallas_call | solution.py:1186
  212.5 3.6 %copy-done.1 = f32[2265216]{0:T(1024)S(1)} copy-done((f32[2265216]{0:T(1024)S(1)}, f32[2265216]{0:T(1024)}, u32[]{:S(2)}) %copy-start.1) | copy-done | bytes 9060888
  216.0 16.1 %final.1 = (f32[17697,128]{1,0:T(8,128)}, f32[17697,128]{1,0:T(8,128)}) custom-call(f32[17697,128]{1,0:T(8,128)S(1)} %bitcast.15, f32[17697,128]{1,0:T(8,128)S(1)} %bitcast.16, bf16[2,9984,128]{2,1,0:T(8,128)(2,1)S(1)} %share.1.pieces), custom_call_target="tpu_custom_call" | custom-call | tf_op jit(solution)/shard_map/final/pallas_call | solution.py:1064
  (42 shorter events, 3.5 us)
Async XLA Ops:
  1.9 3.6 %copy-start = (f32[2265216]{0:T(1024)S(1)}, f32[2265216]{0:T(1024)}, u32[]{:S(2)}) copy-start(f32[2265216]{0:T(1024)} %param.12) | copy-start | bytes 27182596
  5.5 1.2 copy-start.10
  6.7 1.2 copy-start.11
  8.0 0.9 copy-start.16
  31.3 1.1 copy-start.4
  32.3 1.0 copy-start.6
  33.4 1.0 copy-start.8
  34.3 62.9 %collective-permute-start.1 = (bf16[4,32,4096]{2,1,0:T(8,128)(2,1)S(1)}, bf16[4,32,4096]{2,1,0:T(8,128)(2,1)S(1)}, u32[]{:S(2)}, u32[]{:S(2)}) collective-permute-start(bf16[4,32,4096]{2,1,0:T(8,128)(2,1)S(1)} %get-tuple-element.37.refs_2_.refs_0_), channel_id=1, source_target_pairs={{0,4},{4,0},{8,12},{12,8},{16,20},{20,16},{24,28},{28,24},{1,5},{5... | collective-permute-start | bytes 3145736 | tf_op jit(solution)/shard_map/ppermute | solution.py:1203
  35.9 60.7 %collective-permute-start = (bf16[128,512]{1,0:T(8,128)(2,1)S(1)}, bf16[128,512]{1,0:T(8,128)(2,1)S(1)}, u32[]{:S(2)}, u32[]{:S(2)}) collective-permute-start(bf16[128,512]{1,0:T(8,128)(2,1)S(1)} %get-tuple-element.36.refs_0_), channel_id=1, source_target_pairs={{0,4},{4,0},{8,12},{12,8},{16,20},{20,16},{24,28},{28,24},{1,5},{5... | collective-permute-start | bytes 393224 | tf_op jit(solution)/shard_map/ppermute | solution.py:1203
  37.2 1.3 copy-start.5
  38.6 1.3 copy-start.7
  39.8 1.2 copy-start.9
  96.6 0.7 copy-start.17
  97.3 0.9 copy-start.18
  98.2 114.2 %slice-start = ((s8[9064448]{0:T(1024)(128)(4,1)}), s8[675840]{0:T(1024)(128)(4,1)S(1)}, s32[]{:S(2)}) async-start(s8[9064448]{0:T(1024)(128)(4,1)} %bitcast.13), calls=%async_computation | async-start | bytes 1351680
  119.0 0.7 copy-start.12
  119.7 0.7 copy-start.14
  121.2 2.3 copy-start.2
  123.4 2.3 copy-start.3
  125.7 1.0 copy-start.13
  126.7 0.9 copy-start.15
  127.6 84.8 %slice-start.1 = ((s8[9064448]{0:T(1024)(128)(4,1)}), s8[4194304]{0:T(1024)(128)(4,1)S(1)}, s32[]{:S(2)}) async-start(s8[9064448]{0:T(1024)(128)(4,1)} %bitcast.13), calls=%async_computation.1 | async-start | bytes 8388608
  127.6 84.8 %slice-start.2 = ((s8[9064448]{0:T(1024)(128)(4,1)}), s8[4194304]{0:T(1024)(128)(4,1)S(1)}, s32[]{:S(2)}) async-start(s8[9064448]{0:T(1024)(128)(4,1)} %bitcast.13), calls=%async_computation.2 | async-start | bytes 8388608
  212.5 3.6 %copy-start.1 = (f32[2265216]{0:T(1024)S(1)}, f32[2265216]{0:T(1024)}, u32[]{:S(2)}) copy-start(f32[2265216]{0:T(1024)} %param.15) | copy-start | bytes 27182596
  (1 other events, 0.7 us)

commit v3 on v2

--- a/solution.py
+++ b/solution.py
@@ -39,7 +39,8 @@
 LOG2E = 1.4426950408889634
 LN2 = 0.6931471805599453
 NT = (((1,), (1,)), ((), ()))
-TILE = 2
+TILE = 7
+TILE3 = 8
 
 
 def dot(a, b, dims=(((1,), (0,)), ((), ()))):
@@ -55,9 +56,9 @@
     return jnp.where(keep, pltpu.roll(value, by, 0), 0.0)
 
 
-def main_kernel(
+def main_body(
     band, columns, height, heads,
-    rest_rows, info, noisy, target, small, rest, keyval,
+    rest_rows, crop_size, noise_level, aug_level, noisy, target, small, rest, keyval,
     blocks, dconv_w, packet, right,
     act3, diff3, m_cat, m_cat_t, n_cat, n_cat_t, conv_t, probs, dscore, wt3, y_t, z_t, sums,
     stage, query, out_w,
@@ -65,8 +66,9 @@
     tok, kv_block = keyval.shape[1:]
     width = heads * HEAD
     per_block = kv_block // HEAD
-    row0 = info[0]
-    crop = info[1]
+    narrow = lax.axis_index("narrow")
+    row0 = narrow * band
+    crop = crop_size[0]
     pix = TILE * columns
     first_gain, first_query = 9 * C + 2 * LEVELS, 9 * C + 2 * LEVELS + 4
     first_out = first_query + C * heads
@@ -119,11 +121,11 @@
         out_head = out_w[cols, :].astype(BF16)
         m_head = dot(query_head, keyval[block, :, at : at + HEAD], NT) * factor
 
-        @pl.when(info[2] == block)
+        @pl.when(narrow == block)
         def _():
             right[:, at : at + HEAD] = query_head
 
-        @pl.when(info[2] == block + heads // per_block)
+        @pl.when(narrow == block + heads // per_block)
         def _():
             right[:, at : at + HEAD] = out_w[cols, :].T.astype(BF16)
 
@@ -165,9 +167,9 @@
 
     pix_row = lax.broadcasted_iota(jnp.int32, (pix, C), 0) // columns
     pix_col = lax.broadcasted_iota(jnp.int32, (pix, C), 0) % columns
-    @pl.loop(0, (band + 2) // TILE)
+    @pl.loop(0, pl.cdiv(band + 2, TILE))
     def _(t):
-        q = t * TILE
+        q = jnp.minimum(t * TILE, band + 2 - TILE)
         conv = noisy[pl.ds(q + 1, TILE)].astype(F32).reshape(pix, C)
         for dy in range(3):
             window = act3[pl.ds(q + dy, TILE)].reshape(pix, 3 * C)
@@ -180,7 +182,9 @@
         low2 = jnp.concatenate([low, low], axis=1)
         for head in range(heads):
             tcols = slice(head * tok, (head + 1) * tok)
-            score = dot(low2, m_cat[:, tcols])
+            if head % 2 == 0:
+                scores = dot(low2, m_cat[:, head * tok : (head + 2) * tok])
+            score = scores[:, head % 2 * tok : (head % 2 + 1) * tok]
             score = jnp.where(ok, score, -1e30)
             e = jnp.exp2(score - jnp.max(score, axis=1, keepdims=True))
             p = e * (1.0 / jnp.sum(e, axis=1, keepdims=True))
@@ -191,7 +195,7 @@
         valid = (row >= 0) & (row < crop) & (pix_col < crop)
         err = jnp.where(valid, output - target[pl.ds(q, TILE)].astype(F32).reshape(pix, C), 0.0)
         own_row = q + pix_row
-        own = (own_row >= 1) & (own_row <= band)
+        own = (own_row >= jnp.maximum(t * TILE, 1)) & (own_row <= band)
         err_own = jnp.where(own, err, 0.0)
         sums[4:5, :] += jnp.sum(err_own * err_own, axis=0, keepdims=True)
         dout = 2.0 * err
@@ -199,7 +203,9 @@
         dout2 = jnp.concatenate([dout_low, dout_low], axis=1)
         for head in range(heads):
             tcols = slice(head * tok, (head + 1) * tok)
-            dprob = dot(dout2, n_cat_t[:, tcols])
+            if head % 2 == 0:
+                dprobs = dot(dout2, n_cat_t[:, head * tok : (head + 2) * tok])
+            dprob = dprobs[:, head % 2 * tok : (head % 2 + 1) * tok]
             p = probs[:, tcols].astype(F32)
             pd = p * dprob
             ds = pd - p * jnp.sum(pd, axis=1, keepdims=True)
@@ -229,14 +235,14 @@
             diff3[q + k, :, C : 2 * C] = one.astype(BF16)
             diff3[q + k, :, 2 * C : 3 * C] = shifted(one, 1, not_first).astype(BF16)
 
-    @pl.loop(0, band // TILE)
+    @pl.loop(0, band // TILE3)
     def _(t):
-        r = t * TILE
-        grad = jnp.zeros((pix, C), F32)
+        r = t * TILE3
+        grad = jnp.zeros((TILE3 * columns, C), F32)
         for dy in range(3):
-            window = diff3[pl.ds(r + 2 - dy, TILE)].reshape(pix, 3 * C)
+            window = diff3[pl.ds(r + 2 - dy, TILE3)].reshape(TILE3 * columns, 3 * C)
             grad = grad + dot(window, wt3[dy * 3 * C : (dy + 1) * 3 * C, :])
-        x = noisy[pl.ds(r + 2, TILE)].astype(F32).reshape(pix, C)
+        x = noisy[pl.ds(r + 2, TILE3)].astype(F32).reshape(TILE3 * columns, C)
         scaled = x * slope + base
         sig = jax.nn.sigmoid(scaled)
         ds = grad * (sig * (1.0 + scaled * (1.0 - sig)))
@@ -259,49 +265,9 @@
     packet[6:7] = sums[4:5]
     lane = lax.broadcasted_iota(jnp.int32, (1, C), 1)
     facts = jnp.zeros((1, C), F32)
-    for k, fact in enumerate((info[3], info[4], crop)):
+    for k, fact in enumerate((noise_level[0], aug_level[0], crop)):
         facts = jnp.where(lane == k, fact.astype(F32), facts)
     packet[7:8] = jnp.where(row0 == 0, facts, 0.0)
-
-
-def run_main(info, noisy_ext, target_ext, small, rest, keyval, rest_rows):
-    band = target_ext.shape[0] - 2
-    columns = target_ext.shape[1]
-    tok, kv_block = keyval.shape[1:]
-    vmem = pl.BlockSpec(memory_space=pltpu.VMEM)
-    pix = TILE * columns
-    assert 9 * C <= rest_rows and kv_block % HEAD == 0 and HEAD == C
-    return pl.pallas_call(
-        functools.partial(main_kernel, band, columns, H, HEADS, rest_rows),
-        out_shape=(
-            jax.ShapeDtypeStruct((4, C, kv_block // HEAD * tok), BF16),
-            jax.ShapeDtypeStruct((4, 9 * C // 4, C), BF16),
-            jax.ShapeDtypeStruct((8, C), F32),
-            jax.ShapeDtypeStruct((C, kv_block), BF16),
-        ),
-        in_specs=[pl.BlockSpec(memory_space=pltpu.SMEM)] + [vmem] * 5,
-        out_specs=(vmem,) * 4,
-        scratch_shapes=[
-            pltpu.VMEM((band + 4, columns, 3 * C), BF16),
-            pltpu.VMEM((band + 2, columns, 3 * C), BF16),
-            pltpu.VMEM((2 * C, HEADS * tok), BF16),
-            pltpu.VMEM((HEADS * tok, 2 * C), BF16),
-            pltpu.VMEM((HEADS * tok, 2 * C), BF16),
-            pltpu.VMEM((2 * C, HEADS * tok), BF16),
-            pltpu.VMEM((C, 9 * C), F32),
-            pltpu.VMEM((pix, HEADS * tok), BF16),
-            pltpu.VMEM((pix, HEADS * tok), BF16),
-            pltpu.VMEM((9 * C, C), BF16),
-            pltpu.VMEM((C, HEADS * tok), F32),
-            pltpu.VMEM((C, HEADS * tok), F32),
-            pltpu.VMEM((8, C), F32),
-            pltpu.VMEM((rest.shape[1], C), F32),
-            pltpu.VMEM((C * HEADS, C), F32),
-            pltpu.VMEM((HEADS * HEAD, C), F32),
-        ],
-        compiler_params=pltpu.CompilerParams(vmem_limit_bytes=40 * 2**20),
-        name="main",
-    )(info, noisy_ext, target_ext, small, rest, keyval)
 
 
 def cross_ids():
@@ -365,17 +331,14 @@
 WPARTS = 8
 
 
-def front_kernel(
-    kv_rows, rest_rows, noise_level, aug_level, weights, noisy, target, text, mask,
+def front_body(
+    kv_rows, rest_rows, greet, to_group, noise_level, aug_level, weights, noisy, target, text, mask,
     noisy_ext, target_ext, text_all, rest_all, keyval, own_kv, small,
     wide_f32, wide_bf, rest_f32, acc,
     w_sem, in_sem, text_sem, rest_sem, kv_sem, small_sem, halo_sem,
 ):
     ids = cross_ids()
     n, mate, across, corner = ids
-    barrier = pltpu.get_barrier_semaphore()
-    for other in (mate, across, corner):
-        pl.semaphore_signal(barrier, inc=1, device_id={"narrow": other}, device_id_type=MESH)
     band = noisy.shape[1]
     tokens, depth = text.shape[1:]
     in_text = pltpu.make_async_copy(text.at[0], text_all.at[n], in_sem.at[0])
@@ -397,7 +360,7 @@
         copy.start()
     in_target = pltpu.make_async_copy(target.at[0], target_ext.at[pl.ds(1, band)], in_sem.at[3])
     in_target.start()
-    pl.semaphore_wait(barrier, 3)
+    greet()
 
     k_step = depth // KPARTS
     texts = [
@@ -411,6 +374,7 @@
         part.start()
 
     in_rest.wait()
+    rest_f32[rest_rows:] = jnp.zeros((rest_f32.shape[0] - rest_rows, C), F32)
     for k in range(2):
         row_sum = jnp.zeros((1, C), F32)
         for level in (noise_level[0], NOISE_LEVELS + aug_level[0]):
@@ -522,6 +486,7 @@
     own_kv[...] = acc[...].astype(BF16)
     keys = Gather(lambda b: keyval.at[b], kv_sem, ids)
     keys.start()
+    to_group()
 
     for owner in range(4):
         if needs[owner] is not None:
@@ -574,48 +539,9 @@
         part.drain()
 
 
-def run_front(noise_level, aug_level, weights2, noisy, target, text, mask):
-    _, band, columns, _ = noisy.shape
-    _, tokens, depth = text.shape
-    kv_block = 2 * HEADS * HEAD // 4
-    kv_rows = depth * kv_block // C
-    rest_rows = weights2.shape[0] - kv_rows
-    rest_pad = (rest_rows + 15) // 16 * 16
-    vmem = pl.BlockSpec(memory_space=pltpu.VMEM)
-    smem = pl.BlockSpec(memory_space=pltpu.SMEM)
-    hbm = pl.BlockSpec(memory_space=pl.ANY)
-    D = pltpu.SemaphoreType.DMA
-    return pl.pallas_call(
-        functools.partial(front_kernel, kv_rows, rest_rows),
-        out_shape=(
-            jax.ShapeDtypeStruct((band + 4, columns, C), BF16),
-            jax.ShapeDtypeStruct((band + 2, columns, C), BF16),
-            jax.ShapeDtypeStruct((4, tokens, depth), BF16),
-            jax.ShapeDtypeStruct((4, rest_pad, C), BF16),
-            jax.ShapeDtypeStruct((4, 4 * tokens, kv_block), BF16),
-            jax.ShapeDtypeStruct((4 * tokens, kv_block), BF16),
-            jax.ShapeDtypeStruct((4, 8, C), F32),
-        ),
-        in_specs=[smem, smem, hbm, hbm, hbm, hbm, vmem],
-        out_specs=(vmem,) * 7,
-        scratch_shapes=[
-            pltpu.VMEM((kv_rows, C), F32),
-            pltpu.VMEM((depth, kv_block), BF16),
-            pltpu.VMEM((rest_pad, C), F32),
-            pltpu.VMEM((4 * tokens, kv_block), F32),
-            D((WPARTS,)), D((4,)), D((KPARTS, 2, 3)), D((2, 3, 4)), D((2, 3)), D((2, 3)), D((2, 4)),
-        ],
-        compiler_params=pltpu.CompilerParams(
-            collective_id=1, has_side_effects=True, vmem_limit_bytes=36 * 2**20
-        ),
-        name="front",
-    )(noise_level, aug_level, weights2, noisy, target, text, mask)
-
-
-def mid_kernel(
-    gd, height, columns, blocks, conv, packet, right, *refs,
+def mid_body(
+    gd, height, columns, from_group, blocks, conv, packet, right, kvs, texts, *refs,
 ):
-    kvs, texts, refs = refs[:gd], refs[gd : 2 * gd], refs[2 * gd :]
     (
         dkv_all, conv_all, t_all, small_all, scal,
         near_b, near_c, sum_b, sum_c, far_b, far_c, own_b, own_c, group_b, group_c,
@@ -629,20 +555,9 @@
     wide = lax.axis_index("wide")
     group = wide // gd
     spot = lax.rem(wide, gd)
-    tok, kv_block = kvs[0].shape
+    tok, kv_block = kvs.shape[1:]
     heads = kv_block // HEAD
-    barrier = pltpu.get_barrier_semaphore()
-    for other in others:
-        pl.semaphore_signal(barrier, inc=1, device_id={"narrow": other}, device_id_type=MESH)
-
-    @pl.loop(1, wide_count)
-    def _(k):
-        pl.semaphore_signal(
-            barrier, inc=1, device_id={"wide": lax.rem(wide + k, wide_count)}, device_id_type=MESH
-        )
-
     packets[n] = packet[...]
-    pl.semaphore_wait(barrier, 3 + wide_count - 1)
 
     def near(slot, which):
         owner = corner if slot == 0 else mate
@@ -691,16 +606,17 @@
     def _(k):
         wide_copy(k, wide).start()
 
-    depth = texts[0].shape[-1]
+    depth = texts.shape[-1]
+    from_group()
     gram[...] = jnp.zeros_like(gram)
 
     @pl.loop(0, depth // 1024)
     def _(i):
         at = pl.ds(pl.multiple_of(i * 1024, 1024), 1024)
         for a in range(gd):
-            left = texts[a][:, :, at].reshape(tok, 1024)
+            left = texts[a, :, :, at].reshape(tok, 1024)
             for b in range(a, gd):
-                part = dot(left, texts[b][:, :, at].reshape(tok, 1024), NT)
+                part = dot(left, texts[b, :, :, at].reshape(tok, 1024), NT)
                 gram[a * tok : (a + 1) * tok, b * tok : (b + 1) * tok] += part
 
     near(1, 0).wait_recv()
@@ -733,7 +649,7 @@
             cols = slice(h * HEAD, (h + 1) * HEAD)
             part = value[:, h * tok : (h + 1) * tok]
             dkv_all[k * tok : (k + 1) * tok, cols] = (dot(part, right[:, cols], TN) * scale).astype(BF16)
-            term = dot(part, kvs[k][:, cols]) * scale
+            term = dot(part, kvs[k, :, cols]) * scale
             t_own[:, cols] = term if k == 0 else t_own[:, cols] + term
 
     project(0, own_b[...])
@@ -864,76 +780,253 @@
         wide_copy(k, wide).wait_send()
 
 
-def run_mid(gd, wide_count, blocks, conv, packet, right, kvs, texts):
-    tok, kv_block = kvs[0].shape
+def step_kernel(gd, wide_count, kv_rows, rest_rows, band, columns, counts, *refs):
+    refs = list(refs)
+    noise_level, aug_level, crop_size, weights, noisy, target, text, first, second, mask = refs[:10]
+    texts, dkv_all, conv_all, t_all, small_all, scal, first_near, second_near = refs[10:18]
+    n_front, n_main, n_mid = counts
+    at = 18
+    (noisy_ext, target_ext, rest_all, keyval, kvs, small) = refs[at : at + 6]
+    at += 6
+    front_sems = refs[at : at + n_front]
+    at += n_front
+    (blocks, conv, packet, right) = refs[at : at + 4]
+    at += 4
+    mid_refs = refs[at : at + n_mid]
+    at += n_mid
+    group_text_sem, ahead_sem = refs[at], refs[at + 1]
+    ahead = [
+        pltpu.make_async_copy(far, near, ahead_sem.at[k])
+        for k, (far, near) in enumerate(((first, first_near), (second, second_near)))
+    ]
+    n, mate, across, corner = cross_ids()
+    wide = lax.axis_index("wide")
+    group, spot = wide // gd, lax.rem(wide, gd)
+    tok, kv_block = kvs.shape[1:]
+    depth = text.shape[2]
+    barrier = pltpu.get_barrier_semaphore()
+    for other in (mate, across, corner):
+        pl.semaphore_signal(barrier, inc=1, device_id={"narrow": other}, device_id_type=MESH)
+
+    @pl.loop(1, wide_count)
+    def _(k):
+        pl.semaphore_signal(
+            barrier, inc=1, device_id={"wide": lax.rem(wide + k, wide_count)}, device_id_type=MESH
+        )
+
+    def greet():
+        pl.semaphore_wait(barrier, 3 + wide_count - 1)
+
+    def group_send(k, which):
+        buf = (texts, kvs)[which]
+        return pltpu.make_async_remote_copy(
+            src_ref=buf.at[0], dst_ref=buf.at[k],
+            send_sem=group_text_sem.at[0, which, k - 1], recv_sem=group_text_sem.at[1, which, k - 1],
+            device_id={"wide": group * gd + lax.rem(spot + k, gd)}, device_id_type=MESH,
+        )
+
+    def to_group():
+        for which in (1, 0):
+            for k in range(1, gd):
+                group_send(k, which).start()
+
+    def from_group():
+        for which in (1, 0):
+            for k in range(1, gd):
+                group_send(k, which).wait_recv()
+                group_send(k, which).wait_send()
+
+    def front(wide_f32, wide_bf, rest_f32, acc):
+        front_body(
+            kv_rows, rest_rows, greet, to_group, noise_level, aug_level, weights, noisy, target, text, mask,
+            noisy_ext, target_ext, texts.at[0], rest_all, keyval, kvs.at[0], small,
+            wide_f32, wide_bf, rest_f32, acc, *front_sems,
+        )
+
+    V = pltpu.VMEM
+    pl.run_scoped(
+        front, V((kv_rows, C), F32), V((depth, kv_block), BF16), V((rest_all.shape[1], C), F32),
+        V((tok, kv_block), F32),
+    )
+    for copy in ahead:
+        copy.start()
+    pix = TILE * columns
+
+    def main(*scratch):
+        main_body(
+            band, columns, H, HEADS, rest_rows, crop_size, noise_level, aug_level,
+            noisy_ext, target_ext, small, rest_all, keyval, blocks, conv, packet, right, *scratch,
+        )
+
+    pl.run_scoped(
+        main,
+        V((band + 4, columns, 3 * C), BF16),
+        V((band + 2, columns, 3 * C), BF16),
+        V((2 * C, HEADS * tok), BF16),
+        V((HEADS * tok, 2 * C), BF16),
+        V((HEADS * tok, 2 * C), BF16),
+        V((2 * C, HEADS * tok), BF16),
+        V((C, 9 * C), F32),
+        V((pix, HEADS * tok), BF16),
+        V((pix, HEADS * tok), BF16),
+        V((9 * C, C), BF16),
+        V((C, HEADS * tok), F32),
+        V((C, HEADS * tok), F32),
+        V((8, C), F32),
+        V((rest_all.shape[1], C), F32),
+        V((C * HEADS, C), F32),
+        V((HEADS * HEAD, C), F32),
+    )
+
+    def middle(gram):
+        mid_body(
+            gd, H, W, from_group, blocks, conv, packet, right, kvs, texts,
+            dkv_all, conv_all, t_all, small_all, scal, *mid_refs[:15], gram, *mid_refs[15:],
+        )
+
+    pl.run_scoped(middle, V((gd * tok, gd * tok), F32))
+    for copy in ahead:
+        copy.wait()
+
+
+def near(gd):
+    return pltpu.VMEM if gd <= 4 else jax.ShapeDtypeStruct
+
+
+def hold(value, gd):
+    return pltpu.with_memory_space_constraint(value, pltpu.VMEM) if gd <= 4 else value
+
+
+def far(value):
+    return pltpu.with_memory_space_constraint(value, pltpu.HBM)
+
+
+def run_step(
+    gd, wide_count, noise_level, aug_level, crop_size, weights2, noisy, target, text, first, second, mask
+):
+    _, band, columns, _ = noisy.shape
+    _, tokens, depth = text.shape
+    tok = 4 * tokens
+    kv_block = 2 * HEADS * HEAD // 4
+    kv_rows = depth * kv_block // C
+    rest_rows = weights2.shape[0] - kv_rows
+    rest_pad = (rest_rows + 15) // 16 * 16
+    assert 9 * C <= rest_rows and kv_block % HEAD == 0 and HEAD == C
     vmem = pl.BlockSpec(memory_space=pltpu.VMEM)
-    D = pltpu.SemaphoreType.DMA
-    bshape, cshape = blocks.shape[1:], conv.shape[1:]
-    V = pltpu.VMEM
+    smem = pl.BlockSpec(memory_space=pltpu.SMEM)
+    hbm = pl.BlockSpec(memory_space=pltpu.HBM)
+    D, V = pltpu.SemaphoreType.DMA, pltpu.VMEM
     few = max(gd - 1, 1)
+    bshape, cshape = (C, kv_block // HEAD * tok), (9 * C // 4, C)
+    front_sems = [D((WPARTS,)), D((4,)), D((KPARTS, 2, 3)), D((2, 3, 4)), D((2, 3)), D((2, 3)), D((2, 4))]
+    mid_refs = [
+        V((2,) + bshape, BF16), V((2,) + cshape, BF16), V(bshape, BF16), V(cshape, BF16),
+        V(bshape, BF16), V(cshape, BF16), V(bshape, BF16), V(cshape, BF16),
+        V((few,) + bshape, BF16), V((few,) + cshape, BF16),
+        V((4, 8, C), F32), V((wide_count, 8, C), F32),
+        V((C, kv_block), F32), V((C, kv_block), BF16), V(cshape, BF16),
+        V((4, 8, C), F32), V(cshape, F32),
+        D((2, 2, 2)), D((2, 2)), D((2, 2, few)), D((2, 3)), D((2, wide_count)), D((2, 3)), D((2, 4)),
+    ]
     return pl.pallas_call(
-        functools.partial(mid_kernel, gd, H, W),
-        out_shape=(
-            jax.ShapeDtypeStruct((gd * tok, kv_block), BF16),
-            jax.ShapeDtypeStruct((4,) + cshape, BF16),
-            jax.ShapeDtypeStruct((4, C, kv_block), BF16),
-            jax.ShapeDtypeStruct((gd, 8, C), F32),
-            jax.ShapeDtypeStruct((8, C), F32),
+        functools.partial(
+            step_kernel, gd, wide_count, kv_rows, rest_rows, band, columns,
+            (len(front_sems), 0, len(mid_refs)),
         ),
-        in_specs=[vmem] * (4 + 2 * gd),
-        out_specs=(vmem,) * 5,
+        out_shape=tuple(
+            near(gd)(shape, kind)
+            for shape, kind in (
+                ((gd, 4, tokens, depth), BF16),
+                ((gd * tok, kv_block), BF16),
+                ((4,) + cshape, BF16),
+                ((4, C, kv_block), BF16),
+                ((gd, 8, C), F32),
+                ((8, C), F32),
+                (first.shape, F32),
+                (first.shape, F32),
+            )
+        ),
+        in_specs=[smem] * 3 + [hbm] * 6 + [vmem],
+        out_specs=(vmem,) * 8,
         scratch_shapes=[
-            V((2,) + bshape, BF16), V((2,) + cshape, BF16), V(bshape, BF16), V(cshape, BF16),
-            V(bshape, BF16), V(cshape, BF16), V(bshape, BF16), V(cshape, BF16),
-            V((few,) + bshape, BF16), V((few,) + cshape, BF16),
-            V((4, 8, C), F32), V((wide_count, 8, C), F32),
-            V((C, kv_block), F32), V((C, kv_block), BF16), V(cshape, BF16),
-            V((gd * tok, gd * tok), F32), V((4, 8, C), F32), V(cshape, F32),
-            D((2, 2, 2)), D((2, 2)), D((2, 2, few)), D((2, 3)), D((2, wide_count)), D((2, 3)), D((2, 4)),
+            V((band + 4, columns, C), BF16), V((band + 2, columns, C), BF16), V((4, rest_pad, C), BF16),
+            V((4, tok, kv_block), BF16), V((gd, tok, kv_block), BF16), V((4, 8, C), F32),
+            *front_sems,
+            V((4,) + bshape, BF16), V((4,) + cshape, BF16), V((8, C), F32), V((C, kv_block), BF16),
+            *mid_refs,
+            D((2, 2, few)),
+            D((2,)),
         ],
         compiler_params=pltpu.CompilerParams(
-            collective_id=2, has_side_effects=True, vmem_limit_bytes=48 * 2**20
+            collective_id=1, has_side_effects=True, vmem_limit_bytes=(STEP_VMEM if gd <= 4 else 58) * 2**20
         ),
-        name="mid",
-    )(blocks, conv, packet, right, *kvs, *texts)
-
-
-TROWS = 512
+        name="step",
+    )(noise_level, aug_level, crop_size, *map(far, (weights2, noisy, target, text, first, second)), mask)
+
+
+STEP_VMEM = 48
+
+
+AROWS = 1024
+
+
+def adam_tiles(length):
+    return pl.cdiv(length + 17 * C, AROWS * C)
 
 
 def adam_kernel(
-    gd, length, kv_rows, rest_rows, where, *refs,
+    gd, length, kv_rows, rest_rows, *refs,
 ):
-    firsts, texts, refs = refs[:gd], refs[gd : 2 * gd], refs[2 * gd :]
     (
-        dkv, conv, t_all, small, scal, first, second, first_out, second_out, step_out,
-        nat, rest, shift, carry,
+        texts, dkv, conv, t_all, small, scal, first, second, first_out, second_out, step_out,
+        nat, rest, turned_dkv, edge, shift, carry,
     ) = refs
     s = pl.program_id(0)
-    tiles = pl.num_programs(0) - 1
     tok = dkv.shape[0] // gd
-    n, lane0, row_off, row_shift, block0 = (where[k] for k in range(5))
-    kv_blocks = kv_rows // TROWS
-    parts = TROWS // C
-
-    def natural(text_refs, block):
+    n = lax.axis_index("narrow")
+    start = lax.rem(lax.axis_index("wide"), gd) * length
+    row0 = start // C
+    lane0, row_off, row_shift, block0 = lax.rem(start, C), lax.rem(row0, AROWS), lax.rem(row0, 16), row0 // AROWS
+    wrap = C - lane0
+    kv_blocks = kv_rows // AROWS
+    parts = dkv.shape[1] // C
+    cols_tile = AROWS // parts
+
+    def iotas(rows):
+        shape = (rows, C)
+        return lax.broadcasted_iota(jnp.int32, shape, 0), lax.broadcasted_iota(jnp.int32, shape, 1)
+
+    def natural(tile):
+        block = block0 + tile
+        here = pl.multiple_of(tile * AROWS + 8, 8)
+
         @pl.when(block < kv_blocks)
         def _():
-            text = jnp.concatenate([ref[...].reshape(tok, C) for ref in text_refs], axis=0)
-            grad = dot(text, dkv[...], TN)
-            for j in range(parts):
-                nat[pl.ds(TROWS + j, C, stride=parts), :] = grad[:, j * C : (j + 1) * C]
+            at = pl.ds(pl.multiple_of(block * cols_tile, cols_tile), cols_tile)
+            text = jnp.concatenate([texts[k, :, :, at].reshape(tok, cols_tile) for k in range(gd)], axis=0)
+            grad = dot(text, turned_dkv[...], TN)
+            for j in range(parts - 1):
+                nat[pl.ds(here + j, cols_tile, stride=parts), :] = grad[:, j * C : (j + 1) * C]
+            part = grad[:, (parts - 1) * C :]
+            row, lane = iotas(cols_tile)
+            before = jnp.where(row == 0, edge[0:1, :], pltpu.roll(part, 1, 0))
+            nat[pl.ds(here - 1, cols_tile, stride=parts), :] = jnp.where(lane < wrap, before, part)
+            edge[0:1, :] = part[cols_tile - 1 : cols_tile, :]
 
         @pl.when(block >= kv_blocks)
         def _():
-            at = jnp.minimum(block - kv_blocks, rest.shape[0] // TROWS - 1) * TROWS
-            nat[TROWS : 2 * TROWS, :] = rest[pl.ds(pl.multiple_of(at, TROWS), TROWS), :]
-
-    @pl.when(s == 0)
-    def _():
-        rest[...] = jnp.zeros_like(rest)
-        carry[...] = jnp.zeros_like(carry)
-        shift[...] = jnp.zeros_like(shift)
+            at = pl.multiple_of(jnp.minimum((block - kv_blocks) * AROWS, rest.shape[0] - 16 - AROWS), 8)
+            row, lane = iotas(AROWS)
+            both = jnp.where(lane >= lane0, rest[pl.ds(at + 8, AROWS), :], rest[pl.ds(at + 9, AROWS), :])
+            nat[pl.ds(here, AROWS), :] = pltpu.roll(both, wrap, 1)
+
+            @pl.when(block == kv_blocks)
+            def _():
+                row, lane = iotas(8)
+                ahead = pltpu.roll(rest[8:16, :], wrap, 1)
+                nat[pl.ds(here - 1, 1), :] = jnp.where(lane < wrap, edge[...], ahead)[0:1, :]
+
+    def assemble():
         first_table, first_gain = 9 * C, 9 * C + 2 * LEVELS
         first_query = first_gain + 4
         first_out = first_query + C * HEADS
@@ -949,7 +1042,7 @@
                     a, b = max(lo, k * quarter), min(hi, (k + 1) * quarter)
                     if a < b:
                         assert (a, b) == (k * quarter, (k + 1) * quarter)
-                        rest[a - lo : b - lo, :] = conv[k].astype(F32)
+                        rest[8 + a - lo : 8 + b - lo, :] = conv[k].astype(F32)
                 a, b = max(lo, first_query), min(hi, first_out)
                 if a < b:
                     for h in range(HEADS):
@@ -959,121 +1052,112 @@
                         c_lo, c_hi = c0 // 16 * 16, (c1 + 15) // 16 * 16
                         value = t_all[h // heads, c_lo:c_hi, cols].astype(F32)
                         start = first_query + c0 * HEADS + h - lo
-                        rest[pl.ds(start, c1 - c0, stride=HEADS), :] = value[c0 - c_lo : c1 - c_lo]
+                        rest[pl.ds(8 + start, c1 - c0, stride=HEADS), :] = value[c0 - c_lo : c1 - c_lo]
                 for h in range(HEADS):
                     a, b = first_out + h * HEAD, first_out + (h + 1) * HEAD
                     if lo <= a and b <= hi:
                         cols = slice(h % heads * HEAD, h % heads * HEAD + HEAD)
-                        rest[a - lo : b - lo, :] = t_all[2 + h // heads, :, cols].astype(F32).T
+                        rest[8 + a - lo : 8 + b - lo, :] = t_all[2 + h // heads, :, cols].astype(F32).T
                     else:
                         assert b <= lo or hi <= a
                 if lo <= first_gain and first_gain + 4 <= hi:
                     total = small[0, 0:4]
                     for k in range(1, gd):
                         total = total + small[k, 0:4]
-                    rest[first_gain - lo : first_gain + 4 - lo, :] = total
-
-        for k in range(2 * gd):
-            for half in range(2):
-                row = first_table + 2 * where[5 + k] + half - n * rest_rows
-
-                @pl.when((row >= 0) & (row < rest_rows))
-                def _():
-                    rest[pl.ds(row, 1), :] += small[k // 2, 4 + half : 5 + half]
-
-        natural(firsts, block0)
-
-    nat[0:TROWS, :] = nat[TROWS : 2 * TROWS, :]
-    natural(texts, block0 + s + 1)
-
-    lane = lax.broadcasted_iota(jnp.int32, (TROWS, C), 1)
-    row = lax.broadcasted_iota(jnp.int32, (TROWS, C), 0)
-    same_row = nat[pl.ds(row_off, TROWS), :]
-    next_row = nat[pl.ds(row_off + 1, TROWS), :]
-    g = pltpu.roll(jnp.where(lane >= lane0, same_row, next_row), C - lane0, 1) * scal[0:1]
-    one = BETA_ONE * first.reshape(TROWS, C)[...] + (1.0 - BETA_ONE) * g
-    two = BETA_TWO * second.reshape(TROWS, C)[...] + (1.0 - BETA_TWO) * g * g
-    first_out.reshape(TROWS, C)[...] = one
-    second_out.reshape(TROWS, C)[...] = two
+                    rest[8 + first_gain - lo : 8 + first_gain + 4 - lo, :] = total
+
+
+        for k in range(gd):
+            for level, shift_by in ((0, 0), (1, NOISE_LEVELS)):
+                found = jnp.max(small[k, 7:8, level : level + 1]).astype(jnp.int32) + shift_by
+                for half in range(2):
+                    at_row = first_table + 2 * found + half - n * rest_rows
+
+                    @pl.when((at_row >= 0) & (at_row < rest_rows))
+                    def _():
+                        rest[pl.ds(at_row + 8, 1), :] += small[k, 4 + half : 5 + half]
+
+    @pl.when(s == 0)
+    def _():
+        edge[...] = jnp.zeros_like(edge)
+        rest[...] = jnp.zeros_like(rest)
+        carry[...] = jnp.zeros_like(carry)
+        shift[...] = jnp.zeros_like(shift)
+        row, lane = iotas(dkv.shape[0])
+        moved = [
+            pltpu.roll(dkv[:, j * C : (j + 1) * C].astype(F32), wrap, 1) for j in range(parts)
+        ]
+        for j in range(parts):
+            turned_dkv[:, j * C : (j + 1) * C] = jnp.where(
+                lane < wrap, moved[j], moved[(j + 1) % parts]
+            ).astype(BF16)
+
+        @pl.when(start + length > kv_rows * C)
+        def _():
+            assemble()
+
+        natural(0)
+
+    natural(s + 1)
+    row, lane = iotas(AROWS)
+    g = nat[pl.ds(s * AROWS + row_off + 8, AROWS), :] * scal[0:1]
+    one = BETA_ONE * first.reshape(AROWS, C)[...] + (1.0 - BETA_ONE) * g
+    two = BETA_TWO * second.reshape(AROWS, C)[...] + (1.0 - BETA_TWO) * g * g
+    first_out.reshape(AROWS, C)[...] = one
+    second_out.reshape(AROWS, C)[...] = two
     fixed_one = one * (scal[1:2] * (1.0 / (1.0 - BETA_ONE**STEP)))
     fixed_two = two * (1.0 / (1.0 - BETA_TWO**STEP))
-    step = fixed_one / (jnp.sqrt(fixed_two) + ADAM_EPS)
-    step = jnp.where((s * TROWS + row) * C + lane < length, step, 0.0)
+    root = fixed_two * lax.rsqrt(fixed_two)
+    step = fixed_one * pl.reciprocal(root + ADAM_EPS, approx=True)
+    step = jnp.where((s * AROWS + row) * C + lane < length, step, 0.0)
     turned = pltpu.roll(step, lane0, 1)
     above = pltpu.roll(turned, 1, 0)
     above = jnp.where(row == 0, carry[0:1, :], above)
-    carry[0:1, :] = turned[TROWS - 1 : TROWS, :]
-    shift[pl.ds(row_shift, TROWS), :] = jnp.where(lane < lane0, above, turned)
-    step_out[...] = shift[0:TROWS, :].astype(BF16)
-    shift[0:16, :] = shift[TROWS : TROWS + 16, :]
-
-
-def run_adam(where, texts, dkv, conv, t_all, small, scal, first, second, kv_rows, rest_rows):
-    gd = len(texts)
-    length = first.shape[1]
-    tiles = pl.cdiv(length + 17 * C, TROWS * C)
-    last = kv_rows // TROWS - 1
-    fixed = lambda shape: pl.BlockSpec(shape, lambda s, w: (0,) * len(shape))
-    flat = pl.BlockSpec((1, TROWS * C), lambda s, w: (0, s))
-    block = texts[0].shape[:2] + (C,)
-    rest_pad = pl.cdiv(rest_rows, TROWS) * TROWS + TROWS
+    carry[0:1, :] = turned[AROWS - 1 : AROWS, :]
+    shift[pl.ds(row_shift, AROWS), :] = jnp.where(lane < lane0, above, turned)
+    step_out[...] = shift[0:AROWS, :].astype(BF16)
+    shift[0:16, :] = shift[AROWS : AROWS + 16, :]
+
+
+def run_adam(texts, dkv, conv, t_all, small, scal, first, second, length, kv_rows, rest_rows):
+    gd = texts.shape[0]
+    tiles = adam_tiles(length)
+    flat = pl.BlockSpec((1, AROWS * C), lambda s: (0, s))
+    rest_pad = (pl.cdiv(rest_rows, AROWS) + 1) * AROWS + 16
     return pl.pallas_call(
         functools.partial(adam_kernel, gd, length, kv_rows, rest_rows),
         out_shape=(
-            jax.ShapeDtypeStruct(first.shape, F32),
-            jax.ShapeDtypeStruct(first.shape, F32),
-            jax.ShapeDtypeStruct((tiles * TROWS, C), BF16),
+            jax.ShapeDtypeStruct((1, length), F32),
+            jax.ShapeDtypeStruct((1, length), F32),
+            near(gd)((tiles * AROWS, C), BF16),
         ),
-        grid_spec=pltpu.PrefetchScalarGridSpec(
-            num_scalar_prefetch=1,
-            grid=(tiles,),
-            in_specs=[pl.BlockSpec(block, lambda s, w: (0, 0, jnp.minimum(w[4], last)))] * gd
-            + [pl.BlockSpec(block, lambda s, w: (0, 0, jnp.minimum(w[4] + s + 1, last)))] * gd
-            + [fixed(v.shape) for v in (dkv, conv, t_all, small, scal)]
-            + [flat, flat],
-            out_specs=[flat, flat, pl.BlockSpec((TROWS, C), lambda s, w: (s, 0))],
-            scratch_shapes=[
-                pltpu.VMEM((2 * TROWS + 8, C), F32),
-                pltpu.VMEM((rest_pad, C), F32),
-                pltpu.VMEM((TROWS + 16, C), F32),
-                pltpu.VMEM((8, C), F32),
-            ],
-        ),
-        compiler_params=pltpu.CompilerParams(vmem_limit_bytes=32 * 2**20),
+        grid=(tiles,),
+        in_specs=[pl.BlockSpec(memory_space=pltpu.VMEM)] * 6 + [flat, flat],
+        out_specs=[flat, flat, pl.BlockSpec((AROWS, C), lambda s: (s, 0))],
+        scratch_shapes=[
+            pltpu.VMEM(((tiles + 1) * AROWS + 16, C), F32),
+            pltpu.VMEM((rest_pad, C), F32),
+            pltpu.VMEM(dkv.shape, BF16),
+            pltpu.VMEM((8, C), F32),
+            pltpu.VMEM((AROWS + 16, C), F32),
+            pltpu.VMEM((8, C), F32),
+        ],
+        compiler_params=pltpu.CompilerParams(vmem_limit_bytes=ADAM_VMEM),
         name="adam",
-    )(where, *texts, *texts, dkv, conv, t_all, small, scal, first, second)
-
-
-def final_kernel(bases, pad, weights, outer, pieces, new_weights, momentum):
-    b = pl.program_id(0)
-    total = pieces.shape[1]
-    averaged = jnp.zeros((TROWS, C), F32)
-    for p, base in enumerate(bases):
-        at = jnp.clip(b * TROWS - base + pad, 0, total - TROWS)
-        averaged = averaged + pieces[p, pl.ds(pl.multiple_of(at, 16), TROWS), :].astype(F32)
-    w = weights[...]
-    averaged = averaged + (INNER_RATE * DECAY_RATE) * w
-    moved = OUTER_MOMENTUM * outer[...] + averaged
-    momentum[...] = moved
-    new_weights[...] = w - OUTER_RATE * (averaged + OUTER_MOMENTUM * moved)
-
-
-def run_final(weights2, outer2, pieces, bases, pad):
-    rows = weights2.shape[0]
-    block = pl.BlockSpec((TROWS, C), lambda b: (b, 0))
-    return pl.pallas_call(
-        functools.partial(final_kernel, bases, pad),
-        out_shape=(jax.ShapeDtypeStruct(weights2.shape, F32),) * 2,
-        grid=(pl.cdiv(rows, TROWS),),
-        in_specs=[block, block, pl.BlockSpec(pieces.shape, lambda b: (0, 0, 0))],
-        out_specs=(block, block),
-        compiler_params=pltpu.CompilerParams(vmem_limit_bytes=24 * 2**20),
-        name="final",
-    )(weights2, outer2, pieces)
-
-
-def share_kernel(gd, rows, chunk, pad, l1, l2, u_ref, out_ref, recv_a, recv_b, part,
-                 s_u, s_fo, s_fi, s_y, r_a, r_b, r_f, r_y):
+    )(*(hold(v, gd) for v in (texts, dkv, conv, t_all, small, scal, first, second)))
+
+
+ADAM_VMEM = 24 * 2**20
+
+
+def share_kernel(
+    gd, rows, chunk, pad, l1, l2, u_ref, w_far, o_far, out_ref, w_near, o_near,
+    recv_a, recv_b, part, in_sem, s_u, s_fo, s_fi, s_y, r_a, r_b, r_f, r_y,
+):
+    loads = [
+        pltpu.make_async_copy(w_far, w_near.at[pl.ds(0, w_far.shape[0])], in_sem.at[1]),
+        pltpu.make_async_copy(o_far, o_near.at[pl.ds(0, o_far.shape[0])], in_sem.at[2]),
+    ]
     wide = lax.axis_index("wide")
     g = wide // gd
     spot = wide % gd
@@ -1128,6 +1212,8 @@
         @pl.loop(0, chunks)
         def _(c):
             send_a(c).start()
+    for load in loads:
+        load.start()
     for p in range(gd):
         out_ref[p, 0:pad] = jnp.zeros((pad, 128), jnp.bfloat16)
         out_ref[p, pad + rows : rows + 2 * pad] = jnp.zeros((pad, 128), jnp.bfloat16)
@@ -1179,29 +1265,85 @@
             @pl.when(jnp.logical_not(is_root(c)))
             def _():
                 send_b(c).wait_send()
-
-def share(u, gd, rows, chunk, pad, l1, l2):
+    for load in loads:
+        load.wait()
+
+
+def share(u, weights2, outer2, gd, rows, chunk, pad, l1, l2):
     n = rows // chunk
     D = pltpu.SemaphoreType.DMA
+    few = max(gd - 1, 1)
+    held = pl.cdiv(weights2.shape[0], 256) * 256
+    vmem, hbm = pl.BlockSpec(memory_space=pltpu.VMEM), pl.BlockSpec(memory_space=pltpu.HBM)
     return pl.pallas_call(
         functools.partial(share_kernel, gd, rows, chunk, pad, l1, l2),
-        out_shape=jax.ShapeDtypeStruct((gd, rows + 2 * pad, 128), jnp.bfloat16),
-        in_specs=[pl.BlockSpec(memory_space=pltpu.VMEM)],
-        out_specs=pl.BlockSpec(memory_space=pltpu.VMEM),
-        scratch_shapes=[pltpu.VMEM((rows, 128), jnp.bfloat16)] * 3 + [
-            D((n,)), D((n,)), D((n,)), D((max(gd - 1, 1), n)), D((n,)), D((n,)), D((n,)), D((max(gd - 1, 1), n))],
-        compiler_params=pltpu.CompilerParams(collective_id=9, has_side_effects=True, vmem_limit_bytes=24 * 2**20),
+        out_shape=(near(gd)((gd, rows + 2 * pad, C), BF16),) + (near(gd)((held, C), F32),) * 2,
+        in_specs=[vmem, hbm, hbm],
+        out_specs=(vmem,) * 3,
+        scratch_shapes=[pltpu.VMEM((rows, C), BF16)] * 3
+        + [
+            D((3,)), D((n,)), D((n,)), D((n,)), D((few, n)),
+            D((n,)), D((n,)), D((n,)), D((few, n)),
+        ],
+        compiler_params=pltpu.CompilerParams(
+            collective_id=9, has_side_effects=True, vmem_limit_bytes=SHARE_VMEM
+        ),
         name="share",
-    )(u)
-
-
-def ring_gather(value, axis, group):
-    size = lax.axis_size(axis)
-    found = [value]
-    for k in range(1, group):
-        pairs = [(s, s // group * group + (s % group + k) % group) for s in range(size)]
-        found.append(lax.ppermute(value, axis, pairs))
-    return found
+    )(hold(u, gd), far(weights2), far(outer2))
+
+
+SHARE_VMEM = 32 * 2**20
+
+
+def final_kernel(bases, pad, block, weights, outer, pieces, scal, new_weights, momentum, loss, count, held, sem):
+    rows = new_weights.shape[0]
+    total = pieces.shape[1]
+    steps = pl.cdiv(rows, block)
+
+    def writes(b, slot, size):
+        here = pl.ds(b * block, size)
+        return [
+            pltpu.make_async_copy(held.at[slot, k, pl.ds(0, size)], out.at[here], sem.at[slot, k])
+            for k, out in enumerate((new_weights, momentum))
+        ]
+
+    for b in range(steps):
+        slot = b % 3
+        size = min(block, rows - b * block)
+        if b >= 3:
+            for copy in writes(b - 3, slot, block):
+                copy.wait()
+        averaged = jnp.zeros((block, C), F32)
+        for p, base in enumerate(bases):
+            at = min(max(b * block - base + pad, 0), total - block)
+            averaged = averaged + pieces[p, at : at + block, :].astype(F32)
+        w = weights[b * block : (b + 1) * block, :]
+        averaged = averaged + (INNER_RATE * DECAY_RATE) * w
+        moved = OUTER_MOMENTUM * outer[b * block : (b + 1) * block, :] + averaged
+        held[slot, 1] = moved
+        held[slot, 0] = w - OUTER_RATE * (averaged + OUTER_MOMENTUM * moved)
+        for copy in writes(b, slot, size):
+            copy.start()
+    loss[0] = jnp.max(scal[2:3])
+    count[0] = jnp.max(scal[3:4])
+    for b in range(max(steps - 3, 0), steps):
+        for copy in writes(b, b % 3, min(block, rows - b * block)):
+            copy.wait()
+
+
+def run_final(rows, weights2, outer2, pieces, scal, bases, pad):
+    hbm, smem = pl.BlockSpec(memory_space=pltpu.HBM), pl.BlockSpec(memory_space=pltpu.SMEM)
+    block = weights2.shape[0] // 16
+    assert block % 16 == 0 and block <= pad
+    return pl.pallas_call(
+        functools.partial(final_kernel, bases, pad, block),
+        out_shape=(jax.ShapeDtypeStruct((rows, C), F32),) * 2 + (jax.ShapeDtypeStruct((1,), F32),) * 2,
+        in_specs=[pl.BlockSpec(memory_space=pltpu.VMEM)] * 4,
+        out_specs=(hbm, hbm, smem, smem),
+        scratch_shapes=[pltpu.VMEM((3, 2, block, C), F32), pltpu.SemaphoreType.DMA((3, 2))],
+        compiler_params=pltpu.CompilerParams(vmem_limit_bytes=12 * 2**20),
+        name="final",
+    )(*(hold(v, len(bases)) for v in (weights2, outer2, pieces, scal)))
 
 
 def per_device(
@@ -1211,49 +1353,29 @@
     length = first_moment.shape[1]
     wide_count = lax.axis_size("wide")
     gd = wide_count // GROUPS
-    wide_pos = lax.axis_index("wide")
-    narrow_pos = lax.axis_index("narrow")
-    spot = wide_pos % gd
     weights2 = weights.reshape(-1, C)
     outer2 = outer_momentum.reshape(-1, C)
-    band = noisy_input.shape[1]
-
-    noisy_ext, target_ext, text_all, rest_all, keyval, own_kv, small = run_front(
-        noise_level, aug_level, weights2, noisy_input, target, text_tokens, text_mask
+
+    texts, dkv, conv_all, t_all, small_all, scal, first, second = run_step(
+        gd, wide_count, noise_level, aug_level, crop_size, weights2, noisy_input, target, text_tokens,
+        first_moment, second_moment, text_mask,
     )
-    kv_rows = TEXT_D * keyval.shape[2] // C
+    kv_rows = TEXT_D * dkv.shape[1] // C
     rest_rows = weights2.shape[0] - kv_rows
-    texts = ring_gather(text_all, "wide", gd)
-    kvs = ring_gather(own_kv, "wide", gd)
-    info = jnp.stack(
-        [narrow_pos * band, crop_size[0], narrow_pos, noise_level[0], aug_level[0]]
-    ).astype(jnp.int32)
-    blocks, conv, packet, right = run_main(
-        info, noisy_ext, target_ext, small, rest_all, keyval, rest_rows
-    )
-    dkv, conv_all, t_all, small_all, scal = run_mid(
-        gd, wide_count, blocks, conv, packet, right, kvs, texts
-    )
-    start = spot * length
-    levels = small_all[:, 7, :2].astype(jnp.int32) + jnp.array([[0, NOISE_LEVELS]], jnp.int32)
-    row0 = start // C
-    where = jnp.concatenate(
-        [
-            jnp.stack([narrow_pos, start % C, row0 % TROWS, row0 % 16, row0 // TROWS]).astype(jnp.int32),
-            levels.reshape(-1),
-        ]
-    )
     moment_one, moment_two, step = run_adam(
-        where, texts, dkv, conv_all, t_all, small_all, scal, first_moment, second_moment, kv_rows, rest_rows
+        texts, dkv, conv_all, t_all, small_all, scal, first, second, length, kv_rows, rest_rows
     )
     chunk = 320
     rows = pl.cdiv(length // C + 18, chunk) * chunk
-    pieces = share(step, gd, rows, chunk, TROWS, 2, 4)
+    pad = 1120
+    pieces, w_near, o_near = share(step, weights2, outer2, gd, rows, chunk, pad, 2, 4)
     bases = [p * length // C // 16 * 16 for p in range(gd)]
-    new_weights, momentum_out = run_final(weights2, outer2, pieces, bases, TROWS)
+    new_weights, momentum_out, loss, count = run_final(
+        weights2.shape[0], w_near, o_near, pieces, scal, bases, pad
+    )
     return (
         new_weights.reshape(-1), momentum_out.reshape(-1), moment_one, moment_two,
-        scal[2, :1], scal[3, :1],
+        loss, count,
     )
 
 

time: 233 us -> 166 us (0.71)
  Pallas kernels: 199 us -> 163 us
  local copies, waits for them, and re-layouts: 28.4 us -> 0 us
    pallas_call x4 -> x2, Pallas kernels: 114 us -> 83.8 us  [the longest x1 75.8 us: run_step(): pl.pallas_call(functools.partial(step_kernel, gd, wide_count, kv_rows, re...]
    unnamed x46 -> x0, local copies, waits for them, and re-layouts: 27.6 us -> none
    pallas_call x1, Pallas kernels: 15.1 us -> 9.07 us  [run_adam(): pl.pallas_call(functools.partial(adam_kernel, gd, length, kv_rows, rest_r...]
  transfers between devices with their start and end apart: 2 -> 0, of which waited for: 0 -> 0; matrix products, arithmetic and copies ran while one was open for 0% -> 0% of each run, Pallas kernels for 24% -> 0%
where the time goes in v3:
time: 166 us
  Pallas kernels  163 us (98%)
  between operations  2.75 us (2%)
    pallas_call x1, Pallas kernels, run_step(): pl.pallas_call(functools.partial(step_kernel, gd, wide_count, kv_rows, re...  75.8 us
    pallas_call x1, Pallas kernels, share(): pl.pallas_call(functools.partial(share_kernel, gd, rows, chunk, pad, l1,...  70.6 us
    pallas_call x1, Pallas kernels, run_adam(): pl.pallas_call(functools.partial(adam_kernel, gd, length, kv_rows, rest_r...  9.07 us
    pallas_call x1, Pallas kernels, run_final(): pl.pallas_call(functools.partial(final_kernel, bases, pad, block), out_sh...  8.02 us

profile of v3, /device:TPU:0, one launch (start us, length us, event | category | flops | bytes accessed | tf_op | source)
XLA Modules:
  0.0 166.2 jit_solution(14437788836579656400)
XLA Ops:
  2.6 75.8 %step.1 = (bf16[2,4,32,4096]{3,2,1,0:T(8,128)(2,1)S(1)}, bf16[256,512]{1,0:T(8,128)(2,1)S(1)}, bf16[4,288,128]{2,1,0:T(8,128)(2,1)S(1)}, bf16[4,128,512]{2,1,0:T...) custom-call(s32[1]{0:T(128)S(6)} %copy.17.refs_0_, ...), custom_call_target="tpu_custom_call" | custom-call | tf_op jit(solution)/shard_map/step/pallas_call | solution.py:931
  78.4 9.1 %adam.1 = (f32[1,1132608]{1,0:T(1,128)}, f32[1,1132608]{1,0:T(1,128)}, bf16[9216,128]{1,0:T(8,128)(2,1)S(1)}) custom-call(bf16[2,4,32,4096]{3,2,1,0:T(8,128)(2,1)S(1)} %get-tuple-element.24.refs_0_, bf16[256,512]{1,0:T(8,128)(2,1)S(1)} %get-tuple-element.25.refs_1_, bf16[4,288,128]{2,1,0:T(8,128)(2,1)S(1)} %get-tuple-element.26.refs_2_, ...), custom_call_target="tpu_custom_call" | custom-call | tf_op jit(solution)/shard_map/adam/pallas_call | solution.py:1127
  87.4 70.6 %share.1 = (bf16[2,11200,128]{2,1,0:T(8,128)(2,1)S(1)}, f32[17920,128]{1,0:T(8,128)S(1)}, f32[17920,128]{1,0:T(8,128)S(1)}) custom-call(bf16[9216,128]{1,0:T(8,128)(2,1)S(1)} %get-tuple-element.32.u_ref, f32[17697,128]{1,0:T(8,128)} %bitcast.5, f32[17697,128]{1,0:T(8,128)} %bitcast.6), custom_call_target="tpu_custom_call" | custom-call | tf_op jit(solution)/shard_map/share/pallas_call | solution.py:1278
  158.1 8.0 %final.1 = (f32[17697,128]{1,0:T(8,128)}, f32[17697,128]{1,0:T(8,128)}, f32[1]{0:T(128)}, f32[1]{0:T(128)}) custom-call(f32[17920,128]{1,0:T(8,128)S(1)} %get-tuple-element.33.weights, f32[17920,128]{1,0:T(8,128)S(1)} %get-tuple-element.34.outer, bf16[2,11200,128]{2,1,0:T(8,128)(2,1)S(1)} %get-tuple-element.35.pieces, ...), custom_call_target="tpu_custom_call" | custom-call | tf_op jit(solution)/shard_map/final/pallas_call | solution.py:1338

commit v4 on v3

--- a/solution.py
+++ b/solution.py
@@ -56,11 +56,78 @@
     return jnp.where(keep, pltpu.roll(value, by, 0), 0.0)
 
 
+CTILE = 7
+
+
+def vectors(small, height, columns):
+    total = small[0] + small[1] + small[2] + small[3]
+    lane_group = lax.broadcasted_iota(jnp.int32, (C, C), 0) // (C // NORM_GROUPS)
+    same = (lane_group == lax.broadcasted_iota(jnp.int32, (C, C), 1) // (C // NORM_GROUPS)).astype(F32)
+    stats = jnp.dot(total[0:8], same, precision=lax.Precision.HIGHEST, preferred_element_type=F32)
+    count = height * columns * C // NORM_GROUPS
+    mean = stats[0:1] * (1.0 / count)
+    spread = lax.rsqrt(stats[1:2] * (1.0 / count) - mean * mean + EPS_NORM)
+    film_scale, film_shift = 1.0 + total[2:3], total[3:4]
+    gains = total[8:12]
+    gain = gains[0:1] * film_scale
+    offset = gains[1:2] * film_scale + film_shift
+    slope = spread * gain
+    return mean, spread, slope, offset - mean * slope, film_scale, gains
+
+
+def edges(columns):
+    place = lax.broadcasted_iota(jnp.int32, (columns, C), 0)
+    return place > 0, place < columns - 1
+
+
+def activate(band, columns, height, noisy, small, conv_w, act3, wt3):
+    row0 = lax.axis_index("narrow") * band
+    mean, spread, slope, base, film_scale, gains = vectors(small, height, columns)
+    not_first, not_last = edges(columns)
+
+    @pl.loop(0, band + 4)
+    def _(r):
+        scaled = noisy[r].astype(F32) * slope + base
+        value = scaled * jax.nn.sigmoid(scaled)
+        row = row0 + r - 2
+        value = jnp.where(jnp.logical_and(row >= 0, row < height), value, 0.0)
+        value = value.astype(BF16).astype(F32)
+        act3[r, :, 0:C] = shifted(value, 1, not_first).astype(BF16)
+        act3[r, :, C : 2 * C] = value.astype(BF16)
+        act3[r, :, 2 * C : 3 * C] = shifted(value, columns - 1, not_last).astype(BF16)
+
+    for tap in range(9):
+        rows = slice(tap * C, (tap + 1) * C)
+        wt3[rows, :] = conv_w[rows, :].astype(F32).T.astype(BF16)
+
+
+def convolve_tiles(first, last, band, columns, height, noisy, small, conv_w, act3, conv_s, xhat_s, rs_s, low_s):
+    gains = vectors(small, height, columns)[5]
+    pix = CTILE * columns
+
+    @pl.loop(first, last)
+    def _(t):
+        q = jnp.minimum(t * CTILE, band + 2 - CTILE)
+        conv = noisy[pl.ds(q + 1, CTILE)].astype(F32).reshape(pix, C)
+        for dy in range(3):
+            window = act3[pl.ds(q + dy, CTILE)].reshape(pix, 3 * C)
+            conv = conv + dot(window, conv_w[dy * 3 * C : (dy + 1) * 3 * C, :])
+        centered = conv - jnp.mean(conv, axis=1, keepdims=True)
+        rs = lax.rsqrt(jnp.mean(centered * centered, axis=1, keepdims=True) + EPS_NORM)
+        xhat = centered * rs
+        here = pl.ds(q, CTILE)
+        conv_s[here] = conv.reshape(CTILE, columns, C)
+        xhat_s[here] = xhat.reshape(CTILE, columns, C)
+        rs_s[here] = jnp.broadcast_to(rs, (pix, C)).reshape(CTILE, columns, C)
+        low_s[here] = (xhat * gains[2:3] + gains[3:4]).astype(BF16).reshape(CTILE, columns, C)
+
+
 def main_body(
-    band, columns, height, heads,
+    start_near, start_far, band, columns, height, heads,
     rest_rows, crop_size, noise_level, aug_level, noisy, target, small, rest, keyval,
     blocks, dconv_w, packet, right,
-    act3, diff3, m_cat, m_cat_t, n_cat, n_cat_t, conv_t, probs, dscore, wt3, y_t, z_t, sums,
+    act3, wt3, conv_s, xhat_s, rs_s, low_s,
+    diff3, m_cat, m_cat_t, n_cat, n_cat_t, conv_t, probs, dscore, y_t, z_t, sums,
     stage, query, out_w,
 ):
     tok, kv_block = keyval.shape[1:]
@@ -70,7 +137,7 @@
     row0 = narrow * band
     crop = crop_size[0]
     pix = TILE * columns
-    first_gain, first_query = 9 * C + 2 * LEVELS, 9 * C + 2 * LEVELS + 4
+    first_query = 9 * C + 2 * LEVELS + 4
     first_out = first_query + C * heads
 
     def take(first, count, place):
@@ -92,23 +159,10 @@
 
         return place
 
-    gains = []
-    take(first_gain, 4, lambda value, use: gains.append(value))
-    gains = gains[0] if len(gains) == 1 else jnp.concatenate(gains, axis=0)
     take(first_query, C * heads, filler(query))
     take(first_out, width, filler(out_w))
-    conv_w = rest.at[0]
-    total = small[0] + small[1] + small[2] + small[3]
-    lane_group = lax.broadcasted_iota(jnp.int32, (C, C), 0) // (C // NORM_GROUPS)
-    same = (lane_group == lax.broadcasted_iota(jnp.int32, (C, C), 1) // (C // NORM_GROUPS)).astype(F32)
-    stats = jnp.dot(total, same, precision=lax.Precision.HIGHEST, preferred_element_type=F32)
-    count = height * columns * C // NORM_GROUPS
-    mean = stats[0:1] * (1.0 / count)
-    spread = lax.rsqrt(stats[1:2] * (1.0 / count) - mean * mean + EPS_NORM)
-    film_scale, film_shift = 1.0 + total[2:3], total[3:4]
-    gain = gains[0:1] * film_scale
-    offset = gains[1:2] * film_scale + film_shift
-    ln_gain, ln_offset = gains[2:3], gains[3:4]
+    mean, spread, slope, base, film_scale, gains = vectors(small, height, columns)
+    ln_gain = gains[2:3]
     quarter = tok // 4
     masks = [small[owner, 4:5, 0:quarter] for owner in range(4)]
     ok = (jnp.concatenate(masks, axis=1) > 0.0) | (lax.broadcasted_iota(jnp.int32, (1, tok), 1) == 0)
@@ -142,43 +196,19 @@
         top, rest = two_parts(n_head.T)
         n_cat_t[:C, tcols] = top
         n_cat_t[C:, tcols] = rest
-    for tap in range(9):
-        rows = slice(tap * C, (tap + 1) * C)
-        wt3[rows, :] = conv_w[rows, :].astype(F32).T.astype(BF16)
     y_t[...] = jnp.zeros_like(y_t)
     z_t[...] = jnp.zeros_like(z_t)
     conv_t[...] = jnp.zeros_like(conv_t)
     sums[...] = jnp.zeros_like(sums)
-    place = lax.broadcasted_iota(jnp.int32, (columns, C), 0)
-    not_first, not_last = place > 0, place < columns - 1
-    slope = spread * gain
-    base = offset - mean * slope
-
-    @pl.loop(0, band + 4)
-    def _(r):
-        scaled = noisy[r].astype(F32) * slope + base
-        value = scaled * jax.nn.sigmoid(scaled)
-        row = row0 + r - 2
-        value = jnp.where(jnp.logical_and(row >= 0, row < height), value, 0.0)
-        value = value.astype(BF16).astype(F32)
-        act3[r, :, 0:C] = shifted(value, 1, not_first).astype(BF16)
-        act3[r, :, C : 2 * C] = value.astype(BF16)
-        act3[r, :, 2 * C : 3 * C] = shifted(value, columns - 1, not_last).astype(BF16)
-
+    not_first, not_last = edges(columns)
     pix_row = lax.broadcasted_iota(jnp.int32, (pix, C), 0) // columns
     pix_col = lax.broadcasted_iota(jnp.int32, (pix, C), 0) % columns
     @pl.loop(0, pl.cdiv(band + 2, TILE))
     def _(t):
         q = jnp.minimum(t * TILE, band + 2 - TILE)
-        conv = noisy[pl.ds(q + 1, TILE)].astype(F32).reshape(pix, C)
-        for dy in range(3):
-            window = act3[pl.ds(q + dy, TILE)].reshape(pix, 3 * C)
-            conv = conv + dot(window, conv_w[dy * 3 * C : (dy + 1) * 3 * C, :])
-        centered = conv - jnp.mean(conv, axis=1, keepdims=True)
-        rs = lax.rsqrt(jnp.mean(centered * centered, axis=1, keepdims=True) + EPS_NORM)
-        xhat = centered * rs
-        layered = xhat * ln_gain + ln_offset
-        low = layered.astype(BF16)
+        here = pl.ds(q, TILE)
+        conv = conv_s[here].reshape(pix, C)
+        low = low_s[here].reshape(pix, C)
         low2 = jnp.concatenate([low, low], axis=1)
         for head in range(heads):
             tcols = slice(head * tok, (head + 1) * tok)
@@ -213,6 +243,8 @@
         dlay2 = dot(dscore[...], m_cat_t[...])
         dlay = (dlay2[:, :C] + dlay2[:, C:]) * LN2
         dlay_own = jnp.where(own, dlay, 0.0)
+        xhat = xhat_s[here].reshape(pix, C)
+        rs = rs_s[here].reshape(pix, C)
         sums[2:3, :] += jnp.sum(dlay_own * xhat, axis=0, keepdims=True)
         sums[3:4, :] += jnp.sum(dlay_own, axis=0, keepdims=True)
         dxh = dlay * ln_gain
@@ -222,7 +254,7 @@
             - xhat * jnp.mean(dxh * xhat, axis=1, keepdims=True)
         )
         dout_t = (2.0 * err_own).T.astype(BF16)
-        lay_t = jnp.where(own, layered, 0.0).T.astype(BF16)
+        lay_t = jnp.where(own, low.astype(F32), 0.0).T.astype(BF16)
         y_t[...] += dot(dout_t, probs[...])
         z_t[...] += dot(lay_t, dscore[...])
         dconv_t = jnp.where(own, dconv, 0.0).T.astype(BF16)
@@ -235,8 +267,7 @@
             diff3[q + k, :, C : 2 * C] = one.astype(BF16)
             diff3[q + k, :, 2 * C : 3 * C] = shifted(one, 1, not_first).astype(BF16)
 
-    @pl.loop(0, band // TILE3)
-    def _(t):
+    def back(t):
         r = t * TILE3
         grad = jnp.zeros((TILE3 * columns, C), F32)
         for dy in range(3):
@@ -256,6 +287,11 @@
         part = z_t if owner < 2 else y_t
         at = owner % 2 * per_block * tok
         blocks[owner] = part[:, at : at + per_block * tok].astype(BF16)
+    start_near()
+    halves = band // TILE3 // 2
+    pl.loop(0, halves)(back)
+    start_far()
+    pl.loop(halves, band // TILE3)(back)
     a, b = sums[0:1], sums[1:2]
     packet[0:1] = film_scale * b
     packet[1:2] = film_scale * a
@@ -332,7 +368,7 @@
 
 
 def front_body(
-    kv_rows, rest_rows, greet, to_group, noise_level, aug_level, weights, noisy, target, text, mask,
+    kv_rows, rest_rows, greet, to_group, early, noise_level, aug_level, weights, noisy, target, text, mask,
     noisy_ext, target_ext, text_all, rest_all, keyval, own_kv, small,
     wide_f32, wide_bf, rest_f32, acc,
     w_sem, in_sem, text_sem, rest_sem, kv_sem, small_sem, halo_sem,
@@ -383,7 +419,14 @@
             found = found.astype(BF16).astype(F32)
             row_sum = row_sum + jnp.where((row >= 0) & (row < rest_rows), found, 0.0)
         small[n, 2 + k : 3 + k, :] = row_sum
-    small[n, 4:8, :] = jnp.zeros((4, C), F32)
+    small[n, 4:16, :] = jnp.zeros((12, C), F32)
+    for owner in range(4):
+        for k in range(4):
+            row = 9 * C + 2 * LEVELS + k - owner * rest_rows
+            if 0 <= row < rest_rows:
+                @pl.when(n == owner)
+                def _():
+                    small[n, 8 + k : 9 + k, :] = rest_f32[row : row + 1, :].astype(BF16).astype(F32)
     small[n, 4:5, 0:tokens] = mask[...].astype(F32)
     in_noisy.wait()
 
@@ -488,14 +531,34 @@
     keys.start()
     to_group()
 
-    for owner in range(4):
+
+    def relay_rest(owner):
         if needs[owner] is not None:
             @pl.when(across == owner)
             def _():
                 rest_copy(owner, 1, across).wait_recv()
                 rest_copy(owner, 2, mate).start()
 
-    keys.relay()
+    def settle_rest(owner):
+        if needs[owner] is not None:
+            @pl.when(mate == owner)
+            def _():
+                rest_copy(owner, 0, mate).wait_recv()
+
+            @pl.when(corner == owner)
+            def _():
+                rest_copy(owner, 2, mate).wait_recv()
+
+            @pl.when(n == owner)
+            def _():
+                rest_copy(owner, 1, across).wait_send()
+                rest_copy(owner, 0, mate).wait_send()
+
+            @pl.when(across == owner)
+            def _():
+                rest_copy(owner, 2, mate).wait_send()
+
+    relay_rest(0)
     for slot, block in ((0, mate), (1, across), (2, corner)):
         small_copy(slot, block).wait_recv()
         small_copy(slot, n).wait_send()
@@ -514,38 +577,25 @@
         noisy_down.wait_send()
         target_down.wait_send()
 
-    for owner in range(4):
-        if needs[owner] is not None:
-            @pl.when(mate == owner)
-            def _():
-                rest_copy(owner, 0, mate).wait_recv()
-
-            @pl.when(corner == owner)
-            def _():
-                rest_copy(owner, 2, mate).wait_recv()
-
-            @pl.when(n == owner)
-            def _():
-                rest_copy(owner, 1, across).wait_send()
-                rest_copy(owner, 0, mate).wait_send()
-
-            @pl.when(across == owner)
-            def _():
-                rest_copy(owner, 2, mate).wait_send()
-
+    settle_rest(0)
+    early(0)
+    for owner in range(1, 4):
+        relay_rest(owner)
+    keys.relay()
+    early(1)
+    for owner in range(1, 4):
+        settle_rest(owner)
     keys.wait()
     keys.drain()
     for part in texts:
         part.drain()
 
 
-def mid_body(
-    gd, height, columns, from_group, blocks, conv, packet, right, kvs, texts, *refs,
-):
+def mid_stages(gd, height, columns, from_group, blocks, conv, packet, right, kvs, texts, *refs):
     (
         dkv_all, conv_all, t_all, small_all, scal,
         near_b, near_c, sum_b, sum_c, far_b, far_c, own_b, own_c, group_b, group_c,
-        packets, wides, t_own, t_send, c_send, gram, norms, conv_sum,
+        packets, wides, t_own, t_send, c_send, norms, conv_sum,
         near_sem, far_sem, group_sem, packet_sem, wide_sem, norm_sem, give_sem,
     ) = refs
     ids = cross_ids()
@@ -557,7 +607,11 @@
     spot = lax.rem(wide, gd)
     tok, kv_block = kvs.shape[1:]
     heads = kv_block // HEAD
-    packets[n] = packet[...]
+    depth = texts.shape[-1]
+    scale = jnp.where(n < 2, 1.0 / math.sqrt(HEAD), 1.0)
+
+    def lanes(h):
+        return pl.ds(h * tok, tok)
 
     def near(slot, which):
         owner = corner if slot == 0 else mate
@@ -566,34 +620,29 @@
             src.at[owner], dst.at[slot], near_sem.at[0, slot, which], near_sem.at[1, slot, which], mate
         )
 
-    for slot in range(2):
-        for which in range(2):
-            near(slot, which).start()
+    def far(h):
+        if h < heads:
+            src, dst = sum_b.at[:, lanes(h)], far_b.at[:, lanes(h)]
+        else:
+            src, dst = sum_c, far_c
+        return to_narrow(src, dst, far_sem.at[0, h], far_sem.at[1, h], across)
+
+    def group_copy(k, h):
+        if h < heads:
+            src, dst = own_b.at[:, lanes(h)], group_b.at[k - 1, :, lanes(h)]
+        else:
+            src, dst = own_c, group_c.at[k - 1]
+        return pltpu.make_async_remote_copy(
+            src_ref=src, dst_ref=dst,
+            send_sem=group_sem.at[0, h, k - 1], recv_sem=group_sem.at[1, h, k - 1],
+            device_id={"wide": group * gd + lax.rem(spot + k, gd)}, device_id_type=MESH,
+        )
 
     def packet_copy(slot, block):
         return to_narrow(
             packets.at[block], packets.at[block],
             packet_sem.at[0, slot], packet_sem.at[1, slot], others[slot],
         )
-
-    for slot in range(3):
-        packet_copy(slot, n).start()
-
-    def far(which):
-        src, dst = ((sum_b, far_b), (sum_c, far_c))[which]
-        return to_narrow(src, dst, far_sem.at[0, which], far_sem.at[1, which], across)
-
-    near(0, 0).wait_recv()
-    sum_b[...] = (blocks[across].astype(F32) + near_b[0].astype(F32)).astype(BF16)
-    far(0).start()
-    near(0, 1).wait_recv()
-    sum_c[...] = (conv[across].astype(F32) + near_c[0].astype(F32)).astype(BF16)
-    far(1).start()
-
-    for slot, block in enumerate(others):
-        packet_copy(slot, block).wait_recv()
-    item = packets[0] + packets[1] + packets[2] + packets[3]
-    wides[wide] = item
 
     def wide_copy(k, block):
         return pltpu.make_async_remote_copy(
@@ -602,182 +651,210 @@
             device_id={"wide": lax.rem(wide + k, wide_count)}, device_id_type=MESH,
         )
 
-    @pl.loop(1, wide_count)
-    def _(k):
-        wide_copy(k, wide).start()
-
-    depth = texts.shape[-1]
-    from_group()
-    gram[...] = jnp.zeros_like(gram)
-
-    @pl.loop(0, depth // 1024)
-    def _(i):
-        at = pl.ds(pl.multiple_of(i * 1024, 1024), 1024)
+    def start_near():
+        for slot in range(2):
+            for which in range(2):
+                near(slot, which).start()
+
+    def start_far():
+        near(0, 0).wait_recv()
+        sum_b[...] = (blocks[across].astype(F32) + near_b[0].astype(F32)).astype(BF16)
+        for h in range(heads):
+            far(h).start()
+        near(0, 1).wait_recv()
+        sum_c[...] = (conv[across].astype(F32) + near_c[0].astype(F32)).astype(BF16)
+        far(heads).start()
+
+    q_rows, q_from = 96, 80
+
+    def give_head(src_n, h):
+        src, dst = t_send.at[pl.ds(0, q_rows), lanes(h)], t_all.at[src_n, pl.ds(0, q_rows), lanes(h)]
+        return to_narrow(src, dst, give_sem.at[0, 0, h], give_sem.at[1, src_n, h], 2)
+
+    def give_tail(src_n, h):
+        rows = pl.ds(q_from, C - q_from)
+        src, dst = t_send.at[rows, lanes(h)], t_all.at[src_n, rows, lanes(h)]
+        return to_narrow(src, dst, give_sem.at[0, 1, h], give_sem.at[1, src_n, h], 3)
+
+    def give_values(h):
+        src, dst = t_send.at[:, lanes(h)], t_all.at[2, :, lanes(h)]
+        return to_narrow(src, dst, give_sem.at[0, 1, h], give_sem.at[1, 2, h], 3)
+
+    def give_conv(src_n):
+        return to_narrow(
+            c_send, conv_all.at[src_n], give_sem.at[0, 2, 0], give_sem.at[1, src_n, heads], 0
+        )
+
+    def project(k, h, value):
+        cols = slice(h * HEAD, (h + 1) * HEAD)
+        dkv_all[k * tok : (k + 1) * tok, cols] = (dot(value, right[:, cols], TN) * scale).astype(BF16)
+        term = dot(value, kvs[k, :, cols]) * scale
+        t_own[:, cols] = term if k == 0 else t_own[:, cols] + term
+
+    def finish(gram):
+        packets[n] = packet[...]
+        for slot in range(3):
+            packet_copy(slot, n).start()
+        near(1, 0).wait_recv()
+        near(1, 1).wait_recv()
+        for h in range(heads):
+            far(h).wait_recv()
+            at = slice(h * tok, (h + 1) * tok)
+            own_b[:, at] = (
+                blocks[n, :, at].astype(F32) + near_b[1, :, at].astype(F32) + far_b[:, at].astype(F32)
+            ).astype(BF16)
+            for k in range(1, gd):
+                group_copy(k, h).start()
+        for slot, block in enumerate(others):
+            packet_copy(slot, block).wait_recv()
+        wides[wide] = packets[0] + packets[1] + packets[2] + packets[3]
+
+        @pl.loop(1, wide_count)
+        def _(k):
+            wide_copy(k, wide).start()
+
+        far(heads).wait_recv()
+        conv_sum[...] = conv[n].astype(F32) + near_c[1].astype(F32) + far_c[...].astype(F32)
+        own_c[...] = conv_sum[...].astype(BF16)
+        for k in range(1, gd):
+            group_copy(k, heads).start()
+        for h in range(heads):
+            project(0, h, own_b[:, h * tok : (h + 1) * tok])
+        from_group()
+        def text_products(a, firsts):
+            rows = slice(a * tok, (a + 1) * tok) if gd <= 4 else slice(0, tok)
+            gram[rows, :] = jnp.zeros((tok, gd * tok), F32)
+
+            @pl.loop(0, depth // 1024)
+            def _(i):
+                at = pl.ds(pl.multiple_of(i * 1024, 1024), 1024)
+                left = texts[a, :, :, at].reshape(tok, 1024)
+                for b in range(firsts, gd):
+                    part = dot(left, texts[b, :, :, at].reshape(tok, 1024), NT)
+                    gram[rows, b * tok : (b + 1) * tok] += part
+
+        if gd <= 4:
+            for a in range(gd):
+                text_products(a, a)
+        for h in range(heads):
+            for k in range(1, gd):
+                group_copy(k, h).wait_recv()
+                project(k, h, group_b[k - 1, :, h * tok : (h + 1) * tok])
+            at = slice(h * HEAD, (h + 1) * HEAD)
+            t_send[:, at] = t_own[:, at].astype(BF16)
+            for k in range(4):
+                @pl.when(n == k)
+                def _():
+                    if k < 2:
+                        give_head(k, h).start()
+                        give_tail(k, h).start()
+                    elif k == 2:
+                        give_values(h).start()
+                    else:
+                        t_all[3, :, at] = t_send[:, at]
+        for k in range(1, gd):
+            group_copy(k, heads).wait_recv()
+            conv_sum[...] += group_c[k - 1].astype(F32)
+        c_send[...] = conv_sum[...].astype(BF16)
+        for k in range(4):
+            @pl.when(n == k)
+            def _():
+                if k > 0:
+                    give_conv(k).start()
+                else:
+                    conv_all[0] = c_send[...]
+
+        @pl.loop(1, wide_count)
+        def _(k):
+            wide_copy(k, lax.rem(wide + wide_count - k, wide_count)).wait_recv()
+
+        sq = jnp.sum(t_own[...] * t_own[...]) + jnp.sum(conv_sum[...] * conv_sum[...])
         for a in range(gd):
-            left = texts[a, :, :, at].reshape(tok, 1024)
+            da = dkv_all[a * tok : (a + 1) * tok, :]
+            if gd > 4:
+                text_products(a, a)
+            rows = slice(a * tok, (a + 1) * tok) if gd <= 4 else slice(0, tok)
             for b in range(a, gd):
-                part = dot(left, texts[b, :, :, at].reshape(tok, 1024), NT)
-                gram[a * tok : (a + 1) * tok, b * tok : (b + 1) * tok] += part
-
-    near(1, 0).wait_recv()
-    near(1, 1).wait_recv()
-    far(0).wait_recv()
-    own_b[...] = (
-        blocks[n].astype(F32) + near_b[1].astype(F32) + far_b[...].astype(F32)
-    ).astype(BF16)
-
-    def group_copy(k, which):
-        src, dst = ((own_b, group_b), (own_c, group_c))[which]
-        return pltpu.make_async_remote_copy(
-            src_ref=src, dst_ref=dst.at[k - 1],
-            send_sem=group_sem.at[0, which, k - 1], recv_sem=group_sem.at[1, which, k - 1],
-            device_id={"wide": group * gd + lax.rem(spot + k, gd)}, device_id_type=MESH,
-        )
-
-    for k in range(1, gd):
-        group_copy(k, 0).start()
-    far(1).wait_recv()
-    conv_sum[...] = conv[n].astype(F32) + near_c[1].astype(F32) + far_c[...].astype(F32)
-    own_c[...] = conv_sum[...].astype(BF16)
-    for k in range(1, gd):
-        group_copy(k, 1).start()
-
-    scale = jnp.where(n < 2, 1.0 / math.sqrt(HEAD), 1.0)
-
-    def project(k, value):
-        for h in range(heads):
-            cols = slice(h * HEAD, (h + 1) * HEAD)
-            part = value[:, h * tok : (h + 1) * tok]
-            dkv_all[k * tok : (k + 1) * tok, cols] = (dot(part, right[:, cols], TN) * scale).astype(BF16)
-            term = dot(part, kvs[k, :, cols]) * scale
-            t_own[:, cols] = term if k == 0 else t_own[:, cols] + term
-
-    project(0, own_b[...])
-    for k in range(1, gd):
-        group_copy(k, 0).wait_recv()
-        project(k, group_b[k - 1])
-        group_copy(k, 1).wait_recv()
-        conv_sum[...] += group_c[k - 1].astype(F32)
-    t_send[...] = t_own[...].astype(BF16)
-    c_send[...] = conv_sum[...].astype(BF16)
-
-    q_rows = 96
-    q_from = 80
-
-    def give_conv(src_n):
-        return to_narrow(c_send, conv_all.at[src_n], give_sem.at[0, 0], give_sem.at[1, src_n], 0)
-
-    def give_head(src_n):
-        at = pl.ds(0, q_rows)
-        return to_narrow(t_send.at[at], t_all.at[src_n, at], give_sem.at[0, 1], give_sem.at[1, src_n], 2)
-
-    def give_tail(src_n):
-        at = pl.ds(q_from, C - q_from)
-        return to_narrow(t_send.at[at], t_all.at[src_n, at], give_sem.at[0, 2], give_sem.at[1, src_n], 3)
-
-    def give_values():
-        return to_narrow(t_send, t_all.at[2], give_sem.at[0, 1], give_sem.at[1, 2], 3)
-
-    for k in range(4):
-        @pl.when(n == k)
-        def _():
-            if k < 2:
-                give_head(k).start()
-                give_tail(k).start()
-            if k == 2:
-                give_values().start()
-            if k > 0:
-                give_conv(k).start()
-            else:
-                conv_all[0] = c_send[...]
-            if k == 3:
-                t_all[3] = t_send[...]
-
-    @pl.loop(1, wide_count)
-    def _(k):
-        wide_copy(k, lax.rem(wide + wide_count - k, wide_count)).wait_recv()
-
-    sq = jnp.sum(t_own[...] * t_own[...]) + jnp.sum(conv_sum[...] * conv_sum[...])
-    for a in range(gd):
-        da = dkv_all[a * tok : (a + 1) * tok, :]
-        for b in range(a, gd):
-            db = dkv_all[b * tok : (b + 1) * tok, :]
-            top, low = two_parts(gram[a * tok : (a + 1) * tok, b * tok : (b + 1) * tok])
-            part = jnp.sum(da.astype(F32) * (dot(top, db) + dot(low, db)))
-            sq = sq + (part if a == b else 2.0 * part)
-    gains = jnp.zeros((4, C), F32)
-    shared = jnp.zeros((1, C), F32)
-    for a in range(gd):
-        mine = wides[group * gd + a]
-        small_all[a] = mine
-        gains = gains + mine[0:4]
-        for b in range(gd):
-            his = wides[group * gd + b]
-            same = (mine[7:8, 0:1] == his[7:8, 0:1]).astype(F32) + (mine[7:8, 1:2] == his[7:8, 1:2]).astype(F32)
-            shared = shared + same * (mine[4:5] * his[4:5] + mine[5:6] * his[5:6])
-    shared_sq = jnp.sum(gains * gains) + jnp.sum(shared)
-    norms[n] = jnp.full((8, C), sq + jnp.where(n == 0, shared_sq, 0.0), F32)
-
-    def norm_copy(slot, block):
-        return to_narrow(
-            norms.at[block], norms.at[block], norm_sem.at[0, slot], norm_sem.at[1, slot], others[slot]
-        )
-
-    for slot in range(3):
-        norm_copy(slot, n).start()
-
-    def tally(k, found):
-        there = wides[k]
-        crop = there[7:8, 2:3]
-        pixels = jnp.minimum(crop, float(height)) * jnp.minimum(crop, float(columns))
-        mine = jnp.where(k // gd == group, pixels, 0.0)
-        return found[0] + pixels, found[1] + mine, found[2] + jnp.sum(there[6:7], axis=1, keepdims=True)
-
-    none = jnp.zeros((1, 1), F32)
-    total, own_count, loss = lax.fori_loop(0, wide_count, tally, (none, none, none))
-    for slot, block in enumerate(others):
-        norm_copy(slot, block).wait_recv()
-    squares = norms[0, 0:1] + norms[1, 0:1] + norms[2, 0:1] + norms[3, 0:1]
-    norm = jnp.sqrt(squares) / total
-    scal[0:1] = jnp.minimum(1.0, CLIP_NORM / norm) / total
-    scal[1:2] = jnp.broadcast_to(INNER_RATE * own_count / total, (1, C))
-    scal[2:3] = jnp.broadcast_to(loss, (1, C))
-    scal[3:4] = jnp.broadcast_to(total, (1, C))
-    scal[4:8] = jnp.zeros((4, C), F32)
-
-    for k in range(4):
-        @pl.when(n == k)
-        def _():
-            if k < 2:
-                give_head(k).wait_send()
-                give_tail(k).wait_send()
-            if k == 2:
-                give_values().wait_send()
-                give_head(0).wait_recv()
-                give_head(1).wait_recv()
-            if k == 3:
-                give_tail(0).wait_recv()
-                give_tail(1).wait_recv()
-                give_values().wait_recv()
-            if k > 0:
-                give_conv(k).wait_send()
-            else:
-                for j in range(1, 4):
-                    give_conv(j).wait_recv()
-    for slot in range(2):
-        for which in range(2):
-            near(slot, which).wait_send()
-    for which in range(2):
-        far(which).wait_send()
-        for k in range(1, gd):
-            group_copy(k, which).wait_send()
-    for slot in range(3):
-        packet_copy(slot, n).wait_send()
-        norm_copy(slot, n).wait_send()
-
-    @pl.loop(1, wide_count)
-    def _(k):
-        wide_copy(k, wide).wait_send()
+                db = dkv_all[b * tok : (b + 1) * tok, :]
+                top, low = two_parts(gram[rows, b * tok : (b + 1) * tok])
+                part = jnp.sum(da.astype(F32) * (dot(top, db) + dot(low, db)))
+                sq = sq + (part if a == b else 2.0 * part)
+        gains = jnp.zeros((4, C), F32)
+        shared = jnp.zeros((1, C), F32)
+        for a in range(gd):
+            mine = wides[group * gd + a]
+            small_all[a] = mine
+            gains = gains + mine[0:4]
+            for b in range(gd):
+                his = wides[group * gd + b]
+                same = (mine[7:8, 0:1] == his[7:8, 0:1]).astype(F32) + (mine[7:8, 1:2] == his[7:8, 1:2]).astype(F32)
+                shared = shared + same * (mine[4:5] * his[4:5] + mine[5:6] * his[5:6])
+        shared_sq = jnp.sum(gains * gains) + jnp.sum(shared)
+        norms[n] = jnp.full((8, C), sq + jnp.where(n == 0, shared_sq, 0.0), F32)
+
+        def norm_copy(slot, block):
+            return to_narrow(
+                norms.at[block], norms.at[block], norm_sem.at[0, slot], norm_sem.at[1, slot], others[slot]
+            )
+
+        for slot in range(3):
+            norm_copy(slot, n).start()
+
+        def tally(k, found):
+            there = wides[k]
+            crop = there[7:8, 2:3]
+            pixels = jnp.minimum(crop, float(height)) * jnp.minimum(crop, float(columns))
+            mine = jnp.where(k // gd == group, pixels, 0.0)
+            return found[0] + pixels, found[1] + mine, found[2] + jnp.sum(there[6:7], axis=1, keepdims=True)
+
+        none = jnp.zeros((1, 1), F32)
+        total, own_count, loss = lax.fori_loop(0, wide_count, tally, (none, none, none))
+        for slot, block in enumerate(others):
+            norm_copy(slot, block).wait_recv()
+        squares = norms[0, 0:1] + norms[1, 0:1] + norms[2, 0:1] + norms[3, 0:1]
+        norm = jnp.sqrt(squares) / total
+        scal[0:1] = jnp.minimum(1.0, CLIP_NORM / norm) / total
+        scal[1:2] = jnp.broadcast_to(INNER_RATE * own_count / total, (1, C))
+        scal[2:3] = jnp.broadcast_to(loss, (1, C))
+        scal[3:4] = jnp.broadcast_to(total, (1, C))
+        scal[4:8] = jnp.zeros((4, C), F32)
+
+        for k in range(4):
+            @pl.when(n == k)
+            def _():
+                for h in range(heads):
+                    if k < 2:
+                        give_head(k, h).wait_send()
+                        give_tail(k, h).wait_send()
+                    if k == 2:
+                        give_values(h).wait_send()
+                        give_head(0, h).wait_recv()
+                        give_head(1, h).wait_recv()
+                    if k == 3:
+                        give_tail(0, h).wait_recv()
+                        give_tail(1, h).wait_recv()
+                        give_values(h).wait_recv()
+                if k > 0:
+                    give_conv(k).wait_send()
+                else:
+                    for j in range(1, 4):
+                        give_conv(j).wait_recv()
+        for slot in range(2):
+            for which in range(2):
+                near(slot, which).wait_send()
+        for h in range(heads + 1):
+            far(h).wait_send()
+            for k in range(1, gd):
+                group_copy(k, h).wait_send()
+        for slot in range(3):
+            packet_copy(slot, n).wait_send()
+            norm_copy(slot, n).wait_send()
+
+        @pl.loop(1, wide_count)
+        def _(k):
+            wide_copy(k, wide).wait_send()
+
+    return start_near, start_far, finish
 
 
 def step_kernel(gd, wide_count, kv_rows, rest_rows, band, columns, counts, *refs):
@@ -787,7 +864,8 @@
     n_front, n_main, n_mid = counts
     at = 18
     (noisy_ext, target_ext, rest_all, keyval, kvs, small) = refs[at : at + 6]
-    at += 6
+    act3, wt3, conv_s, xhat_s, rs_s, low_s = refs[at + 6 : at + 12]
+    at += 12
     front_sems = refs[at : at + n_front]
     at += n_front
     (blocks, conv, packet, right) = refs[at : at + 4]
@@ -836,9 +914,17 @@
                 group_send(k, which).wait_recv()
                 group_send(k, which).wait_send()
 
+    def early(part):
+        common = (band, columns, H, noisy_ext, small, rest_all.at[0], act3)
+        tiles = pl.cdiv(band + 2, CTILE)
+        if part == 0:
+            activate(*common, wt3)
+        bounds = (0, 2) if part == 0 else (2, tiles)
+        convolve_tiles(*bounds, *common, conv_s, xhat_s, rs_s, low_s)
+
     def front(wide_f32, wide_bf, rest_f32, acc):
         front_body(
-            kv_rows, rest_rows, greet, to_group, noise_level, aug_level, weights, noisy, target, text, mask,
+            kv_rows, rest_rows, greet, to_group, early, noise_level, aug_level, weights, noisy, target, text, mask,
             noisy_ext, target_ext, texts.at[0], rest_all, keyval, kvs.at[0], small,
             wide_f32, wide_bf, rest_f32, acc, *front_sems,
         )
@@ -852,15 +938,20 @@
         copy.start()
     pix = TILE * columns
 
+    start_near, start_far, finish = mid_stages(
+        gd, H, W, from_group, blocks, conv, packet, right, kvs, texts,
+        dkv_all, conv_all, t_all, small_all, scal, *mid_refs,
+    )
+
     def main(*scratch):
         main_body(
-            band, columns, H, HEADS, rest_rows, crop_size, noise_level, aug_level,
-            noisy_ext, target_ext, small, rest_all, keyval, blocks, conv, packet, right, *scratch,
+            start_near, start_far, band, columns, H, HEADS, rest_rows, crop_size, noise_level, aug_level,
+            noisy_ext, target_ext, small, rest_all, keyval, blocks, conv, packet, right,
+            act3, wt3, conv_s, xhat_s, rs_s, low_s, *scratch,
         )
 
     pl.run_scoped(
         main,
-        V((band + 4, columns, 3 * C), BF16),
         V((band + 2, columns, 3 * C), BF16),
         V((2 * C, HEADS * tok), BF16),
         V((HEADS * tok, 2 * C), BF16),
@@ -869,7 +960,6 @@
         V((C, 9 * C), F32),
         V((pix, HEADS * tok), BF16),
         V((pix, HEADS * tok), BF16),
-        V((9 * C, C), BF16),
         V((C, HEADS * tok), F32),
         V((C, HEADS * tok), F32),
         V((8, C), F32),
@@ -878,13 +968,7 @@
         V((HEADS * HEAD, C), F32),
     )
 
-    def middle(gram):
-        mid_body(
-            gd, H, W, from_group, blocks, conv, packet, right, kvs, texts,
-            dkv_all, conv_all, t_all, small_all, scal, *mid_refs[:15], gram, *mid_refs[15:],
-        )
-
-    pl.run_scoped(middle, V((gd * tok, gd * tok), F32))
+    pl.run_scoped(finish, V((gd * tok if gd <= 4 else tok, gd * tok), F32))
     for copy in ahead:
         copy.wait()
 
@@ -917,6 +1001,7 @@
     hbm = pl.BlockSpec(memory_space=pltpu.HBM)
     D, V = pltpu.SemaphoreType.DMA, pltpu.VMEM
     few = max(gd - 1, 1)
+    heads = kv_block // HEAD
     bshape, cshape = (C, kv_block // HEAD * tok), (9 * C // 4, C)
     front_sems = [D((WPARTS,)), D((4,)), D((KPARTS, 2, 3)), D((2, 3, 4)), D((2, 3)), D((2, 3)), D((2, 4))]
     mid_refs = [
@@ -926,7 +1011,8 @@
         V((4, 8, C), F32), V((wide_count, 8, C), F32),
         V((C, kv_block), F32), V((C, kv_block), BF16), V(cshape, BF16),
         V((4, 8, C), F32), V(cshape, F32),
-        D((2, 2, 2)), D((2, 2)), D((2, 2, few)), D((2, 3)), D((2, wide_count)), D((2, 3)), D((2, 4)),
+        D((2, 2, 2)), D((2, heads + 1)), D((2, heads + 1, few)), D((2, 3)), D((2, wide_count)), D((2, 3)),
+        D((2, 4, heads + 1)),
     ]
     return pl.pallas_call(
         functools.partial(
@@ -950,7 +1036,9 @@
         out_specs=(vmem,) * 8,
         scratch_shapes=[
             V((band + 4, columns, C), BF16), V((band + 2, columns, C), BF16), V((4, rest_pad, C), BF16),
-            V((4, tok, kv_block), BF16), V((gd, tok, kv_block), BF16), V((4, 8, C), F32),
+            V((4, tok, kv_block), BF16), V((gd, tok, kv_block), BF16), V((4, 16, C), F32),
+            V((band + 4, columns, 3 * C), BF16), V((9 * C, C), BF16),
+            *[V((band + 2, columns, C), F32)] * 3, V((band + 2, columns, C), BF16),
             *front_sems,
             V((4,) + bshape, BF16), V((4,) + cshape, BF16), V((8, C), F32), V((C, kv_block), BF16),
             *mid_refs,
@@ -1365,10 +1453,10 @@
     moment_one, moment_two, step = run_adam(
         texts, dkv, conv_all, t_all, small_all, scal, first, second, length, kv_rows, rest_rows
     )
-    chunk = 320
+    chunk = 160
     rows = pl.cdiv(length // C + 18, chunk) * chunk
     pad = 1120
-    pieces, w_near, o_near = share(step, weights2, outer2, gd, rows, chunk, pad, 2, 4)
+    pieces, w_near, o_near = share(step, weights2, outer2, gd, rows, chunk, pad, 3, 6)
     bases = [p * length // C // 16 * 16 for p in range(gd)]
     new_weights, momentum_out, loss, count = run_final(
         weights2.shape[0], w_near, o_near, pieces, scal, bases, pad

time: 166 us -> 159 us (0.958)
  Pallas kernels: 163 us -> 156 us
    pallas_call x1, Pallas kernels: 75.8 us -> 70.2 us  [run_step(): pl.pallas_call(functools.partial(step_kernel, gd, wide_count, kv_rows, re...]
    pallas_call x1, Pallas kernels: 70.6 us -> 68.9 us  [share(): pl.pallas_call(functools.partial(share_kernel, gd, rows, chunk, pad, l1,...]
where the time goes in v4:
time: 159 us
  Pallas kernels  156 us (98%)
  between operations  2.77 us (2%)
    pallas_call x1, Pallas kernels, run_step(): pl.pallas_call(functools.partial(step_kernel, gd, wide_count, kv_rows, re...  70.2 us
    pallas_call x1, Pallas kernels, share(): pl.pallas_call(functools.partial(share_kernel, gd, rows, chunk, pad, l1,...  68.9 us
    pallas_call x1, Pallas kernels, run_adam(): pl.pallas_call(functools.partial(adam_kernel, gd, length, kv_rows, rest_r...  9.07 us
    pallas_call x1, Pallas kernels, run_final(): pl.pallas_call(functools.partial(final_kernel, bases, pad, block), out_sh...  8.02 us

profile of v4, /device:TPU:0, one launch (start us, length us, event | category | flops | bytes accessed | tf_op | source)
XLA Modules:
  0.0 159.0 jit_solution(21642542572553725)
XLA Ops:
  2.6 70.2 %step.1 = (bf16[2,4,32,4096]{3,2,1,0:T(8,128)(2,1)S(1)}, bf16[256,512]{1,0:T(8,128)(2,1)S(1)}, bf16[4,288,128]{2,1,0:T(8,128)(2,1)S(1)}, bf16[4,128,512]{2,1,0:T...) custom-call(s32[1]{0:T(128)S(6)} %copy.17.refs_0_, ...), custom_call_target="tpu_custom_call" | custom-call | tf_op jit(solution)/shard_map/step/pallas_call | solution.py:1017
  72.8 9.1 %adam.1 = (f32[1,1132608]{1,0:T(1,128)}, f32[1,1132608]{1,0:T(1,128)}, bf16[9216,128]{1,0:T(8,128)(2,1)S(1)}) custom-call(bf16[2,4,32,4096]{3,2,1,0:T(8,128)(2,1)S(1)} %get-tuple-element.24.refs_0_, bf16[256,512]{1,0:T(8,128)(2,1)S(1)} %get-tuple-element.25.refs_1_, bf16[4,288,128]{2,1,0:T(8,128)(2,1)S(1)} %get-tuple-element.26.refs_2_, ...), custom_call_target="tpu_custom_call" | custom-call | tf_op jit(solution)/shard_map/adam/pallas_call | solution.py:1215
  81.8 68.9 %share.1 = (bf16[2,11200,128]{2,1,0:T(8,128)(2,1)S(1)}, f32[17920,128]{1,0:T(8,128)S(1)}, f32[17920,128]{1,0:T(8,128)S(1)}) custom-call(bf16[9216,128]{1,0:T(8,128)(2,1)S(1)} %get-tuple-element.32.u_ref, f32[17697,128]{1,0:T(8,128)} %bitcast.5, f32[17697,128]{1,0:T(8,128)} %bitcast.6), custom_call_target="tpu_custom_call" | custom-call | tf_op jit(solution)/shard_map/share/pallas_call | solution.py:1366
  150.8 8.0 %final.1 = (f32[17697,128]{1,0:T(8,128)}, f32[17697,128]{1,0:T(8,128)}, f32[1]{0:T(128)}, f32[1]{0:T(128)}) custom-call(f32[17920,128]{1,0:T(8,128)S(1)} %get-tuple-element.33.weights, f32[17920,128]{1,0:T(8,128)S(1)} %get-tuple-element.34.outer, bf16[2,11200,128]{2,1,0:T(8,128)(2,1)S(1)} %get-tuple-element.35.pieces, ...), custom_call_target="tpu_custom_call" | custom-call | tf_op jit(solution)/shard_map/final/pallas_call | solution.py:1426

commit v5 on v4

--- a/solution.py
+++ b/solution.py
@@ -39,7 +39,7 @@
 LOG2E = 1.4426950408889634
 LN2 = 0.6931471805599453
 NT = (((1,), (1,)), ((), ()))
-TILE = 7
+TILE = 8
 TILE3 = 8
 
 
@@ -56,7 +56,7 @@
     return jnp.where(keep, pltpu.roll(value, by, 0), 0.0)
 
 
-CTILE = 7
+CTILE = 16
 
 
 def vectors(small, height, columns):
@@ -107,10 +107,10 @@
 
     @pl.loop(first, last)
     def _(t):
-        q = jnp.minimum(t * CTILE, band + 2 - CTILE)
-        conv = noisy[pl.ds(q + 1, CTILE)].astype(F32).reshape(pix, C)
+        q = t * CTILE
+        conv = noisy[pl.ds(q + 2, CTILE)].astype(F32).reshape(pix, C)
         for dy in range(3):
-            window = act3[pl.ds(q + dy, CTILE)].reshape(pix, 3 * C)
+            window = act3[pl.ds(q + 1 + dy, CTILE)].reshape(pix, 3 * C)
             conv = conv + dot(window, conv_w[dy * 3 * C : (dy + 1) * 3 * C, :])
         centered = conv - jnp.mean(conv, axis=1, keepdims=True)
         rs = lax.rsqrt(jnp.mean(centered * centered, axis=1, keepdims=True) + EPS_NORM)
@@ -123,11 +123,11 @@
 
 
 def main_body(
-    start_near, start_far, band, columns, height, heads,
+    start_near, start_far, edge_send, edge_wait, band, columns, height, heads,
     rest_rows, crop_size, noise_level, aug_level, noisy, target, small, rest, keyval,
     blocks, dconv_w, packet, right,
-    act3, wt3, conv_s, xhat_s, rs_s, low_s,
-    diff3, m_cat, m_cat_t, n_cat, n_cat_t, conv_t, probs, dscore, y_t, z_t, sums,
+    act3, wt3, conv_s, xhat_s, rs_s, low_s, diff3,
+    m_cat, m_cat_t, n_cat, n_cat_t, conv_t, probs, dscore, y_t, z_t, sums,
     stage, query, out_w,
 ):
     tok, kv_block = keyval.shape[1:]
@@ -203,9 +203,11 @@
     not_first, not_last = edges(columns)
     pix_row = lax.broadcasted_iota(jnp.int32, (pix, C), 0) // columns
     pix_col = lax.broadcasted_iota(jnp.int32, (pix, C), 0) % columns
-    @pl.loop(0, pl.cdiv(band + 2, TILE))
+    tiles = band // TILE
+
+    @pl.loop(0, tiles)
     def _(t):
-        q = jnp.minimum(t * TILE, band + 2 - TILE)
+        q = jnp.where(t == 0, 0, jnp.where(t == 1, tiles - 1, t - 1)) * TILE
         here = pl.ds(q, TILE)
         conv = conv_s[here].reshape(pix, C)
         low = low_s[here].reshape(pix, C)
@@ -221,13 +223,9 @@
             probs[:, tcols] = p.astype(BF16)
         mixed = dot(probs[...], n_cat[...])
         output = conv + mixed[:, :C] + mixed[:, C:]
-        row = row0 + q - 1 + pix_row
-        valid = (row >= 0) & (row < crop) & (pix_col < crop)
-        err = jnp.where(valid, output - target[pl.ds(q, TILE)].astype(F32).reshape(pix, C), 0.0)
-        own_row = q + pix_row
-        own = (own_row >= jnp.maximum(t * TILE, 1)) & (own_row <= band)
-        err_own = jnp.where(own, err, 0.0)
-        sums[4:5, :] += jnp.sum(err_own * err_own, axis=0, keepdims=True)
+        valid = (row0 + q + pix_row < crop) & (pix_col < crop)
+        err = jnp.where(valid, output - target[pl.ds(q + 1, TILE)].astype(F32).reshape(pix, C), 0.0)
+        sums[4:5, :] += jnp.sum(err * err, axis=0, keepdims=True)
         dout = 2.0 * err
         dout_low = dout.astype(BF16)
         dout2 = jnp.concatenate([dout_low, dout_low], axis=1)
@@ -242,30 +240,34 @@
             dscore[:, tcols] = ds.astype(BF16)
         dlay2 = dot(dscore[...], m_cat_t[...])
         dlay = (dlay2[:, :C] + dlay2[:, C:]) * LN2
-        dlay_own = jnp.where(own, dlay, 0.0)
         xhat = xhat_s[here].reshape(pix, C)
         rs = rs_s[here].reshape(pix, C)
-        sums[2:3, :] += jnp.sum(dlay_own * xhat, axis=0, keepdims=True)
-        sums[3:4, :] += jnp.sum(dlay_own, axis=0, keepdims=True)
+        sums[2:3, :] += jnp.sum(dlay * xhat, axis=0, keepdims=True)
+        sums[3:4, :] += jnp.sum(dlay, axis=0, keepdims=True)
         dxh = dlay * ln_gain
         dconv = dout + rs * (
             dxh
             - jnp.mean(dxh, axis=1, keepdims=True)
             - xhat * jnp.mean(dxh * xhat, axis=1, keepdims=True)
         )
-        dout_t = (2.0 * err_own).T.astype(BF16)
-        lay_t = jnp.where(own, low.astype(F32), 0.0).T.astype(BF16)
+        dout_t = dout.T.astype(BF16)
+        lay_t = low.astype(F32).T.astype(BF16)
         y_t[...] += dot(dout_t, probs[...])
         z_t[...] += dot(lay_t, dscore[...])
-        dconv_t = jnp.where(own, dconv, 0.0).T.astype(BF16)
+        dconv_t = dconv.T.astype(BF16)
         for dy in range(3):
-            window = act3[pl.ds(q + dy, TILE)].reshape(pix, 3 * C)
+            window = act3[pl.ds(q + 1 + dy, TILE)].reshape(pix, 3 * C)
             conv_t[:, dy * 3 * C : (dy + 1) * 3 * C] += dot(dconv_t, window)
         for k in range(TILE):
             one = dconv[k * columns : (k + 1) * columns]
-            diff3[q + k, :, 0:C] = shifted(one, columns - 1, not_last).astype(BF16)
-            diff3[q + k, :, C : 2 * C] = one.astype(BF16)
-            diff3[q + k, :, 2 * C : 3 * C] = shifted(one, 1, not_first).astype(BF16)
+            diff3[q + 1 + k, :, 0:C] = shifted(one, columns - 1, not_last).astype(BF16)
+            diff3[q + 1 + k, :, C : 2 * C] = one.astype(BF16)
+            diff3[q + 1 + k, :, 2 * C : 3 * C] = shifted(one, 1, not_first).astype(BF16)
+
+        for order in range(2):
+            @pl.when(t == order)
+            def _():
+                edge_send(order)
 
     def back(t):
         r = t * TILE3
@@ -288,6 +290,7 @@
         at = owner % 2 * per_block * tok
         blocks[owner] = part[:, at : at + per_block * tok].astype(BF16)
     start_near()
+    edge_wait()
     halves = band // TILE3 // 2
     pl.loop(0, halves)(back)
     start_far()
@@ -460,32 +463,21 @@
     noisy_down = to_narrow(
         noisy_ext.at[pl.ds(band, 2)], noisy_ext.at[pl.ds(0, 2)], halo_sem.at[0, 1], halo_sem.at[1, 1], down
     )
-    target_up = to_narrow(
-        target_ext.at[pl.ds(1, 1)], target_ext.at[pl.ds(band + 1, 1)], halo_sem.at[0, 2], halo_sem.at[1, 2], up
-    )
-    target_down = to_narrow(
-        target_ext.at[pl.ds(band, 1)], target_ext.at[pl.ds(0, 1)], halo_sem.at[0, 3], halo_sem.at[1, 3], down
-    )
-
     @pl.when(n > 0)
     def _():
         noisy_up.start()
-        target_up.start()
 
     @pl.when(n < 3)
     def _():
         noisy_down.start()
-        target_down.start()
 
     @pl.when(n == 0)
     def _():
         noisy_ext[0:2] = jnp.zeros((2,) + noisy_ext.shape[1:], BF16)
-        target_ext[0:1] = jnp.zeros((1,) + target_ext.shape[1:], BF16)
 
     @pl.when(n == 3)
     def _():
         noisy_ext[band + 2 : band + 4] = jnp.zeros((2,) + noisy_ext.shape[1:], BF16)
-        target_ext[band + 1 : band + 2] = jnp.zeros((1,) + target_ext.shape[1:], BF16)
 
     needs = rest_needs(rest_rows)
     rest_all[n] = rest_f32[...].astype(BF16)
@@ -566,16 +558,12 @@
     @pl.when(n > 0)
     def _():
         noisy_down.wait_recv()
-        target_down.wait_recv()
         noisy_up.wait_send()
-        target_up.wait_send()
 
     @pl.when(n < 3)
     def _():
         noisy_up.wait_recv()
-        target_up.wait_recv()
         noisy_down.wait_send()
-        target_down.wait_send()
 
     settle_rest(0)
     early(0)
@@ -864,15 +852,15 @@
     n_front, n_main, n_mid = counts
     at = 18
     (noisy_ext, target_ext, rest_all, keyval, kvs, small) = refs[at : at + 6]
-    act3, wt3, conv_s, xhat_s, rs_s, low_s = refs[at + 6 : at + 12]
-    at += 12
+    act3, wt3, conv_s, xhat_s, rs_s, low_s, diff3 = refs[at + 6 : at + 13]
+    at += 13
     front_sems = refs[at : at + n_front]
     at += n_front
     (blocks, conv, packet, right) = refs[at : at + 4]
     at += 4
     mid_refs = refs[at : at + n_mid]
     at += n_mid
-    group_text_sem, ahead_sem = refs[at], refs[at + 1]
+    group_text_sem, ahead_sem, edge_sem = refs[at : at + 3]
     ahead = [
         pltpu.make_async_copy(far, near, ahead_sem.at[k])
         for k, (far, near) in enumerate(((first, first_near), (second, second_near)))
@@ -916,10 +904,10 @@
 
     def early(part):
         common = (band, columns, H, noisy_ext, small, rest_all.at[0], act3)
-        tiles = pl.cdiv(band + 2, CTILE)
+        tiles = band // CTILE
         if part == 0:
             activate(*common, wt3)
-        bounds = (0, 2) if part == 0 else (2, tiles)
+        bounds = (0, tiles // 2) if part == 0 else (tiles // 2, tiles)
         convolve_tiles(*bounds, *common, conv_s, xhat_s, rs_s, low_s)
 
     def front(wide_f32, wide_bf, rest_f32, acc):
@@ -943,16 +931,44 @@
         dkv_all, conv_all, t_all, small_all, scal, *mid_refs,
     )
 
+    def edge(order):
+        src, dst = (1, band + 1) if order == 0 else (band, 0)
+        other = jnp.maximum(n - 1, 0) if order == 0 else jnp.minimum(n + 1, 3)
+        return to_narrow(diff3.at[src], diff3.at[dst], edge_sem.at[0, order], edge_sem.at[1, order], other)
+
+    def edge_send(order):
+        @pl.when(n > 0 if order == 0 else n < 3)
+        def _():
+            edge(order).start()
+
+    def edge_wait():
+        @pl.when(n > 0)
+        def _():
+            edge(1).wait_recv()
+            edge(0).wait_send()
+
+        @pl.when(n < 3)
+        def _():
+            edge(0).wait_recv()
+            edge(1).wait_send()
+
+        @pl.when(n == 0)
+        def _():
+            diff3[0] = jnp.zeros(diff3.shape[1:], BF16)
+
+        @pl.when(n == 3)
+        def _():
+            diff3[band + 1] = jnp.zeros(diff3.shape[1:], BF16)
+
     def main(*scratch):
         main_body(
-            start_near, start_far, band, columns, H, HEADS, rest_rows, crop_size, noise_level, aug_level,
+            start_near, start_far, edge_send, edge_wait, band, columns, H, HEADS, rest_rows, crop_size, noise_level, aug_level,
             noisy_ext, target_ext, small, rest_all, keyval, blocks, conv, packet, right,
-            act3, wt3, conv_s, xhat_s, rs_s, low_s, *scratch,
+            act3, wt3, conv_s, xhat_s, rs_s, low_s, diff3, *scratch,
         )
 
     pl.run_scoped(
         main,
-        V((band + 2, columns, 3 * C), BF16),
         V((2 * C, HEADS * tok), BF16),
         V((HEADS * tok, 2 * C), BF16),
         V((HEADS * tok, 2 * C), BF16),
@@ -1038,24 +1054,26 @@
             V((band + 4, columns, C), BF16), V((band + 2, columns, C), BF16), V((4, rest_pad, C), BF16),
             V((4, tok, kv_block), BF16), V((gd, tok, kv_block), BF16), V((4, 16, C), F32),
             V((band + 4, columns, 3 * C), BF16), V((9 * C, C), BF16),
-            *[V((band + 2, columns, C), F32)] * 3, V((band + 2, columns, C), BF16),
+            *[V((band, columns, C), F32)] * 3, V((band, columns, C), BF16),
+            V((band + 2, columns, 3 * C), BF16),
             *front_sems,
             V((4,) + bshape, BF16), V((4,) + cshape, BF16), V((8, C), F32), V((C, kv_block), BF16),
             *mid_refs,
             D((2, 2, few)),
             D((2,)),
+            D((2, 2)),
         ],
         compiler_params=pltpu.CompilerParams(
-            collective_id=1, has_side_effects=True, vmem_limit_bytes=(STEP_VMEM if gd <= 4 else 58) * 2**20
+            collective_id=1, has_side_effects=True, vmem_limit_bytes=(STEP_VMEM if gd <= 4 else 60) * 2**20
         ),
         name="step",
     )(noise_level, aug_level, crop_size, *map(far, (weights2, noisy, target, text, first, second)), mask)
 
 
-STEP_VMEM = 48
-
-
-AROWS = 1024
+STEP_VMEM = 40
+
+
+AROWS = 2048
 
 
 def adam_tiles(length):

time: 159 us -> 154 us (0.969)
  Pallas kernels: 156 us -> 151 us
    pallas_call x1, Pallas kernels: 70.2 us -> 65.7 us  [run_step(): pl.pallas_call(functools.partial(step_kernel, gd, wide_count, kv_rows, re...]
where the time goes in v5:
time: 154 us
  Pallas kernels  151 us (98%)
  between operations  2.76 us (2%)
    pallas_call x1, Pallas kernels, share(): pl.pallas_call(functools.partial(share_kernel, gd, rows, chunk, pad, l1,...  68.7 us
    pallas_call x1, Pallas kernels, run_step(): pl.pallas_call(functools.partial(step_kernel, gd, wide_count, kv_rows, re...  65.7 us
    pallas_call x1, Pallas kernels, run_adam(): pl.pallas_call(functools.partial(adam_kernel, gd, length, kv_rows, rest_r...  8.2 us
    pallas_call x1, Pallas kernels, run_final(): pl.pallas_call(functools.partial(final_kernel, bases, pad, block), out_sh...  8.02 us

profile of v5, /device:TPU:0, one launch (start us, length us, event | category | flops | bytes accessed | tf_op | source)
XLA Modules:
  0.0 154.0 jit_solution(16763687224026158773)
XLA Ops:
  2.6 0.0 copy-start
  2.6 0.6 copy-done
  3.2 65.7 %step.1 = (bf16[2,4,32,4096]{3,2,1,0:T(8,128)(2,1)S(1)}, bf16[256,512]{1,0:T(8,128)(2,1)S(1)}, bf16[4,288,128]{2,1,0:T(8,128)(2,1)S(1)}, bf16[4,128,512]{2,1,0:T...) custom-call(s32[1]{0:T(128)S(6)} %copy.17.refs_0_, ...), custom_call_target="tpu_custom_call" | custom-call | tf_op jit(solution)/shard_map/step/pallas_call | solution.py:1033
  68.9 8.2 %adam.1 = (f32[1,1132608]{1,0:T(1,128)}, f32[1,1132608]{1,0:T(1,128)}, bf16[10240,128]{1,0:T(8,128)(2,1)S(1)}) custom-call(bf16[2,4,32,4096]{3,2,1,0:T(8,128)(2,1)S(1)} %get-tuple-element.24.refs_0_, bf16[256,512]{1,0:T(8,128)(2,1)S(1)} %get-tuple-element.25.refs_1_, bf16[4,288,128]{2,1,0:T(8,128)(2,1)S(1)} %get-tuple-element.26.refs_2_, ...), custom_call_target="tpu_custom_call" | custom-call | tf_op jit(solution)/shard_map/adam/pallas_call | solution.py:1233
  77.1 68.7 %share.1 = (bf16[2,11200,128]{2,1,0:T(8,128)(2,1)S(1)}, f32[17920,128]{1,0:T(8,128)S(1)}, f32[17920,128]{1,0:T(8,128)S(1)}) custom-call(bf16[10240,128]{1,0:T(8,128)(2,1)S(1)} %get-tuple-element.32.u_ref, f32[17697,128]{1,0:T(8,128)} %bitcast.5, f32[17697,128]{1,0:T(8,128)} %bitcast.6), custom_call_target="tpu_custom_call" | custom-call | tf_op jit(solution)/shard_map/share/pallas_call | solution.py:1384
  145.9 8.0 %final.1 = (f32[17697,128]{1,0:T(8,128)}, f32[17697,128]{1,0:T(8,128)}, f32[1]{0:T(128)}, f32[1]{0:T(128)}) custom-call(f32[17920,128]{1,0:T(8,128)S(1)} %get-tuple-element.33.weights, f32[17920,128]{1,0:T(8,128)S(1)} %get-tuple-element.34.outer, bf16[2,11200,128]{2,1,0:T(8,128)(2,1)S(1)} %get-tuple-element.35.pieces, ...), custom_call_target="tpu_custom_call" | custom-call | tf_op jit(solution)/shard_map/final/pallas_call | solution.py:1444
Async XLA Ops:
  2.6 0.7 copy-start

commit v6 on v5

--- a/solution.py
+++ b/solution.py
@@ -291,7 +291,7 @@
         blocks[owner] = part[:, at : at + per_block * tok].astype(BF16)
     start_near()
     edge_wait()
-    halves = band // TILE3 // 2
+    halves = 1
     pl.loop(0, halves)(back)
     start_far()
     pl.loop(halves, band // TILE3)(back)

time: 154 us -> 154 us (level)
  no operation moved by 1% of the time
where the time goes in v6:
time: 154 us; the launch traced here: 153 us
  Pallas kernels  150 us (97%)
  between operations  2.76 us (2%)
    pallas_call x1, Pallas kernels, share(): pl.pallas_call(functools.partial(share_kernel, gd, rows, chunk, pad, l1,...  68.8 us
    pallas_call x1, Pallas kernels, run_step(): pl.pallas_call(functools.partial(step_kernel, gd, wide_count, kv_rows, re...  65 us
    pallas_call x1, Pallas kernels, run_adam(): pl.pallas_call(functools.partial(adam_kernel, gd, length, kv_rows, rest_r...  8.2 us
    pallas_call x1, Pallas kernels, run_final(): pl.pallas_call(functools.partial(final_kernel, bases, pad, block), out_sh...  8.02 us

profile of v6, /device:TPU:0, one launch (start us, length us, event | category | flops | bytes accessed | tf_op | source)
XLA Modules:
  0.0 153.4 jit_solution(16568947988433048960)
XLA Ops:
  2.6 0.0 copy-start
  2.6 0.6 copy-done
  3.2 65.0 %step.1 = (bf16[2,4,32,4096]{3,2,1,0:T(8,128)(2,1)S(1)}, bf16[256,512]{1,0:T(8,128)(2,1)S(1)}, bf16[4,288,128]{2,1,0:T(8,128)(2,1)S(1)}, bf16[4,128,512]{2,1,0:T...) custom-call(s32[1]{0:T(128)S(6)} %copy.17.refs_0_, ...), custom_call_target="tpu_custom_call" | custom-call | tf_op jit(solution)/shard_map/step/pallas_call | solution.py:1033
  68.2 8.2 %adam.1 = (f32[1,1132608]{1,0:T(1,128)}, f32[1,1132608]{1,0:T(1,128)}, bf16[10240,128]{1,0:T(8,128)(2,1)S(1)}) custom-call(bf16[2,4,32,4096]{3,2,1,0:T(8,128)(2,1)S(1)} %get-tuple-element.24.refs_0_, bf16[256,512]{1,0:T(8,128)(2,1)S(1)} %get-tuple-element.25.refs_1_, bf16[4,288,128]{2,1,0:T(8,128)(2,1)S(1)} %get-tuple-element.26.refs_2_, ...), custom_call_target="tpu_custom_call" | custom-call | tf_op jit(solution)/shard_map/adam/pallas_call | solution.py:1233
  76.4 68.8 %share.1 = (bf16[2,11200,128]{2,1,0:T(8,128)(2,1)S(1)}, f32[17920,128]{1,0:T(8,128)S(1)}, f32[17920,128]{1,0:T(8,128)S(1)}) custom-call(bf16[10240,128]{1,0:T(8,128)(2,1)S(1)} %get-tuple-element.32.u_ref, f32[17697,128]{1,0:T(8,128)} %bitcast.5, f32[17697,128]{1,0:T(8,128)} %bitcast.6), custom_call_target="tpu_custom_call" | custom-call | tf_op jit(solution)/shard_map/share/pallas_call | solution.py:1384
  145.2 8.0 %final.1 = (f32[17697,128]{1,0:T(8,128)}, f32[17697,128]{1,0:T(8,128)}, f32[1]{0:T(128)}, f32[1]{0:T(128)}) custom-call(f32[17920,128]{1,0:T(8,128)S(1)} %get-tuple-element.33.weights, f32[17920,128]{1,0:T(8,128)S(1)} %get-tuple-element.34.outer, bf16[2,11200,128]{2,1,0:T(8,128)(2,1)S(1)} %get-tuple-element.35.pieces, ...), custom_call_target="tpu_custom_call" | custom-call | tf_op jit(solution)/shard_map/final/pallas_call | solution.py:1444
Async XLA Ops:
  2.6 0.7 copy-start

commit v7 on v6

--- a/solution.py
+++ b/solution.py
@@ -250,11 +250,11 @@
             - jnp.mean(dxh, axis=1, keepdims=True)
             - xhat * jnp.mean(dxh * xhat, axis=1, keepdims=True)
         )
-        dout_t = dout.T.astype(BF16)
-        lay_t = low.astype(F32).T.astype(BF16)
+        dout_t = dout_low.T
+        lay_t = low.T
         y_t[...] += dot(dout_t, probs[...])
         z_t[...] += dot(lay_t, dscore[...])
-        dconv_t = dconv.T.astype(BF16)
+        dconv_t = dconv.astype(BF16).T
         for dy in range(3):
             window = act3[pl.ds(q + 1 + dy, TILE)].reshape(pix, 3 * C)
             conv_t[:, dy * 3 * C : (dy + 1) * 3 * C] += dot(dconv_t, window)

time: 154 us -> 153 us (level)
  no operation moved by 1% of the time
where the time goes in v7:
time: 153 us
  Pallas kernels  150 us (98%)
  between operations  2.76 us (2%)
    pallas_call x1, Pallas kernels, share(): pl.pallas_call(functools.partial(share_kernel, gd, rows, chunk, pad, l1,...  68.8 us
    pallas_call x1, Pallas kernels, run_step(): pl.pallas_call(functools.partial(step_kernel, gd, wide_count, kv_rows, re...  64.8 us
    pallas_call x1, Pallas kernels, run_adam(): pl.pallas_call(functools.partial(adam_kernel, gd, length, kv_rows, rest_r...  8.2 us
    pallas_call x1, Pallas kernels, run_final(): pl.pallas_call(functools.partial(final_kernel, bases, pad, block), out_sh...  8.02 us

profile of v7, /device:TPU:0, one launch (start us, length us, event | category | flops | bytes accessed | tf_op | source)
XLA Modules:
  0.0 153.2 jit_solution(3142342125091753344)
XLA Ops:
  2.6 0.0 copy-start
  2.6 0.6 copy-done
  3.2 64.8 %step.1 = (bf16[2,4,32,4096]{3,2,1,0:T(8,128)(2,1)S(1)}, bf16[256,512]{1,0:T(8,128)(2,1)S(1)}, bf16[4,288,128]{2,1,0:T(8,128)(2,1)S(1)}, bf16[4,128,512]{2,1,0:T...) custom-call(s32[1]{0:T(128)S(6)} %copy.17.refs_0_, ...), custom_call_target="tpu_custom_call" | custom-call | tf_op jit(solution)/shard_map/step/pallas_call | solution.py:1033
  68.0 8.2 %adam.1 = (f32[1,1132608]{1,0:T(1,128)}, f32[1,1132608]{1,0:T(1,128)}, bf16[10240,128]{1,0:T(8,128)(2,1)S(1)}) custom-call(bf16[2,4,32,4096]{3,2,1,0:T(8,128)(2,1)S(1)} %get-tuple-element.24.refs_0_, bf16[256,512]{1,0:T(8,128)(2,1)S(1)} %get-tuple-element.25.refs_1_, bf16[4,288,128]{2,1,0:T(8,128)(2,1)S(1)} %get-tuple-element.26.refs_2_, ...), custom_call_target="tpu_custom_call" | custom-call | tf_op jit(solution)/shard_map/adam/pallas_call | solution.py:1233
  76.2 68.8 %share.1 = (bf16[2,11200,128]{2,1,0:T(8,128)(2,1)S(1)}, f32[17920,128]{1,0:T(8,128)S(1)}, f32[17920,128]{1,0:T(8,128)S(1)}) custom-call(bf16[10240,128]{1,0:T(8,128)(2,1)S(1)} %get-tuple-element.32.u_ref, f32[17697,128]{1,0:T(8,128)} %bitcast.5, f32[17697,128]{1,0:T(8,128)} %bitcast.6), custom_call_target="tpu_custom_call" | custom-call | tf_op jit(solution)/shard_map/share/pallas_call | solution.py:1384
  145.0 8.0 %final.1 = (f32[17697,128]{1,0:T(8,128)}, f32[17697,128]{1,0:T(8,128)}, f32[1]{0:T(128)}, f32[1]{0:T(128)}) custom-call(f32[17920,128]{1,0:T(8,128)S(1)} %get-tuple-element.33.weights, f32[17920,128]{1,0:T(8,128)S(1)} %get-tuple-element.34.outer, bf16[2,11200,128]{2,1,0:T(8,128)(2,1)S(1)} %get-tuple-element.35.pieces, ...), custom_call_target="tpu_custom_call" | custom-call | tf_op jit(solution)/shard_map/final/pallas_call | solution.py:1444
Async XLA Ops:
  2.6 0.7 copy-start
